TPU v7x, 256 devices: a whole 4x4x8 slice. The times are simulated.
256 devices in a mesh: rep: 16 (over y, z_lo), tp: 16 (over x, z_hi, core).
Axes of the slice: x: 4, y: 4, z: 8 (z_hi: 2, z_lo: 4; z = z_hi * 4 + z_lo), core: 2. Of those that a mesh axis runs over, the one named last changes fastest.
Arguments:
- hidden: bfloat16 [2, 2048, 8192], P(None, 'rep', 'tp'), may hold values from -6 to 6
- query_base_weight: bfloat16 [8192, 4096], P(None, 'tp'), may hold values from -0.0625 to 0.0625
- output_base_weight: bfloat16 [4096, 8192], P('tp'), may hold values from -0.09375 to 0.09375
- cache: bfloat16 [2048, 16, 32, 256], P('rep', 'tp'), may hold values from -310 to 310, as said below
- fresh: bfloat16 [2048, 16, 2, 256], P('rep', 'tp'), may hold values from -4 to 4, as said below
- lengths: int32 [2048], P('rep'), may hold values from 2 to 32, as said below
- grad_query_down: float32 [16, 64, 8192], P('rep', None, 'tp'), may hold values from -20000 to 20000
- grad_query_up: float32 [16, 64, 4096], P('rep', None, 'tp'), may hold values from -20000 to 20000
- grad_output_down: float32 [16, 64, 4096], P('rep', None, 'tp'), may hold values from -20000 to 20000
- grad_output_up: float32 [16, 64, 8192], P('rep', None, 'tp'), may hold values from -20000 to 20000
- ask_left_matrix: float32 [64, 8192], P('rep', 'tp'), may hold values from -0.0625 to 0.0625
- ask_right_matrix: float32 [64, 4096], P('rep', 'tp'), may hold values from -0.375 to 0.375
- proj_left_matrix: float32 [64, 4096], P('rep', 'tp'), may hold values from -0.09375 to 0.09375
- proj_right_matrix: float32 [64, 8192], P('rep', 'tp'), may hold values from -0.375 to 0.375
- mean_gradient_ask_left: float32 [64, 8192], P('rep', 'tp'), may hold values from -6 to 6
- mean_gradient_ask_right: float32 [64, 4096], P('rep', 'tp'), may hold values from -6 to 6
- mean_gradient_proj_left: float32 [64, 4096], P('rep', 'tp'), may hold values from -6 to 6
- mean_gradient_proj_right: float32 [64, 8192], P('rep', 'tp'), may hold values from -6 to 6
- variance_ask_left: float32 [64, 8192], P('rep', 'tp'), may hold values from 0.25 to 4
- variance_ask_right: float32 [64, 4096], P('rep', 'tp'), may hold values from 0.25 to 4
- variance_proj_left: float32 [64, 4096], P('rep', 'tp'), may hold values from 0.25 to 4
- variance_proj_right: float32 [64, 8192], P('rep', 'tp'), may hold values from 0.25 to 4
Outputs:
- decoded: bfloat16 [2, 2048, 8192], P(None, 'rep', 'tp')
- next_query_down: float32 [64, 8192], P('rep', 'tp')
- next_query_up: float32 [64, 4096], P('rep', 'tp')
- next_output_down: float32 [64, 4096], P('rep', 'tp')
- next_output_up: float32 [64, 8192], P('rep', 'tp')
- next_moment_query_down: float32 [64, 8192], P('rep', 'tp')
- next_moment_query_up: float32 [64, 4096], P('rep', 'tp')
- next_moment_output_down: float32 [64, 4096], P('rep', 'tp')
- next_moment_output_up: float32 [64, 8192], P('rep', 'tp')
- next_square_query_down: float32 [64, 8192], P('rep', 'tp')
- next_square_query_up: float32 [64, 4096], P('rep', 'tp')
- next_square_output_down: float32 [64, 4096], P('rep', 'tp')
- next_square_output_up: float32 [64, 8192], P('rep', 'tp')
Inputs may be any that keep to these rules, and one draw needn't show every extreme that they name: `lengths`: every rollout group's block of 128 rows holds a row with 32 filled slots. `cache`: tensor ranks whose query heads share a key-value head hold equal copies. `fresh`: tensor ranks whose query heads share a key-value head hold equal copies.
All inputs are finite; a program needn't handle non-finite values.
Results may differ from a plain program's by a relative error of at most 0.011.
Values may be sent and summed in bfloat16 or wider, within the bound.
No kernel may reach another device: no remote copies, remote signals or barrier semaphores. Data moves between devices by JAX's collectives and lax.ppermute only.
A program may use at most 128 MiB of HBM per device.

v0:
```python
import math

import jax
import jax.numpy as jnp
from jax import lax
from jax.sharding import PartitionSpec as P

HEAD_SPAN = 128
LOW_DIMENSION = 64
ALPHA_DIVIDEND = 32
PARAMS = 1572864


beta_one = 0.9
beta_two = 0.999
bias_one = 1.0 - math.exp(1000.0 * math.log(0.9))
bias_two = 1.0 - math.exp(1000.0 * math.log(0.999))
adam_eps = 1e-08
learn_rate = 0.005
norm_eps = 1e-06
rope_base = 1000000.0


def adam_update(factor, gradient, moment, square, clip_factor):
    scaled = clip_factor * gradient
    moment_new = beta_one * moment + (1.0 - beta_one) * scaled
    square_new = beta_two * square + (1.0 - beta_two) * scaled * scaled
    update = moment_new / bias_one / (jnp.sqrt(square_new / bias_two) + adam_eps)
    return (factor - learn_rate * update, moment_new, square_new)


def sum_squares(parts):
    return (
        jnp.sum(parts[0] * parts[0])
        + jnp.sum(parts[1] * parts[1])
        + jnp.sum(parts[2] * parts[2])
        + jnp.sum(parts[3] * parts[3])
    )


def rotate_heads(queries, positions):
    half_size = queries.shape[-1] // 2
    frequency = jnp.power(
        rope_base, -2.0 * jnp.arange(half_size, dtype=jnp.float32) / queries.shape[-1]
    )
    angles = positions.astype(jnp.float32)[:, None] * frequency[None, :]
    cosine = jnp.cos(angles)[:, None, :]
    sine_part = jnp.sin(angles)[:, None, :]
    lower_half = queries[..., :half_size]
    upper_half = queries[..., half_size:]
    return jnp.concatenate(
        [
            lower_half * cosine - upper_half * sine_part,
            upper_half * cosine + lower_half * sine_part,
        ],
        axis=-1,
    )


def attend(queries, cache_rows, fresh_rows, row_lengths, offset):
    row_count = queries.shape[0]
    head_count = queries.shape[1] // HEAD_SPAN
    rotated = rotate_heads(queries.reshape(row_count, head_count, HEAD_SPAN), row_lengths + offset)
    scaled = (rotated * (1.0 / math.sqrt(HEAD_SPAN))).astype(jnp.bfloat16)
    fresh_part = fresh_rows[:, : offset + 1]
    scores = jnp.einsum(
        "rhd,rcd->rhc", scaled, cache_rows[:, :, :HEAD_SPAN], preferred_element_type=jnp.float32
    )
    live_mask = jnp.arange(cache_rows.shape[1])[None, :] < row_lengths[:, None]
    scores = jnp.where(live_mask[:, None, :], scores, -1e30)
    fresh_scores = jnp.einsum(
        "rhd,rjd->rhj", scaled, fresh_part[:, :, :HEAD_SPAN], preferred_element_type=jnp.float32
    )
    row_max = jnp.maximum(jnp.max(scores, axis=-1), jnp.max(fresh_scores, axis=-1))[..., None]
    cache_exp = jnp.exp(scores - row_max)
    fresh_exp = jnp.exp(fresh_scores - row_max)
    denominator = jnp.sum(cache_exp, axis=-1, keepdims=True) + jnp.sum(
        fresh_exp, axis=-1, keepdims=True
    )
    cache_weights = (cache_exp / denominator).astype(jnp.bfloat16)
    fresh_weights = (fresh_exp / denominator).astype(jnp.bfloat16)
    attended = jnp.einsum(
        "rhc,rcd->rhd",
        cache_weights,
        cache_rows[:, :, HEAD_SPAN:],
        preferred_element_type=jnp.float32,
    )
    attended = attended + jnp.einsum(
        "rhj,rjd->rhd",
        fresh_weights,
        fresh_part[:, :, HEAD_SPAN:],
        preferred_element_type=jnp.float32,
    )
    return attended.reshape(row_count, head_count * HEAD_SPAN).astype(jnp.bfloat16)


def on_device(
    hidden,
    query_base_weight,
    output_base_weight,
    cache,
    fresh,
    lengths,
    grad_query_down,
    grad_query_up,
    grad_output_down,
    grad_output_up,
    ask_left_matrix,
    ask_right_matrix,
    proj_left_matrix,
    proj_right_matrix,
    mean_gradient_ask_left,
    mean_gradient_ask_right,
    mean_gradient_proj_left,
    mean_gradient_proj_right,
    variance_ask_left,
    variance_ask_right,
    variance_proj_left,
    variance_proj_right,
):
    gradients = (grad_query_down[0], grad_query_up[0], grad_output_down[0], grad_output_up[0])
    share_rows = gradients[0].shape[0] // lax.axis_size("rep")
    summed_whole = lax.psum((gradients[0], gradients[1], gradients[2], gradients[3]), "rep")
    total_squares = lax.psum(sum_squares(summed_whole), "tp")
    first_row = lax.axis_index("rep") * share_rows
    summed = tuple(
        (lax.dynamic_slice_in_dim(entry, first_row, share_rows, 0) for entry in summed_whole)
    )
    clip_factor = jnp.minimum(1.0, math.sqrt(PARAMS) / (jnp.sqrt(total_squares) + norm_eps))
    factors = (ask_left_matrix, ask_right_matrix, proj_left_matrix, proj_right_matrix)
    moments = (
        mean_gradient_ask_left,
        mean_gradient_ask_right,
        mean_gradient_proj_left,
        mean_gradient_proj_right,
    )
    squares = (variance_ask_left, variance_ask_right, variance_proj_left, variance_proj_right)
    updated = [
        adam_update(factors[index], summed[index], moments[index], squares[index], clip_factor)
        for index in range(4)
    ]
    factor_copies = [entry[0].astype(jnp.bfloat16) for entry in updated]
    row_parts = (
        lax.all_gather(factor_copies[0], "rep", axis=0, tiled=True),
        lax.all_gather(factor_copies[1], "rep", axis=0, tiled=True),
        lax.all_gather(factor_copies[2], "rep", axis=0, tiled=True),
        lax.all_gather(factor_copies[3], "rep", axis=0, tiled=True),
    )
    wide_parts = (
        lax.all_gather(row_parts[0], "tp", axis=1, tiled=True),
        lax.all_gather(row_parts[3], "tp", axis=1, tiled=True),
    )
    down_full, out_up_full = wide_parts
    up_cols, out_down_cols = (row_parts[1], row_parts[2])
    delta_multiplier = ALPHA_DIVIDEND / LOW_DIMENSION
    contract_pair = (((0,), (0,)), ((), ()))
    merged_query_weight = (
        query_base_weight.astype(jnp.float32)
        + delta_multiplier
        * lax.dot_general(down_full, up_cols, contract_pair, preferred_element_type=jnp.float32)
    ).astype(jnp.bfloat16)
    column_count = hidden.shape[2]
    merged_output_weight = (
        output_base_weight.astype(jnp.float32)
        + delta_multiplier
        * lax.dot_general(
            out_down_cols, out_up_full, contract_pair, preferred_element_type=jnp.float32
        )
    ).astype(jnp.bfloat16)
    own_cache = cache[:, 0]
    own_fresh = fresh[:, 0]
    outputs = []
    for offset in range(2):
        queries = jnp.dot(
            lax.all_gather(hidden[offset], "tp", axis=1, tiled=True),
            merged_query_weight,
            preferred_element_type=jnp.float32,
        )
        attended = attend(queries, own_cache, own_fresh, lengths, offset)
        partial_out = jnp.dot(attended, merged_output_weight, preferred_element_type=jnp.float32)
        whole_out = lax.psum(partial_out, "tp")
        summed_out = lax.dynamic_slice_in_dim(
            whole_out, lax.axis_index("tp") * column_count, column_count, 1
        )
        outputs.append((hidden[offset].astype(jnp.float32) + summed_out).astype(jnp.bfloat16))
    decoded = jnp.stack(outputs)
    return (
        decoded,
        updated[0][0],
        updated[1][0],
        updated[2][0],
        updated[3][0],
        updated[0][1],
        updated[1][1],
        updated[2][1],
        updated[3][1],
        updated[0][2],
        updated[1][2],
        updated[2][2],
        updated[3][2],
    )


def solution(mesh):
    return jax.shard_map(
        on_device,
        mesh=mesh,
        in_specs=(
            P(None, "rep", "tp"),
            P(None, "tp"),
            P("tp", None),
            P("rep", "tp", None, None),
            P("rep", "tp", None, None),
            P("rep"),
            P("rep", None, "tp"),
            P("rep", None, "tp"),
            P("rep", None, "tp"),
            P("rep", None, "tp"),
            P("rep", "tp"),
            P("rep", "tp"),
            P("rep", "tp"),
            P("rep", "tp"),
            P("rep", "tp"),
            P("rep", "tp"),
            P("rep", "tp"),
            P("rep", "tp"),
            P("rep", "tp"),
            P("rep", "tp"),
            P("rep", "tp"),
            P("rep", "tp"),
        ),
        out_specs=(
            P(None, "rep", "tp"),
            P("rep", "tp"),
            P("rep", "tp"),
            P("rep", "tp"),
            P("rep", "tp"),
            P("rep", "tp"),
            P("rep", "tp"),
            P("rep", "tp"),
            P("rep", "tp"),
            P("rep", "tp"),
            P("rep", "tp"),
            P("rep", "tp"),
            P("rep", "tp"),
        ),
        check_vma=False,
    )
```

profile of v0, /device:TPU:8, one launch (start us, length us, event | category | flops | bytes accessed | tf_op | source)
XLA Modules:
  0.0 896.0 jit_solution(8911965234019670786)
XLA Ops:
  7.2 0.7 all-reduce.7.cloned.1.call-update
  8.0 161.5 %all-reduce.7.cloned.1.call-done = (f32[64,256]{1,0:T(8,128)}, f32[64,512]{1,0:T(8,128)}, f32[64,256]{1,0:T(8,128)}, f32[64,512]{1,0:T(8,128)}) async-done(((f32[64,256]{1,0:T(8,128)}, f32[64,512]{1,0:T(8,128)}, f32[64,256]{1,0:T(8,128)}, f32[64,512]{1,0:T(8,128)}), (f32[64,256]{1,0:T(8,128)}, f32[64,512]{1,0:T(8,128)}, f32[64,256]{1,0:T(8,128)}, f32[64,512]{1,0:T(8,128)})) %all-reduce.7.cloned.1.call-update) | async-done | bytes 393232 | tf_op jit(solution)/shard_map/psum | solution.py:123
  169.5 1.5 multiply_reduce_fusion.2
  171.0 1.6 multiply_reduce_fusion
  175.2 43.3 %psum.53 = f32[]{:T(128)} all-reduce(f32[]{:T(128)S(6)} %add.118), channel_id=1, replica_groups=mesh['rep'=16,'tp'=16] {'tp'}, use_global_device_ids=true, to_apply=%region_8.0 | all-reduce | flops 1 | bytes 8 | tf_op jit(solution)/shard_map/psum | solution.py:124
  219.2 1.4 convert_bitcast_fusion
  220.5 41.3 %all-gather.5 = bf16[16,4,512]{2,1,0:T(4,128)(2,1)S(1)} all-gather(bf16[1,4,512]{2,1,0:T(4,128)(2,1)S(1)} %get-tuple-element.27), channel_id=1, replica_groups=mesh['rep'=16,'tp'=16] {'rep'}, dimensions={0}, use_global_device_ids=true | all-gather | bytes 69632 | tf_op jit(solution)/shard_map/all_gather | solution.py:147
  261.8 0.6 reshape.203
  262.6 1.4 convert_bitcast_fusion.1
  264.0 40.4 %all-gather.2 = bf16[16,4,512]{2,1,0:T(4,128)(2,1)S(1)} all-gather(bf16[1,4,512]{2,1,0:T(4,128)(2,1)S(1)} %get-tuple-element.23), channel_id=1, replica_groups=mesh['rep'=16,'tp'=16] {'rep'}, dimensions={0}, use_global_device_ids=true | all-gather | bytes 69632 | tf_op jit(solution)/shard_map/all_gather | solution.py:144
  304.3 0.7 reshape.197
  305.1 1.7 fusion.50
  307.4 0.7 fusion.53
  308.2 0.7 iota_compare_fusion
  308.9 0.9 slice_convert_fusion
  310.3 1.4 convert_bitcast_fusion.2
  311.7 36.2 %all-gather.4 = bf16[16,4,256]{2,1,0:T(4,128)(2,1)S(1)} all-gather(bf16[1,4,256]{2,1,0:T(4,128)(2,1)S(1)} %get-tuple-element.31), channel_id=1, replica_groups=mesh['rep'=16,'tp'=16] {'rep'}, dimensions={0}, use_global_device_ids=true | all-gather | bytes 34816 | tf_op jit(solution)/shard_map/all_gather | solution.py:146
  347.9 1.4 convert_bitcast_fusion.3
  349.3 37.5 %all-gather.3 = bf16[16,4,256]{2,1,0:T(4,128)(2,1)S(1)} all-gather(bf16[1,4,256]{2,1,0:T(4,128)(2,1)S(1)} %get-tuple-element.19), channel_id=1, replica_groups=mesh['rep'=16,'tp'=16] {'rep'}, dimensions={0}, use_global_device_ids=true | all-gather | bytes 34816 | tf_op jit(solution)/shard_map/all_gather | solution.py:145
  386.8 5.7 fusion.3
  392.6 5.8 fusion.2
  398.4 34.2 %all-gather.17.cloned.1.call-done = bf16[1,128,8192]{2,1,0:T(8,128)(2,1)} async-done(((bf16[1,128,512]{2,1,0:T(8,128)(2,1)}), bf16[1,128,8192]{2,1,0:T(8,128)(2,1)}) %all-gather.17.cloned.1.call-update) | async-done | bytes 2097168 | tf_op jit(solution)/shard_map/all_gather | solution.py:175
  432.6 4.1 fusion.4
  436.8 57.8 %all-gather.15.cloned.1.call-done = bf16[1,128,8192]{2,1,0:T(8,128)(2,1)} async-done(((bf16[1,128,512]{2,1,0:T(8,128)(2,1)}), bf16[1,128,8192]{2,1,0:T(8,128)(2,1)}) %all-gather.15.cloned.1.call-update) | async-done | bytes 2097168 | tf_op jit(solution)/shard_map/all_gather | solution.py:175
  494.6 4.1 fusion.6
  500.3 0.7 fusion.56
  501.0 0.7 fusion.54
  504.0 2.7 fusion.24
  507.2 2.7 fusion.27
  509.9 377.4 %all-reduce.5.cloned.1.call-done = (f32[128,8192]{1,0:T(8,128)}, f32[128,8192]{1,0:T(8,128)}) async-done(((f32[128,8192]{1,0:T(8,128)}, f32[128,8192]{1,0:T(8,128)}), (f32[128,8192]{1,0:T(8,128)}, f32[128,8192]{1,0:T(8,128)})) %all-reduce.5.cloned.1.call-update) | async-done | bytes 8388624 | tf_op jit(solution)/shard_map/psum | solution.py:181
  887.3 1.1 fusion.17
  888.4 0.7 pad_maximum_fusion
  (47 shorter events, 5.6 us)
Async XLA Ops:
  7.2 162.3 %all-reduce.7.cloned.1.call-start = ((), (), s32[]{:S(2)}) async-start(), calls=%async_computation.5 | async-start | bytes 786432 | tf_op jit(solution)/shard_map/psum | solution.py:123
  7.9 378.9 %all-gather.13.cloned.1.call-start = ((), (), s32[]{:S(2)}) async-start(), calls=%async_computation.1 | async-start | bytes 1114112 | tf_op jit(solution)/shard_map/all_gather | solution.py:151
  262.5 130.1 %all-gather.11.cloned.1.call-start = ((), (), s32[]{:S(2)}) async-start(), calls=%async_computation | async-start | bytes 1114112 | tf_op jit(solution)/shard_map/all_gather | solution.py:150
  305.0 127.6 %all-gather.17.cloned.1.call-start = ((), (), s32[]{:S(2)}) async-start(), calls=%async_computation.3 | async-start | bytes 2228224 | tf_op jit(solution)/shard_map/all_gather | solution.py:175
  306.8 187.8 %all-gather.15.cloned.1.call-start = ((), (), s32[]{:S(2)}) async-start(), calls=%async_computation.2 | async-start | bytes 2228224 | tf_op jit(solution)/shard_map/all_gather | solution.py:175
  307.4 580.0 %all-reduce.5.cloned.1.call-start = ((), (), s32[]{:S(2)}) async-start(), calls=%async_computation.4 | async-start | bytes 16777216 | tf_op jit(solution)/shard_map/psum | solution.py:181
  436.8 62.7 %copy-start.2 = (bf16[128,1,2,256]{3,2,1,0:T(2,128)(2,1)S(1)}, bf16[128,1,2,256]{3,2,1,0:T(2,128)(2,1)}, u32[]{:S(2)}) copy-start(bf16[128,1,2,256]{3,2,1,0:T(2,128)(2,1)} %param.26) | copy-start | bytes 393220
  436.8 63.5 %copy-start.3 = (bf16[128,1,32,256]{3,2,1,0:T(8,128)(2,1)S(1)}, bf16[128,1,32,256]{3,2,1,0:T(8,128)(2,1)}, u32[]{:S(2)}) copy-start(bf16[128,1,32,256]{3,2,1,0:T(8,128)(2,1)} %param.25) | copy-start | bytes 6291460
  501.7 2.3 copy-start
  509.9 377.5 %copy-start.1 = (bf16[2,128,512]{2,1,0:T(8,128)(2,1)S(1)}, bf16[2,128,512]{2,1,0:T(8,128)(2,1)}, u32[]{:S(2)}) copy-start(bf16[2,128,512]{2,1,0:T(8,128)(2,1)} %param.22) | copy-start | bytes 786436
Sparse Core Ops, SparseCore 0:
  10.9 158.5 all-reduce.6
  262.6 53.8 all-gather.12
  319.4 51.6 all-gather.10
  373.8 58.7 all-gather.16
  435.9 58.6 all-gather.14
  510.0 377.2 all-reduce.4
where the time goes:
time: 897 us; the launch traced here: 896 us
  waiting for transfers between devices  632 us (70%)
  blocking collectives  199 us (22%)
  matrix products  28.5 us (3%)
  between operations  17.7 us (2%)
  other arithmetic  15.1 us (2%)
    psum x1, waiting for transfers between devices, on_device(): whole_out = lax.psum(partial_out, 'tp')  377 us
    psum x1, waiting for transfers between devices, on_device(): lax.psum((gradients[0], gradients[1], gradients[2], gradients[3]), 'rep')  161 us
    all_gather x2, waiting for transfers between devices, on_device(): lax.all_gather(hidden[offset], 'tp', axis=1, tiled=True)  92 us
    psum x1, blocking collectives, on_device(): total_squares = lax.psum(sum_squares(summed_whole), 'tp')  43.3 us
    all_gather x1, blocking collectives, on_device(): lax.all_gather(factor_copies[3], 'rep', axis=0, tiled=True)  41.3 us
    all_gather x1, blocking collectives, on_device(): lax.all_gather(factor_copies[0], 'rep', axis=0, tiled=True)  40.4 us
    all_gather x1, blocking collectives, on_device(): lax.all_gather(factor_copies[1], 'rep', axis=0, tiled=True)  37.5 us
    all_gather x1, blocking collectives, on_device(): lax.all_gather(factor_copies[2], 'rep', axis=0, tiled=True)  36.2 us
  transfers between devices with their start and end apart: 6, of which 4 were waited for; matrix products, arithmetic and copies ran while one was open for 3% of the time, Pallas kernels for 0%

commit v1 on v0

v1 whole, which is shorter than its diff:
```python
import math

import jax
import jax.numpy as jnp
from jax import lax
from jax.experimental import pallas as pl
from jax.experimental.pallas import tpu as pltpu
from jax.sharding import PartitionSpec as P

HEAD = 128
PARAMS = 1572864
N = 16

beta_one = 0.9
beta_two = 0.999
bias_one = 1.0 - math.exp(1000.0 * math.log(0.9))
bias_two = 1.0 - math.exp(1000.0 * math.log(0.999))
adam_eps = 1e-08
learn_rate = 0.005
norm_eps = 1e-06
rope_base = 1000000.0

bf16 = jnp.bfloat16
f32 = jnp.float32


def adam_update(factor, gradient, moment, square, clip_factor):
    scaled = clip_factor * gradient
    moment_new = beta_one * moment + (1.0 - beta_one) * scaled
    square_new = beta_two * square + (1.0 - beta_two) * scaled * scaled
    update = moment_new / bias_one / (jnp.sqrt(square_new / bias_two) + adam_eps)
    return (factor - learn_rate * update, moment_new, square_new)


def shift(value, move):
    return lax.ppermute(value, "tp", [(i, move(i)) for i in range(N)])


def to_core(value):
    return shift(value, lambda i: i ^ 1)


def to_z(value):
    return shift(value, lambda i: i ^ 2)


def to_right(value):
    return shift(value, lambda i: (i + 4) % N)


def to_left(value):
    return shift(value, lambda i: (i + 12) % N)


def give_all(value, axis):
    wide = lax.optimization_barrier(jnp.broadcast_to(value[None], (N,) + value.shape))
    return lax.all_to_all(wide, axis, 0, 0)


def dot(a, b, contract=((1,), (0,))):
    return lax.dot_general(a, b, (contract, ((), ())), preferred_element_type=f32)


def base_kernel(order, mine, other, w_mine, w_other, out):
    @pl.when(pl.program_id(0) == 0)
    def _():
        out[...] = jnp.zeros_like(out)

    out[...] += dot(mine[0], w_mine[0]) + dot(other[0], w_other[0])


def base_queries(order, mine, other, weight):
    weight = weight.reshape(N, 512, 256)
    return pl.pallas_call(
        base_kernel,
        grid_spec=pltpu.PrefetchScalarGridSpec(
            num_scalar_prefetch=1,
            grid=(8,),
            in_specs=[
                pl.BlockSpec((1, 256, 512), lambda k, o: (k, 0, 0)),
                pl.BlockSpec((1, 256, 512), lambda k, o: (k, 0, 0)),
                pl.BlockSpec((1, 512, 256), lambda k, o: (o[k], 0, 0)),
                pl.BlockSpec((1, 512, 256), lambda k, o: (o[k + 8], 0, 0)),
            ],
            out_specs=pl.BlockSpec((256, 256), lambda k, o: (0, 0)),
        ),
        out_shape=jax.ShapeDtypeStruct((256, 256), f32),
        cost_estimate=pl.CostEstimate(
            flops=2 * 256 * 8192 * 256, bytes_accessed=8 << 20, transcendentals=0
        ),
    )(order, mine, other, weight, weight)


ROWS = 16


def attend_kernel(base, low, up, cosine, sine, lens, cache, fresh, out):
    half = pl.program_id(0)
    base_row = pl.multiple_of(half * ROWS, ROWS)
    lows = jnp.sum(low[:, 0].astype(f32), axis=0).astype(bf16)
    ups = up[...]
    zero = jnp.zeros_like(ups)
    pieces = []
    for step in range(2):
        both = jnp.concatenate([ups, zero] if step == 0 else [zero, ups], axis=0)
        query = base[step] + 0.5 * dot(lows, both)
        for head in range(2):
            one = query[:, head * HEAD : (head + 1) * HEAD]
            turned = one * cosine[step] + pltpu.roll(one, HEAD // 2, 1) * sine[step]
            pieces.append((turned * (1.0 / math.sqrt(HEAD))).astype(bf16))
    queries = jnp.concatenate(pieces, axis=0)
    keys = cache[:, :HEAD]
    values = cache[:, HEAD:]
    new_keys = fresh[:, :HEAD]
    new_values = fresh[:, HEAD:]
    scores = dot(queries, keys, ((1,), (1,)))
    new_scores = dot(queries, new_keys, ((1,), (1,)))
    slots = lax.broadcasted_iota(jnp.int32, scores.shape, 1)
    rows = lax.broadcasted_iota(jnp.int32, scores.shape, 0) & (ROWS - 1)
    length = jnp.concatenate([lens[...]] * 4, axis=0)
    length = jnp.concatenate([length] * (scores.shape[1] // HEAD), axis=1)
    live = ((slots >> 5) == rows) & ((slots & 31) < length)
    scores = jnp.where(live, scores, -1e30)
    new_slots = lax.broadcasted_iota(jnp.int32, new_scores.shape, 1)
    new_index = lax.broadcasted_iota(jnp.int32, new_scores.shape, 0)
    new_live = ((new_slots >> 1) == (new_index & (ROWS - 1))) & (
        (new_slots & 1) <= (new_index >> 5)
    )
    new_scores = jnp.where(new_live, new_scores, -1e30)
    top = jnp.maximum(
        jnp.max(scores, axis=1, keepdims=True), jnp.max(new_scores, axis=1, keepdims=True)
    )
    weights = jnp.exp(scores - top)
    new_weights = jnp.exp(new_scores - top)
    total = jnp.sum(weights, axis=1, keepdims=True) + jnp.sum(new_weights, axis=1, keepdims=True)
    inverse = 1.0 / total
    result = dot((weights * inverse).astype(bf16), values)
    result = result + dot((new_weights * inverse).astype(bf16), new_values)
    for step in range(2):
        for head in range(2):
            at = (step * 2 + head) * ROWS
            out[step, :, head * HEAD : (head + 1) * HEAD] = result[at : at + ROWS].astype(bf16)


def attention(base, low, up, cosine, sine, lens, cache, fresh):
    return pl.pallas_call(
        attend_kernel,
        grid=(128 // ROWS,),
        in_specs=[
            pl.BlockSpec((2, ROWS, 256), lambda k: (0, k, 0)),
            pl.BlockSpec((N, 1, ROWS, 128), lambda k: (0, 0, k, 0)),
            pl.BlockSpec((64, 256), lambda k: (0, 0)),
            pl.BlockSpec((2, ROWS, 128), lambda k: (0, k, 0)),
            pl.BlockSpec((2, ROWS, 128), lambda k: (0, k, 0)),
            pl.BlockSpec((ROWS, 128), lambda k: (k, 0)),
            pl.BlockSpec((ROWS * 32, 256), lambda k: (k, 0)),
            pl.BlockSpec((ROWS * 2, 256), lambda k: (k, 0)),
        ],
        out_specs=pl.BlockSpec((2, ROWS, 256), lambda k: (0, k, 0)),
        out_shape=jax.ShapeDtypeStruct((2, 128, 256), bf16),
        cost_estimate=pl.CostEstimate(
            flops=2 * 512 * 512 * 256, bytes_accessed=3 << 20, transcendentals=512 * 512
        ),
    )(base, low, up, cosine, sine, lens, cache, fresh)


def project_kernel(order, mine, other, w_mine, w_other, out):
    out[0] = (dot(mine[...], w_mine[...]) + dot(other[...], w_other[...])).astype(bf16)


def project(order, mine, other, w_mine, w_other):
    return pl.pallas_call(
        project_kernel,
        grid_spec=pltpu.PrefetchScalarGridSpec(
            num_scalar_prefetch=1,
            grid=(8,),
            in_specs=[
                pl.BlockSpec((256, 256), lambda k, o: (0, 0)),
                pl.BlockSpec((256, 256), lambda k, o: (0, 0)),
                pl.BlockSpec((256, 512), lambda k, o: (0, o[k])),
                pl.BlockSpec((256, 512), lambda k, o: (0, o[k] // 2)),
            ],
            out_specs=pl.BlockSpec((1, 256, 512), lambda k, o: (k, 0, 0)),
        ),
        out_shape=jax.ShapeDtypeStruct((8, 256, 512), bf16),
        cost_estimate=pl.CostEstimate(
            flops=2 * 256 * 512 * 4096, bytes_accessed=6 << 20, transcendentals=0
        ),
    )(order, mine, other, w_mine, w_other)


def on_device(
    hidden,
    query_base_weight,
    output_base_weight,
    cache,
    fresh,
    lengths,
    grad_query_down,
    grad_query_up,
    grad_output_down,
    grad_output_up,
    *state,
):
    widths = (512, 256, 256, 512)
    cuts = (512, 768, 1024)
    rank = lax.axis_index("tp")
    core = rank % 2
    z_hi = (rank // 2) % 2
    x = rank // 4

    order = jnp.stack(
        [
            ((x + dx) % 4) * 4 + (z_hi ^ dz) * 2 + core
            for dx in (0, 1, 2, 3)
            for dz in (0, 1)
        ]
    ).astype(jnp.int32)
    orders = jnp.concatenate([order, order ^ 1])

    gradient = jnp.concatenate(
        [grad_query_down[0], grad_query_up[0], grad_output_down[0], grad_output_up[0]], axis=1
    ).reshape(N, 4, 1536)
    summed = jnp.sum(lax.all_to_all(gradient, "rep", 0, 0), axis=0)

    zed = to_z(hidden)
    pair = jnp.stack([hidden, zed])
    left = to_right(pair)
    right = to_left(pair)

    factor = jnp.concatenate(state[0:4], axis=1)
    moment = jnp.concatenate(state[4:8], axis=1)
    square = jnp.concatenate(state[8:12], axis=1)
    whole = lax.all_gather(
        jnp.concatenate([factor, moment, square], axis=1).reshape(8, 2304), "rep", axis=0
    ).reshape(N, 4, 3, 1536)

    squares = jnp.sum(summed * summed)
    high = squares.astype(bf16)
    low = (squares - high.astype(f32)).astype(bf16)
    tail = jnp.where(
        lax.broadcasted_iota(jnp.int32, (4, 128), 0) == 0, high, low
    )
    sent = jnp.concatenate([summed.astype(bf16), tail], axis=1)
    all_summed = give_all(sent, "rep")
    own_squares = jnp.sum(all_summed[:, 0:2, 1536].astype(f32))

    far_a = to_right(left[:, 0])
    far_b = to_left(right[:, 1])
    far = jnp.stack([far_a, far_b], axis=1)
    mine = jnp.stack([pair, right, far, left]).reshape(8, 256, 512)
    other = to_core(mine)

    total_squares = jnp.sum(give_all(jnp.full((1, 128), own_squares), "tp")[:, 0, 0])
    clip_factor = jnp.minimum(1.0, math.sqrt(PARAMS) / (jnp.sqrt(total_squares) + norm_eps))

    base = base_queries(orders, mine, other, query_base_weight).reshape(2, 128, 256)

    copies, _, _ = adam_update(
        whole[:, :, 0],
        all_summed[:, :, :1536].astype(f32),
        whole[:, :, 1],
        whole[:, :, 2],
        clip_factor,
    )
    copies = copies.astype(bf16).reshape(64, 1536)
    down, up, out_down, out_up = jnp.split(copies, cuts, axis=1)

    low_part = jnp.concatenate(
        [dot(hidden[0], down, ((1,), (1,))), dot(hidden[1], down, ((1,), (1,)))], axis=1
    ).astype(bf16)
    lows = give_all(low_part[None], "tp")

    updated, moved, squared = adam_update(factor, summed, moment, square, clip_factor)

    exponents = -2.0 * jnp.arange(64, dtype=f32) / HEAD
    frequency = jnp.power(rope_base, exponents)
    positions = (lengths[None, :] + jnp.arange(2, dtype=jnp.int32)[:, None]).astype(f32)
    angles = positions[:, :, None] * frequency
    cosine = jnp.cos(angles)
    sine = jnp.sin(angles)
    cosine = jnp.concatenate([cosine, cosine], axis=2)
    sine = jnp.concatenate([-sine, sine], axis=2)
    lens = jnp.broadcast_to(lengths[:, None], (128, 128))
    attended = attention(
        base, lows, up, cosine, sine, lens, cache.reshape(4096, 256), fresh.reshape(256, 256)
    ).reshape(256, 256)

    blocks = output_base_weight.reshape(256, 8, 2, 512)
    give = lax.dynamic_index_in_dim(blocks, 1 - core, 2, keepdims=False).reshape(256, 4096)
    taken = to_core(give)
    attended_other = to_core(attended)
    partial = project(order, attended, attended_other, output_base_weight, taken)
    partial = partial.reshape(4, 2, 2, 128, 512)

    inner = dot(attended, out_down, ((1,), (1,)))
    inner = jnp.concatenate([inner[:128], inner[128:]], axis=1).astype(bf16)
    inner = jnp.sum(give_all(inner, "tp").astype(f32), axis=0).astype(bf16)
    inner = jnp.concatenate([inner[:, :64], inner[:, 64:]], axis=0)

    from_left = to_right(partial[2, :, 0])
    from_right = to_left(partial[2, :, 1])
    go_right = jnp.stack(
        [(partial[1, :, 0].astype(f32) + from_left.astype(f32)).astype(bf16), partial[1, :, 1]],
        axis=1,
    )
    go_left = jnp.stack(
        [partial[3, :, 0], (partial[3, :, 1].astype(f32) + from_right.astype(f32)).astype(bf16)],
        axis=1,
    )
    sums = (
        partial[0].astype(f32) + to_right(go_right).astype(f32) + to_left(go_left).astype(f32)
    )
    from_z = to_z(sums[1].astype(bf16))
    decoded = (
        hidden.astype(f32)
        + sums[0]
        + from_z.astype(f32)
        + 0.5 * dot(inner, out_up).reshape(2, 128, 512)
    ).astype(bf16)

    return (
        decoded,
        *jnp.split(updated, cuts, axis=1),
        *jnp.split(moved, cuts, axis=1),
        *jnp.split(squared, cuts, axis=1),
    )


def solution(mesh):
    return jax.shard_map(
        on_device,
        mesh=mesh,
        in_specs=(
            P(None, "rep", "tp"),
            P(None, "tp"),
            P("tp", None),
            P("rep", "tp", None, None),
            P("rep", "tp", None, None),
            P("rep"),
        )
        + (P("rep", None, "tp"),) * 4
        + (P("rep", "tp"),) * 12,
        out_specs=(P(None, "rep", "tp"),) + (P("rep", "tp"),) * 12,
        check_vma=False,
    )
```

time: 897 us -> 223 us (0.25)
  the two profiles are of different devices: /device:TPU:8 before, /device:TPU:1 now
where the time goes in v1:
time: 223 us; the launch traced here: 222 us
  starting transfers between devices  71.8 us (32%)
  waiting for transfers between devices  44.8 us (20%)
  local copies, waits for them, and re-layouts  43.9 us (20%)
  Pallas kernels  24.7 us (11%)
  other arithmetic  17.3 us (8%)
  between operations  16.8 us (8%)
  matrix products  2.28 us (1%)
    all_to_all x4, starting transfers between devices, give_all(): return lax.all_to_all(wide, axis, 0, 0)  40.7 us
    ppermute x13, starting transfers between devices, shift(): return lax.ppermute(value, 'tp', [(i, move(i)) for i in range(N)])  25.4 us
    ppermute x13, waiting for transfers between devices, shift(): return lax.ppermute(value, 'tp', [(i, move(i)) for i in range(N)])  19.5 us
    all_to_all x4, waiting for transfers between devices, give_all(): return lax.all_to_all(wide, axis, 0, 0)  19.3 us
    dynamic_slice x1, local copies, waits for them, and re-layouts, on_device(): lax.dynamic_index_in_dim(blocks, 1 - core, 2, keepdims=False)  13.5 us
    pallas_call x1, Pallas kernels, attention(): pl.pallas_call(attend_kernel, grid=(128 // ROWS,), in_specs=[pl.BlockSpec...  8.54 us
    pallas_call x1, Pallas kernels, base_queries(): pl.pallas_call(base_kernel, grid_spec=pltpu.PrefetchScalarGridSpec(num_sc...  8.11 us
    pallas_call x1, Pallas kernels, project(): pl.pallas_call(project_kernel, grid_spec=pltpu.PrefetchScalarGridSpec(num...  8 us
  transfers between devices with their start and end apart: 19, of which 11 were waited for; matrix products, arithmetic and copies ran while one was open for 27% of the time, Pallas kernels for 8%

profile of v1, /device:TPU:1, one launch (start us, length us, event | category | flops | bytes accessed | tf_op | source)
XLA Modules:
  0.0 221.5 jit_solution(5647026982856121018)
XLA Ops:
  7.3 7.8 %collective-permute-start = (bf16[2,128,512]{2,1,0:T(8,128)(2,1)}, bf16[2,128,512]{2,1,0:T(8,128)(2,1)S(1)}, u32[]{:S(2)}, u32[]{:S(2)}) collective-permute-start(bf16[2,128,512]{2,1,0:T(8,128)(2,1)} %param.22), channel_id=1, source_target_pairs={{0,2},{1,3},{2,0},{3,1},{4,6},{5,7},{6,4},{7,5},{8,10},{9,11},{10,... | collective-permute-start | bytes 786440 | tf_op jit(solution)/shard_map/ppermute | solution.py:36
  19.6 5.7 %all-to-all-start = ((f32[16,4,1536]{2,1,0:T(4,128)}), f32[16,4,1536]{2,1,0:T(4,128)S(1)}, u32[]{:S(2)}, u32[]{:S(2)}) async-start(f32[16,4,1536]{2,1,0:T(4,128)} %pad_maximum_fusion.4), calls=%async_computation | async-start | bytes 786432 | tf_op jit(solution)/shard_map/all_to_all | solution.py:224
  26.3 7.8 %reshape.152 = bf16[256,8,2,512]{3,2,1,0:T(2,128)(2,1)} reshape(bf16[256,8192]{1,0:T(8,128)(2,1)} %w_mine.1) | data formatting | bytes 8388608 | tf_op jit(solution)/shard_map/reshape | solution.py:289
  34.1 13.5 %dynamic-slice_reduce_fusion = bf16[256,8,512]{2,1,0:T(8,128)(2,1)S(1)} fusion(bf16[256,8,2,512]{3,2,1,0:T(2,128)(2,1)} %reshape.152, s32[]{:T(128)S(6)} %select_n.60), kind=kLoop, calls=%fused_computation | loop fusion | bytes 4194308 | tf_op jit(solution)/shard_map/jit(dynamic_index_in_dim)/dynamic_slice | solution.py:290
  47.6 2.3 %copy.116 = bf16[32,8,8,512]{3,1,2,0:T(8,128)(2,1)} copy(bf16[32,8,8,512]{3,2,1,0:T(8,128)(2,1)S(1)} %bitcast.119) | data formatting | bytes 4194304
  51.3 1.3 collective-permute-start.2
  52.5 1.5 collective-permute-start.1
  56.9 7.2 %all-to-all-start.1 = ((bf16[16,4,1664]{2,1,0:T(4,128)(2,1)}), bf16[16,4,1664]{2,1,0:T(4,128)(2,1)S(1)}, u32[]{:S(2)}, u32[]{:S(2)}) async-start(bf16[16,4,1664]{2,1,0:T(4,128)(2,1)} %broadcast_in_dim.18), calls=%async_computation.1 | async-start | bytes 425984 | tf_op jit(solution)/shard_map/all_to_all | solution.py:57
  64.1 1.8 collective-permute-done.1
  65.9 2.8 %collective-permute-start.4 = (bf16[2,128,512]{2,1,0:T(8,128)(2,1)S(1)}, bf16[2,128,512]{2,1,0:T(8,128)(2,1)}, u32[]{:S(2)}, u32[]{:S(2)}) collective-permute-start(bf16[2,128,512]{2,1,0:T(8,128)(2,1)S(1)} %slice_bitcast_fusion.7), channel_id=1, source_target_pairs={{0,12},{1,13},{2,14},{3,15},{4,0},{5,1},{6,2},{7,3},{8,4},{9,5},{1... | collective-permute-start | bytes 786440 | tf_op jit(solution)/shard_map/ppermute | solution.py:36
  69.6 1.2 fusion.31
  70.8 2.4 %collective-permute-done.4 = bf16[2,128,512]{2,1,0:T(8,128)(2,1)} collective-permute-done((bf16[2,128,512]{2,1,0:T(8,128)(2,1)S(1)}, bf16[2,128,512]{2,1,0:T(8,128)(2,1)}, u32[]{:S(2)}, u32[]{:S(2)}) %collective-permute-start.4) | collective-permute-done | bytes 262176 | tf_op jit(solution)/shard_map/ppermute | solution.py:36
  73.3 3.3 %collective-permute-done.3 = bf16[2,128,512]{2,1,0:T(8,128)(2,1)S(1)} collective-permute-done((bf16[2,128,512]{2,1,0:T(8,128)(2,1)S(1)}, bf16[2,128,512]{2,1,0:T(8,128)(2,1)S(1)}, u32[]{:S(2)}, u32[]{:S(2)}) %collective-permute-start.3) | collective-permute-done | bytes 262176 | tf_op jit(solution)/shard_map/ppermute | solution.py:36
  79.5 5.4 %all-to-all-start.2 = ((f32[16,1,128]{2,1,0:T(1,128)}), f32[16,1,128]{2,1,0:T(1,128)S(1)}, u32[]{:S(2)}, u32[]{:S(2)}) async-start(f32[16,1,128]{2,1,0:T(1,128)} %broadcast_in_dim_broadcast_in_dim_broadcast_in_dim.3), calls=%async_computation.2 | async-start | bytes 16384 | tf_op jit(solution)/shard_map/all_to_all | solution.py:57
  84.9 1.4 pad_maximum_fusion
  86.8 7.5 %all-to-all-done.2 = f32[16,1,128]{2,1,0:T(1,128)S(1)} async-done(((f32[16,1,128]{2,1,0:T(1,128)}), f32[16,1,128]{2,1,0:T(1,128)S(1)}, u32[]{:S(2)}, u32[]{:S(2)}) %all-to-all-start.2) | async-done | bytes 8224 | tf_op jit(solution)/shard_map/all_to_all | solution.py:57
  95.6 5.9 %all-gather.2.cloned.1.call-done = f32[16,8,2304]{2,1,0:T(8,128)} async-done(((f32[1,8,2304]{2,1,0:T(8,128)}), f32[16,8,2304]{2,1,0:T(8,128)}) %all-gather.2.cloned.1.call-update) | async-done | bytes 1179664 | tf_op jit(solution)/shard_map/all_gather | solution.py:234
  101.5 2.6 %reshape.147 = f32[16,4,3,1536]{3,2,1,0:T(4,128)} reshape(f32[16,8,2304]{2,1,0:T(8,128)} %all-gather.2.cloned.1.call-done) | data formatting | bytes 2359296 | tf_op jit(solution)/shard_map/reshape | solution.py:236
  104.1 3.8 %fusion.39 = (f32[16,4,1,1536]{3,2,1,0:T(1,128)S(1)}, f32[16,4,1,1536]{3,2,1,0:T(1,128)S(1)}, f32[16,4,1,1536]{3,2,1,0:T(1,128)S(1)}) fusion(f32[16,4,3,1536]{3,2,1,0:T(4,128)} %reshape.147), kind=kLoop, calls=%fused_computation.96 | loop fusion | flops 98304 | bytes 2359296 | tf_op jit(solution)/shard_map/slice | solution.py:262
  110.1 19.4 %all-to-all-start.3 = ((bf16[16,1,128,128]{3,2,1,0:T(8,128)(2,1)}), bf16[16,1,128,128]{3,2,1,0:T(8,128)(2,1)S(1)}, u32[]{:S(2)}, u32[]{:S(2)}) async-start(bf16[16,1,128,128]{3,2,1,0:T(8,128)(2,1)} %broadcast_in_dim.19), calls=%async_computation.3 | async-start | bytes 1048576 | tf_op jit(solution)/shard_map/all_to_all | solution.py:57
  130.7 1.6 reshape.150.fresh
  135.3 8.1 %shard_map.309 = f32[256,256]{1,0:T(8,128)} custom-call(s32[16]{0:T(128)} %concatenate.57.order, bf16[8,256,512]{2,1,0:T(8,128)(2,1)} %bitcast.118, bf16[8,256,512]{2,1,0:T(8,128)(2,1)} %collective-permute-done.5.other, bf16[16,512,256]{2,1,0:T(8,128)(2,1)} %bitcast.113, bf16[16,512,256]{2,1,0:T(8,128)(2,1)} %bitcast.114), custom_call_target="tpu_custom_call" | custom-call | flops 1073741824 | bytes 8388608 | tf_op jit(solution)/shard_map/pallas_call | solution.py:74
  145.4 8.5 %shard_map.310 = bf16[2,128,256]{2,1,0:T(8,128)(2,1)} custom-call(f32[2,128,256]{2,1,0:T(8,128)} %bitcast.128, bf16[16,1,128,128]{3,2,1,0:T(8,128)(2,1)} %copy-done.2, bf16[64,256]{1,0:T(8,128)(2,1)} %split.65.up, f32[2,128,128]{2,1,0:T(8,128)} %get-tuple-element.48.cosine, f32[2,128,128]{2,1,0:T(8,128)} %get-tuple-element.49.sine, ...), custom_call_target="tpu_custom_call" | custom-call | flops 134217728 | bytes 3145728 | tf_op jit(solution)/shard_map/pallas_call | solution.py:146
  156.5 8.0 %shard_map.311 = bf16[8,256,512]{2,1,0:T(8,128)(2,1)} custom-call(s32[8]{0:T(128)} %stack.80.order, bf16[256,256]{1,0:T(8,128)(2,1)} %bitcast.124, bf16[256,256]{1,0:T(8,128)(2,1)} %copy-done.14, bf16[256,8192]{1,0:T(8,128)(2,1)} %w_mine.1, bf16[256,4096]{1,0:T(8,128)(2,1)} %collective-permute-done.7.w_other), custom_call_target="tpu_custom_call" | custom-call | flops 1073741824 | bytes 6291456 | tf_op jit(solution)/shard_map/pallas_call | solution.py:172
  164.5 1.4 slice_bitcast_fusion.5
  168.5 5.1 %collective-permute-done.10 = bf16[2,128,512]{2,1,0:T(8,128)(2,1)S(1)} collective-permute-done((bf16[2,128,512]{2,1,0:T(8,128)(2,1)S(1)}, bf16[2,128,512]{2,1,0:T(8,128)(2,1)S(1)}, u32[]{:S(2)}, u32[]{:S(2)}) %collective-permute-start.10) | collective-permute-done | bytes 262176 | tf_op jit(solution)/shard_map/ppermute | solution.py:36
  173.6 1.9 collective-permute-done.8
  177.4 2.7 %collective-permute-start.11 = (bf16[2,2,128,512]{3,2,1,0:T(8,128)(2,1)}, bf16[2,2,128,512]{3,2,1,0:T(8,128)(2,1)S(1)}, u32[]{:S(2)}, u32[]{:S(2)}) collective-permute-start(bf16[2,2,128,512]{3,2,1,0:T(8,128)(2,1)} %pad_maximum_fusion.3), channel_id=1, source_target_pairs={{0,12},{1,13},{2,14},{3,15},{4,0},{5,1},{6,2},{7,3},{8,4},{9,5},{1... | collective-permute-start | bytes 1572872 | tf_op jit(solution)/shard_map/ppermute | solution.py:36
  181.1 8.7 %all-to-all-start.4 = ((bf16[16,128,128]{2,1,0:T(8,128)(2,1)}), bf16[16,128,128]{2,1,0:T(8,128)(2,1)S(1)}, u32[]{:S(2)}, u32[]{:S(2)}) async-start(bf16[16,128,128]{2,1,0:T(8,128)(2,1)} %broadcast_in_dim.21), calls=%async_computation.4 | async-start | bytes 1048576 | tf_op jit(solution)/shard_map/all_to_all | solution.py:57
  192.3 5.4 %collective-permute-start.12 = (bf16[2,128,512]{2,1,0:T(8,128)(2,1)S(1)}, bf16[2,128,512]{2,1,0:T(8,128)(2,1)S(1)}, u32[]{:S(2)}, u32[]{:S(2)}) collective-permute-start(bf16[2,128,512]{2,1,0:T(8,128)(2,1)S(1)} %fusion.20), channel_id=1, source_target_pairs={{0,2},{1,3},{2,0},{3,1},{4,6},{5,7},{6,4},{7,5},{8,10},{9,11},{10,... | collective-permute-start | bytes 786440 | tf_op jit(solution)/shard_map/ppermute | solution.py:36
  197.7 10.7 %all-to-all-done.4 = bf16[16,128,128]{2,1,0:T(8,128)(2,1)S(1)} async-done(((bf16[16,128,128]{2,1,0:T(8,128)(2,1)}), bf16[16,128,128]{2,1,0:T(8,128)(2,1)S(1)}, u32[]{:S(2)}, u32[]{:S(2)}) %all-to-all-start.4) | async-done | bytes 524320 | tf_op jit(solution)/shard_map/all_to_all | solution.py:57
  209.6 4.2 %collective-permute-done.12 = bf16[2,128,512]{2,1,0:T(8,128)(2,1)S(1)} collective-permute-done((bf16[2,128,512]{2,1,0:T(8,128)(2,1)S(1)}, bf16[2,128,512]{2,1,0:T(8,128)(2,1)S(1)}, u32[]{:S(2)}, u32[]{:S(2)}) %collective-permute-start.12) | collective-permute-done | bytes 262176 | tf_op jit(solution)/shard_map/ppermute | solution.py:36
  (148 shorter events, 33.8 us)
Async XLA Ops:
  7.3 18.2 %copy-start.21 = (f32[4,512]{1,0:T(4,128)S(1)}, f32[4,512]{1,0:T(4,128)}, u32[]{:S(2)}) copy-start(f32[4,512]{1,0:T(4,128)} %param.40) | copy-start | bytes 24580
  7.3 18.2 %copy-start.27 = (f32[4,256]{1,0:T(4,128)S(1)}, f32[4,256]{1,0:T(4,128)}, u32[]{:S(2)}) copy-start(f32[4,256]{1,0:T(4,128)} %param.41) | copy-start | bytes 12292
  7.3 18.2 %copy-start.28 = (f32[4,256]{1,0:T(4,128)S(1)}, f32[4,256]{1,0:T(4,128)}, u32[]{:S(2)}) copy-start(f32[4,256]{1,0:T(4,128)} %param.42) | copy-start | bytes 12292
  7.3 18.3 %copy-start.22 = (f32[4,512]{1,0:T(4,128)S(1)}, f32[4,512]{1,0:T(4,128)}, u32[]{:S(2)}) copy-start(f32[4,512]{1,0:T(4,128)} %param.43) | copy-start | bytes 24580
  7.3 43.8 %collective-permute-start = (bf16[2,128,512]{2,1,0:T(8,128)(2,1)}, bf16[2,128,512]{2,1,0:T(8,128)(2,1)S(1)}, u32[]{:S(2)}, u32[]{:S(2)}) collective-permute-start(bf16[2,128,512]{2,1,0:T(8,128)(2,1)} %param.22), channel_id=1, source_target_pairs={{0,2},{1,3},{2,0},{3,1},{4,6},{5,7},{6,4},{7,5},{8,10},{9,11},{10,... | collective-permute-start | bytes 786440 | tf_op jit(solution)/shard_map/ppermute | solution.py:36
  19.6 34.4 %all-to-all-start = ((f32[16,4,1536]{2,1,0:T(4,128)}), f32[16,4,1536]{2,1,0:T(4,128)S(1)}, u32[]{:S(2)}, u32[]{:S(2)}) async-start(f32[16,4,1536]{2,1,0:T(4,128)} %pad_maximum_fusion.4), calls=%async_computation | async-start | bytes 786432 | tf_op jit(solution)/shard_map/all_to_all | solution.py:224
  25.3 76.3 %all-gather.2.cloned.1.call-start = ((), (), s32[]{:S(2)}) async-start(), calls=%async_computation.5 | async-start | bytes 1253376 | tf_op jit(solution)/shard_map/all_gather | solution.py:234
  49.9 105.4 %collective-permute-start.7 = (bf16[256,4096]{1,0:T(8,128)(2,1)}, bf16[256,4096]{1,0:T(8,128)(2,1)}, u32[]{:S(2)}, u32[]{:S(2)}) collective-permute-start(bf16[256,4096]{1,0:T(8,128)(2,1)} %bitcast.61), channel_id=1, source_target_pairs={{0,1},{1,0},{2,3},{3,2},{4,5},{5,4},{6,7},{7,6},{8,9},{9,8},{10,11... | collective-permute-start | bytes 6291464 | tf_op jit(solution)/shard_map/ppermute | solution.py:36
  51.3 17.4 %collective-permute-start.2 = (bf16[2,2,128,512]{3,2,1,0:T(8,128)(2,1)S(1)}, bf16[2,2,128,512]{3,2,1,0:T(8,128)(2,1)S(1)}, u32[]{:S(2)}, u32[]{:S(2)}) collective-permute-start(bf16[2,2,128,512]{3,2,1,0:T(8,128)(2,1)S(1)} %get-tuple-element.26), channel_id=1, source_target_pairs={{0,4},{1,5},{2,6},{3,7},{4,8},{5,9},{6,10},{7,11},{8,12},{9,13},{1... | collective-permute-start | bytes 1572872 | tf_op jit(solution)/shard_map/ppermute | solution.py:36
  52.5 13.3 %collective-permute-start.1 = (bf16[2,2,128,512]{3,2,0,1:T(8,128)(2,1)S(1)}, bf16[2,2,128,512]{3,2,0,1:T(8,128)(2,1)S(1)}, u32[]{:S(2)}, u32[]{:S(2)}) collective-permute-start(bf16[2,2,128,512]{3,2,0,1:T(8,128)(2,1)S(1)} %copy.89), channel_id=1, source_target_pairs={{0,12},{1,13},{2,14},{3,15},{4,0},{5,1},{6,2},{7,3},{8,4},{9,5},{1... | collective-permute-start | bytes 1572872 | tf_op jit(solution)/shard_map/ppermute | solution.py:36
  54.1 22.5 %copy-start.12 = (f32[4,1536]{1,0:T(4,128)}, f32[4,1536]{1,0:T(4,128)S(1)}, u32[]{:S(2)}) copy-start(f32[4,1536]{1,0:T(4,128)S(1)} %reduce_sum.48) | copy-start | bytes 73732
  56.9 20.8 %all-to-all-start.1 = ((bf16[16,4,1664]{2,1,0:T(4,128)(2,1)}), bf16[16,4,1664]{2,1,0:T(4,128)(2,1)S(1)}, u32[]{:S(2)}, u32[]{:S(2)}) async-start(bf16[16,4,1664]{2,1,0:T(4,128)(2,1)} %broadcast_in_dim.18), calls=%async_computation.1 | async-start | bytes 425984 | tf_op jit(solution)/shard_map/all_to_all | solution.py:57
  65.9 19.0 %copy-start.5 = (bf16[2,2,128,512]{3,2,0,1:T(8,128)(2,1)}, bf16[2,2,128,512]{3,2,0,1:T(8,128)(2,1)S(1)}, u32[]{:S(2)}) copy-start(bf16[2,2,128,512]{3,2,0,1:T(8,128)(2,1)S(1)} %collective-permute-done.1) | copy-start | bytes 1572868
  65.9 7.4 %collective-permute-start.4 = (bf16[2,128,512]{2,1,0:T(8,128)(2,1)S(1)}, bf16[2,128,512]{2,1,0:T(8,128)(2,1)}, u32[]{:S(2)}, u32[]{:S(2)}) collective-permute-start(bf16[2,128,512]{2,1,0:T(8,128)(2,1)S(1)} %slice_bitcast_fusion.7), channel_id=1, source_target_pairs={{0,12},{1,13},{2,14},{3,15},{4,0},{5,1},{6,2},{7,3},{8,4},{9,5},{1... | collective-permute-start | bytes 786440 | tf_op jit(solution)/shard_map/ppermute | solution.py:36
  68.7 7.9 %collective-permute-start.3 = (bf16[2,128,512]{2,1,0:T(8,128)(2,1)S(1)}, bf16[2,128,512]{2,1,0:T(8,128)(2,1)S(1)}, u32[]{:S(2)}, u32[]{:S(2)}) collective-permute-start(bf16[2,128,512]{2,1,0:T(8,128)(2,1)S(1)} %slice_bitcast_fusion.8), channel_id=1, source_target_pairs={{0,4},{1,5},{2,6},{3,7},{4,8},{5,9},{6,10},{7,11},{8,12},{9,13},{1... | collective-permute-start | bytes 786440 | tf_op jit(solution)/shard_map/ppermute | solution.py:36
  79.5 14.8 %all-to-all-start.2 = ((f32[16,1,128]{2,1,0:T(1,128)}), f32[16,1,128]{2,1,0:T(1,128)S(1)}, u32[]{:S(2)}, u32[]{:S(2)}) async-start(f32[16,1,128]{2,1,0:T(1,128)} %broadcast_in_dim_broadcast_in_dim_broadcast_in_dim.3), calls=%async_computation.2 | async-start | bytes 16384 | tf_op jit(solution)/shard_map/all_to_all | solution.py:57
  86.3 21.7 %copy-start.1 = (bf16[4,2,2,128,512]{4,3,2,1,0:T(8,128)(2,1)}, bf16[4,2,2,128,512]{4,3,2,1,0:T(8,128)(2,1)S(1)}, u32[]{:S(2)}) copy-start(bf16[4,2,2,128,512]{4,3,2,1,0:T(8,128)(2,1)S(1)} %pad_maximum_fusion) | copy-start | bytes 6291460
  86.3 49.0 %collective-permute-start.5 = (bf16[8,256,512]{2,1,0:T(8,128)(2,1)S(1)}, bf16[8,256,512]{2,1,0:T(8,128)(2,1)}, u32[]{:S(2)}, u32[]{:S(2)}) collective-permute-start(bf16[8,256,512]{2,1,0:T(8,128)(2,1)S(1)} %bitcast.117), channel_id=1, source_target_pairs={{0,1},{1,0},{2,3},{3,2},{4,5},{5,4},{6,7},{7,6},{8,9},{9,8},{10,11... | collective-permute-start | bytes 6291464 | tf_op jit(solution)/shard_map/ppermute | solution.py:36
  108.0 24.4 %copy-start.10 = (f32[2,128,64]{2,1,0:T(8,128)S(1)}, f32[2,128,64]{2,1,0:T(8,128)}, u32[]{:S(2)}) copy-start(f32[2,128,64]{2,1,0:T(8,128)} %get-tuple-element.46) | copy-start | bytes 196612
  108.0 24.3 %copy-start.11 = (f32[2,128,64]{2,1,0:T(8,128)S(1)}, f32[2,128,64]{2,1,0:T(8,128)}, u32[]{:S(2)}) copy-start(f32[2,128,64]{2,1,0:T(8,128)} %get-tuple-element.47) | copy-start | bytes 196612
  108.6 24.6 %copy-start.13 = (f32[4,1536]{1,0:T(4,128)S(1)}, f32[4,1536]{1,0:T(4,128)}, u32[]{:S(2)}) copy-start(f32[4,1536]{1,0:T(4,128)} %copy-done.12) | copy-start | bytes 73732
  108.6 24.6 %copy-start.17 = (f32[4,512]{1,0:T(4,128)S(1)}, f32[4,512]{1,0:T(4,128)}, u32[]{:S(2)}) copy-start(f32[4,512]{1,0:T(4,128)} %param.35) | copy-start | bytes 24580
  108.6 24.6 %copy-start.19 = (f32[4,512]{1,0:T(4,128)S(1)}, f32[4,512]{1,0:T(4,128)}, u32[]{:S(2)}) copy-start(f32[4,512]{1,0:T(4,128)} %param.36) | copy-start | bytes 24580
  108.7 34.7 %copy-start.9 = (bf16[64,1536]{1,0:T(8,128)(2,1)}, bf16[64,1536]{1,0:T(8,128)(2,1)S(1)}, u32[]{:S(2)}) copy-start(bf16[64,1536]{1,0:T(8,128)(2,1)S(1)} %reshape.148) | copy-start | bytes 589828
  110.1 34.5 %all-to-all-start.3 = ((bf16[16,1,128,128]{3,2,1,0:T(8,128)(2,1)}), bf16[16,1,128,128]{3,2,1,0:T(8,128)(2,1)S(1)}, u32[]{:S(2)}, u32[]{:S(2)}) async-start(bf16[16,1,128,128]{3,2,1,0:T(8,128)(2,1)} %broadcast_in_dim.19), calls=%async_computation.3 | async-start | bytes 1048576 | tf_op jit(solution)/shard_map/all_to_all | solution.py:57
  154.0 1.9 collective-permute-start.6
  166.0 7.6 %collective-permute-start.10 = (bf16[2,128,512]{2,1,0:T(8,128)(2,1)S(1)}, bf16[2,128,512]{2,1,0:T(8,128)(2,1)S(1)}, u32[]{:S(2)}, u32[]{:S(2)}) collective-permute-start(bf16[2,128,512]{2,1,0:T(8,128)(2,1)S(1)} %get-tuple-element.21), channel_id=1, source_target_pairs={{0,12},{1,13},{2,14},{3,15},{4,0},{5,1},{6,2},{7,3},{8,4},{9,5},{1... | collective-permute-start | bytes 786440 | tf_op jit(solution)/shard_map/ppermute | solution.py:36
  167.1 8.4 %collective-permute-start.8 = (bf16[2,128,512]{2,1,0:T(8,128)(2,1)S(1)}, bf16[2,128,512]{2,1,0:T(8,128)(2,1)S(1)}, u32[]{:S(2)}, u32[]{:S(2)}) collective-permute-start(bf16[2,128,512]{2,1,0:T(8,128)(2,1)S(1)} %get-tuple-element.18), channel_id=1, source_target_pairs={{0,4},{1,5},{2,6},{3,7},{4,8},{5,9},{6,10},{7,11},{8,12},{9,13},{1... | collective-permute-start | bytes 786440 | tf_op jit(solution)/shard_map/ppermute | solution.py:36
  176.5 14.5 %collective-permute-start.9 = (bf16[2,2,128,512]{3,2,1,0:T(8,128)(2,1)}, bf16[2,2,128,512]{3,2,1,0:T(8,128)(2,1)}, u32[]{:S(2)}, u32[]{:S(2)}) collective-permute-start(bf16[2,2,128,512]{3,2,1,0:T(8,128)(2,1)} %pad_maximum_fusion.2), channel_id=1, source_target_pairs={{0,4},{1,5},{2,6},{3,7},{4,8},{5,9},{6,10},{7,11},{8,12},{9,13},{1... | collective-permute-start | bytes 1572872 | tf_op jit(solution)/shard_map/ppermute | solution.py:36
  177.4 13.7 %collective-permute-start.11 = (bf16[2,2,128,512]{3,2,1,0:T(8,128)(2,1)}, bf16[2,2,128,512]{3,2,1,0:T(8,128)(2,1)S(1)}, u32[]{:S(2)}, u32[]{:S(2)}) collective-permute-start(bf16[2,2,128,512]{3,2,1,0:T(8,128)(2,1)} %pad_maximum_fusion.3), channel_id=1, source_target_pairs={{0,12},{1,13},{2,14},{3,15},{4,0},{5,1},{6,2},{7,3},{8,4},{9,5},{1... | collective-permute-start | bytes 1572872 | tf_op jit(solution)/shard_map/ppermute | solution.py:36
  181.1 27.3 %all-to-all-start.4 = ((bf16[16,128,128]{2,1,0:T(8,128)(2,1)}), bf16[16,128,128]{2,1,0:T(8,128)(2,1)S(1)}, u32[]{:S(2)}, u32[]{:S(2)}) async-start(bf16[16,128,128]{2,1,0:T(8,128)(2,1)} %broadcast_in_dim.21), calls=%async_computation.4 | async-start | bytes 1048576 | tf_op jit(solution)/shard_map/all_to_all | solution.py:57
  192.3 21.5 %collective-permute-start.12 = (bf16[2,128,512]{2,1,0:T(8,128)(2,1)S(1)}, bf16[2,128,512]{2,1,0:T(8,128)(2,1)S(1)}, u32[]{:S(2)}, u32[]{:S(2)}) collective-permute-start(bf16[2,128,512]{2,1,0:T(8,128)(2,1)S(1)} %fusion.20), channel_id=1, source_target_pairs={{0,2},{1,3},{2,0},{3,1},{4,6},{5,7},{6,4},{7,5},{8,10},{9,11},{10,... | collective-permute-start | bytes 786440 | tf_op jit(solution)/shard_map/ppermute | solution.py:36
  (18 other events, 221.1 us)
Sparse Core Ops, SparseCore 0:
  27.9 73.5 all-gather.1

commit v2 on v1

v2 whole, which is shorter than its diff:
```python
import functools
import math

import jax
import jax.numpy as jnp
from jax import lax
from jax.experimental import pallas as pl
from jax.experimental.pallas import tpu as pltpu
from jax.sharding import PartitionSpec as P

HEAD = 128
PARAMS = 1572864
N = 16

beta_one = 0.9
beta_two = 0.999
bias_one = 1.0 - math.exp(1000.0 * math.log(0.9))
bias_two = 1.0 - math.exp(1000.0 * math.log(0.999))
adam_eps = 1e-08
learn_rate = 0.005
norm_eps = 1e-06
rope_base = 1000000.0

bf16 = jnp.bfloat16
f32 = jnp.float32


def adam_update(factor, gradient, moment, square, clip_factor):
    scaled = clip_factor * gradient
    moment_new = beta_one * moment + (1.0 - beta_one) * scaled
    square_new = beta_two * square + (1.0 - beta_two) * scaled * scaled
    update = moment_new / bias_one / (jnp.sqrt(square_new / bias_two) + adam_eps)
    return (factor - learn_rate * update, moment_new, square_new)


def shift(value, move):
    return lax.ppermute(value, "tp", [(i, move(i)) for i in range(N)])


def to_core(value):
    return shift(value, lambda i: i ^ 1)


def to_z(value):
    return shift(value, lambda i: i ^ 2)


def to_replica(value, bit):
    return lax.ppermute(value, "rep", [(i, i ^ bit) for i in range(N)])


def to_right(value):
    return shift(value, lambda i: (i + 4) % N)


def to_left(value):
    return shift(value, lambda i: (i + 12) % N)


def dot(a, b, contract=((1,), (0,))):
    return lax.dot_general(a, b, (contract, ((), ())), preferred_element_type=f32)


VMEM = pl.BlockSpec(memory_space=pltpu.VMEM)
SMEM = pl.BlockSpec(memory_space=pltpu.SMEM)
ANY = pl.BlockSpec(memory_space=pl.ANY)
HBM = pl.BlockSpec(memory_space=pltpu.HBM)
LARGE, SMALL = 60 << 20, 24 << 20
CHAIN = 48 << 20
WIDTHS = (512, 256, 256, 512)
BLOCKS = [(i, c) for i, w in enumerate(WIDTHS) for c in range(0, w, HEAD)]


class Fetched:
    def __init__(self, copy, ref):
        self.copy, self.ref, self.waited = copy, ref, False

    def there(self):
        if not self.waited:
            self.copy.wait()
            self.waited = True
        return self.ref

    def __getitem__(self, index):
        return self.there()[index]


def call(kernel, shapes, *args, scalars=0, fetch=(), take=(), tokens=(), room=(), limit=LARGE, flops=0, moved=1 << 20):
    out = [jax.ShapeDtypeStruct(s, d) for s, d in shapes]
    single = len(out) == 1
    parts = [f if isinstance(f, tuple) else (f, f.shape, None) for f in (*fetch, *take)]
    first, count = len(args), len(args) + len(parts)
    skip = count + len(tokens)

    def body(*refs):
        ins, outs = refs[:count], refs[skip : skip + len(out)]
        scratch = refs[skip + len(out) :]
        held = []
        for i, (_, _, view) in enumerate(parts):
            source = ins[first + i]
            if view is not None:
                source = view(source, *ins[:scalars])
            copy = pltpu.make_async_copy(source, scratch[i], scratch[len(parts)].at[i])
            copy.start()
            held.append(Fetched(copy, scratch[i]))
        kernel(*ins[:first], *held, *outs, *scratch[len(scratch) - len(room) :])
        for one in held:
            one.there()

    return pl.pallas_call(
        body,
        in_specs=[SMEM] * scalars
        + [VMEM] * (first - scalars)
        + [HBM] * len(fetch)
        + [ANY] * (len(take) + len(tokens)),
        out_specs=VMEM if single else [VMEM] * len(out),
        out_shape=out[0] if single else out,
        scratch_shapes=[pltpu.VMEM(shape, one.dtype) for one, shape, _ in parts]
        + ([pltpu.SemaphoreType.DMA((len(parts),))] if parts else [])
        + list(room),
        cost_estimate=pl.CostEstimate(flops=flops, bytes_accessed=moved, transcendentals=0),
        compiler_params=pltpu.CompilerParams(vmem_limit_bytes=limit),
    )(*args, *[one for one, _, _ in parts], *tokens)


def join_kernel(shape, places):
    def body(*refs):
        out = refs[-2]
        copies = [
            pltpu.make_async_copy(refs[i].at[source], out.at[target], refs[-1].at[n])
            for n, (i, source, target) in enumerate(places)
        ]
        for copy in copies:
            copy.start()
        for copy in copies:
            copy.wait()

    return body


def join(shape, places, *arrays, token=None):
    arrays = arrays if token is None else arrays + (token,)
    body = join_kernel(shape, places)

    def kernel(*refs):
        body(*refs[: len(arrays)], *refs[len(arrays) :])

    return pl.pallas_call(
        kernel,
        in_specs=[ANY] * len(arrays),
        out_specs=VMEM,
        out_shape=jax.ShapeDtypeStruct(shape, arrays[0].dtype),
        scratch_shapes=[pltpu.SemaphoreType.DMA((len(places),))],
        cost_estimate=pl.CostEstimate(flops=0, bytes_accessed=1 << 20, transcendentals=0),
        compiler_params=pltpu.CompilerParams(vmem_limit_bytes=SMALL),
    )(*arrays)


ALL, ONE, TWO = pl.ds(0, 256), pl.ds(0, 128), pl.ds(128, 128)


def both_of(held, bit):
    near, far = pl.ds(0, bit), pl.ds(bit, bit)
    return join(
        (2 * bit, 144, HEAD), [(0, near, near), (1, near, far)], held, to_replica(held, bit)
    )


def beyond(left, right, token=None):
    return (
        to_right(join((128, 512), [(0, ONE, ONE)], left, token=token)),
        to_left(join((128, 512), [(0, TWO, ONE)], right, token=token)),
    )


def along_x(own, right, far_a, far_b, left):
    places = [(0, ALL, (0, ALL)), (1, ALL, (1, ALL)), (4, ALL, (3, ALL))]
    places += [(2, ONE, (2, ONE)), (3, ONE, (2, TWO))]
    return join((4, 256, 512), places, own, right, far_a, far_b, left)


def stacked(pieces):
    return jnp.concatenate(pieces, axis=0)


def pack_gradients(a, b, c, d, out):
    refs = (a, b, c, d)
    for r in range(N):
        for j in range(0, 12, 2):
            out[r, 4 * j : 4 * j + 8] = stacked(
                [
                    refs[i][0, 4 * r : 4 * r + 4, at : at + HEAD]
                    for i, at in BLOCKS[j : j + 2]
                ]
            )


def pack_state(*refs):
    out = refs[-1]
    for q in range(3):
        rows = stacked([refs[4 * q + i][:, at : at + HEAD] for i, at in BLOCKS])
        out[0, 48 * q : 48 * q + 48] = rows.astype(bf16)


def sum_gradients(parts, summed, message):
    total = jnp.sum(parts[...], axis=0)
    for j, (i, at) in enumerate(BLOCKS):
        summed[:, j * HEAD : (j + 1) * HEAD] = total[4 * j : 4 * j + 4]
    squares = jnp.full((16, HEAD), jnp.sum(total * total))
    high = squares.astype(bf16).astype(f32)
    rows = lax.broadcasted_iota(jnp.int32, (16, HEAD), 0)
    tail = jnp.where(rows == 0, high, squares - high)
    whole = jnp.concatenate([total, tail], axis=0).astype(bf16)
    message[...] = jnp.broadcast_to(whole[None], message.shape)


def column_squares(parts, message):
    tails = parts[:, 48:64, 0:HEAD].astype(f32)
    rows = lax.broadcasted_iota(jnp.int32, tails.shape, 1)
    lanes = lax.broadcasted_iota(jnp.int32, tails.shape, 2)
    total = jnp.sum(jnp.where((rows < 2) & (lanes == 0), tails, 0.0))
    message[...] = jnp.full(message.shape, total)


def clip_of(squares):
    total = jnp.sum(jnp.max(squares[:, 0], axis=1, keepdims=True), axis=0, keepdims=True)
    return jnp.minimum(1.0, math.sqrt(PARAMS) / (jnp.sqrt(total) + norm_eps))


def make_copies(
    me, hidden, squares, parts, state_near, state_far, message, up, out_down, out_up, copies
):
    clip = clip_of(squares)
    for r in range(N):
        place = me[0] ^ r
        near, far = state_near[place & 7], state_far[place & 7]
        state = jnp.where(place < 8, near, far).astype(f32)
        new, _, _ = adam_update(
            state[0:48], parts[r, 0:48].astype(f32), state[48:96], state[96:144], clip
        )
        copies[r] = new

    def block(j):
        return stacked([copies[r, 4 * j : 4 * j + 4] for r in range(N)]).astype(bf16)

    blocks = [block(j) for j in range(12)]
    low = dot(hidden[...], jnp.concatenate(blocks[0:4], axis=1), ((1,), (1,)))
    low = jnp.concatenate([low[:128], low[128:]], axis=1).astype(bf16)
    message[...] = jnp.broadcast_to(low[None], message.shape)
    for target, first, last in ((up, 4, 6), (out_down, 6, 8), (out_up, 8, 12)):
        for j in range(first, last):
            target[:, (j - first) * HEAD : (j - first + 1) * HEAD] = blocks[j]


def update_state(*refs):
    squares, ins, summed, outs = refs[0], refs[1:13], refs[13], refs[14:]
    clip = clip_of(squares)
    at = 0
    for i, width in enumerate(WIDTHS):
        results = adam_update(
            ins[i][...], summed[:, at : at + width], ins[4 + i][...], ins[8 + i][...], clip
        )
        for q in range(3):
            outs[4 * q + i][...] = results[q]
        at += width


def base_queries(dz, order, weight, *refs):
    before = refs[0] if dz == 1 else None
    mine, other, out = refs[dz:]
    total = jnp.zeros((256, 256), f32)
    weight = weight.there()
    for dx in range(4):
        for flip, pieces in enumerate((mine, other)):
            place = order[2 * dx + dz] ^ flip
            total += dot(pieces[dx], weight[pl.ds(pl.multiple_of(place * 512, 512), 512), :])
    out[...] = total if before is None else total + before[...]


ROWS = 16


def attention(low, base, up, tables, cache, fresh, out):
    ups = up[...]
    zero = jnp.zeros_like(ups)
    lows = jnp.sum(low[...].astype(f32), axis=0).astype(bf16)
    turned = []
    for step in range(2):
        both = jnp.concatenate([ups, zero] if step == 0 else [zero, ups], axis=0)
        query = base[step * 128 : (step + 1) * 128] + 0.5 * dot(lows, both)
        for head in range(2):
            one = query[:, head * HEAD : (head + 1) * HEAD]
            one = one * tables[step] + pltpu.roll(one, HEAD // 2, 1) * tables[2 + step]
            turned.append((one * (1.0 / math.sqrt(HEAD))).astype(bf16))
    shape = (4 * ROWS, ROWS * 32)
    slots = lax.broadcasted_iota(jnp.int32, shape, 1)
    rows = lax.broadcasted_iota(jnp.int32, shape, 0) & (ROWS - 1)
    own = (slots >> 5) == rows
    slots = (slots & 31).astype(f32)
    new_shape = (4 * ROWS, ROWS * 2)
    new_slots = lax.broadcasted_iota(jnp.int32, new_shape, 1)
    new_index = lax.broadcasted_iota(jnp.int32, new_shape, 0)
    new_live = ((new_slots >> 1) == (new_index & (ROWS - 1))) & (
        (new_slots & 1) <= (new_index >> 5)
    )
    for k in range(128 // ROWS):
        at = k * ROWS
        queries = stacked([one[at : at + ROWS] for one in turned])
        held = cache[at * 32 : (at + ROWS) * 32]
        new = fresh[at * 2 : (at + ROWS) * 2]
        scores = dot(queries, held[:, :HEAD], ((1,), (1,)))
        new_scores = dot(queries, new[:, :HEAD], ((1,), (1,)))
        length = stacked([tables[4, at : at + ROWS]] * 4)
        length = jnp.concatenate([length] * (shape[1] // HEAD), axis=1)
        scores = jnp.where(own & (slots < length), scores, -1e30)
        new_scores = jnp.where(new_live, new_scores, -1e30)
        top = jnp.maximum(
            jnp.max(scores, axis=1, keepdims=True), jnp.max(new_scores, axis=1, keepdims=True)
        )
        weights = jnp.exp(scores - top)
        new_weights = jnp.exp(new_scores - top)
        total = jnp.sum(weights, axis=1, keepdims=True)
        total = total + jnp.sum(new_weights, axis=1, keepdims=True)
        inverse = 1.0 / total
        result = dot((weights * inverse).astype(bf16), held[:, HEAD:])
        result = result + dot((new_weights * inverse).astype(bf16), new[:, HEAD:])
        for step in range(2):
            for head in range(2):
                first = (step * 2 + head) * ROWS
                out[
                    step * 128 + at : step * 128 + at + ROWS, head * HEAD : (head + 1) * HEAD
                ] = result[first : first + ROWS].astype(bf16)


def give_columns(core, *refs):
    weight, out = refs[:8], refs[8]
    for k in range(8):
        out[:, k * 512 : (k + 1) * 512] = weight[k][...]


def columns(k, other):
    def view(ref, order):
        place = order[k] >> 1 if other else order[k]
        return ref.at[:, pl.ds(pl.multiple_of(place * 512, 512), 512)]

    return view


def columns_of(weights, k):
    return [(w, (256, 512), columns(k, i == 1)) for i, w in enumerate(weights)]


def lay_out(counts, order, *refs):
    total = sum(counts)
    blocks, outs = list(refs[: 2 * total]), refs[2 * total :]
    for out, count in zip(outs, counts):
        for i in range(count):
            out[i, :256] = blocks.pop(0)[...]
            out[i, 256:] = blocks.pop(0)[...]


def project_far(mine, other, weight, down, down_other, right, left, low):
    inner = dot(mine[...], down[...], ((1,), (1,))) + dot(
        other[...], down_other[...], ((1,), (1,))
    )
    packed = jnp.concatenate([inner[32 * i : 32 * i + 32] for i in range(8)], axis=1)
    low[...] = packed
    right[128:] = packed.astype(bf16)
    left[128:] = packed.astype(bf16)
    both = jnp.concatenate([mine[...], other[...]], axis=1)
    result = dot(both, weight[0])
    right[:128] = result[:128].astype(bf16)
    left[:128] = result[128:].astype(bf16)


def project_near(mine, other, weight, *targets):
    both = jnp.concatenate([mine[...], other[...]], axis=1)
    for i, target in enumerate(targets):
        target[...] = dot(both, weight[i])


def project_later(mine, other, weight, right, left, *targets):
    both = jnp.concatenate([mine[...], other[...]], axis=1)
    result = dot(both, weight[0])
    right[...] = result[:128].astype(bf16)
    left[...] = result[128:].astype(bf16)
    for i, target in enumerate(targets):
        target[...] = dot(both, weight[i + 1])


def forward(right, left, from_left, from_right, go_right, go_left):
    go_right[:128] = (right[:128] + from_left[:128].astype(f32)).astype(bf16)
    go_right[128:256] = right[128:].astype(bf16)
    go_left[:128] = left[:128].astype(bf16)
    go_left[128:256] = (left[128:] + from_right[:128].astype(f32)).astype(bf16)
    if go_right.shape[0] > 256:
        go_right[256:] = from_left[128:]
        go_left[256:] = from_right[128:]


def add_x(keep, low, from_left, from_right, far_left, far_right, message):
    message[:256] = (
        keep[...] + far_left[:256].astype(f32) + far_right[:256].astype(f32)
    ).astype(bf16)
    message[256:] = (
        low[...]
        + from_left[128:].astype(f32)
        + from_right[128:].astype(f32)
        + far_left[256:].astype(f32)
    ).astype(bf16)


def own_part(keep, far_left, far_right, hidden, out):
    out[...] = (
        hidden[...].astype(f32)
        + keep[...]
        + far_left[...].astype(f32)
        + far_right[...].astype(f32)
    )


def finish(own, message, from_z, out_up, out):
    packed = (message[256:].astype(f32) + from_z[256:].astype(f32)).astype(bf16)
    inner = stacked([packed[:, 64 * i : 64 * i + 64] for i in range(8)])
    out[...] = (
        own[...] + from_z[:256].astype(f32) + 0.5 * dot(inner, out_up[...])
    ).astype(bf16)


def on_device(
    hidden,
    query_base_weight,
    output_base_weight,
    cache,
    fresh,
    lengths,
    grad_query_down,
    grad_query_up,
    grad_output_down,
    grad_output_up,
    *state,
):
    rank = lax.axis_index("tp")
    core = rank % 2
    z_hi = (rank // 2) % 2
    x = rank // 4

    steps = jnp.arange(8, dtype=jnp.int32)
    order = ((x + steps // 2) % 4) * 4 + (z_hi ^ (steps % 2)) * 2 + core

    gradient = call(
        pack_gradients,
        [((N, 48, HEAD), f32)],
        fetch=(grad_query_down, grad_query_up, grad_output_down, grad_output_up),
    )
    parts = lax.all_to_all(gradient, "rep", 0, 0)

    hidden = hidden.reshape(256, 512)
    left = to_right(hidden)
    right = to_left(hidden)
    held = call(pack_state, [((1, 144, HEAD), bf16)], fetch=state)
    held = both_of(held, 1)
    held = both_of(held, 2)

    summed, message = call(
        sum_gradients,
        [((4, 1536), f32), ((N, 64, HEAD), bf16)],
        parts,
        tokens=(left, right, held),
        moved=CHAIN,
        limit=SMALL,
    )
    all_parts = lax.all_to_all(message, "rep", 0, 0)
    far_a, far_b = beyond(left, right)
    held = both_of(held, 4)

    squares_sent = call(
        column_squares,
        [((N, 8, HEAD), f32)],
        all_parts,
        moved=CHAIN,
        limit=SMALL,
    )
    squares = lax.all_to_all(squares_sent, "tp", 0, 0)
    zed = to_z(join((256, 512), [(0, ALL, ALL)], hidden, token=summed))
    held_far = to_replica(held, 8)
    set_h = along_x(hidden, right, far_a, far_b, left)
    set_h_other = to_core(set_h)

    def given(k):
        return lambda ref, core: ref.at[
            :, pl.ds(pl.multiple_of((2 * k + 1 - core[0]) * 512, 512), 512)
        ]

    give = call(
        give_columns,
        [((256, 4096), bf16)],
        core.reshape(1),
        scalars=1,
        fetch=[(output_base_weight, (256, 512), given(k)) for k in range(8)],
        moved=4 << 20,
    )
    weights = (output_base_weight, to_core(give))
    used = ((5,), (3, 7), (4, 1, 2, 6, 0))
    counts = tuple(map(len, used))
    w_far, w_near, w_later = call(
        functools.partial(lay_out, counts),
        [((count, 512, 512), bf16) for count in counts],
        order,
        scalars=1,
        fetch=[one for ks in used for k in ks for one in columns_of(weights, k)],
        moved=8 << 20,
    )

    message, up, out_down, out_up = call(
        make_copies,
        [((N, 128, HEAD), bf16), ((64, 256), bf16), ((64, 256), bf16), ((64, 512), bf16)],
        lax.axis_index("rep").reshape(1),
        scalars=1,
        fetch=(hidden,),
        take=(squares, all_parts, held, held_far),
        moved=CHAIN,
        room=[pltpu.VMEM((N, 48, HEAD), f32)],
    )
    lows = lax.all_to_all(message, "tp", 0, 0)
    out_down_other = to_core(out_down)
    updated = call(
        update_state,
        [((4, w), f32) for _ in range(3) for w in WIDTHS],
        squares,
        fetch=state,
        take=(summed,),
    )
    left_z = to_right(zed)
    right_z = to_left(zed)
    set_z = along_x(zed, right_z, *beyond(left_z, right_z), left_z)
    set_z_other = to_core(set_z)
    cost = dict(scalars=1, flops=256 * 8192 * 256, moved=4 << 20)
    base = call(
        functools.partial(base_queries, 0),
        [((256, 256), f32)],
        order,
        fetch=(query_base_weight,),
        take=(set_h, set_h_other),
        **cost,
    )
    base = call(
        functools.partial(base_queries, 1),
        [((256, 256), f32)],
        order,
        fetch=(query_base_weight,),
        take=(base, set_z, set_z_other),
        **cost,
    )

    frequency = jnp.power(rope_base, -2.0 * jnp.arange(64, dtype=f32) / HEAD)
    positions = (lengths[None, :] + jnp.arange(2, dtype=jnp.int32)[:, None]).astype(f32)
    angles = positions[:, :, None] * frequency
    cosine = jnp.cos(angles)
    sine = jnp.sin(angles)
    tables = jnp.concatenate(
        [
            jnp.concatenate([cosine, cosine], axis=2),
            jnp.concatenate([-sine, sine], axis=2),
            jnp.broadcast_to(lengths.astype(f32)[None, :, None], (1, 128, HEAD)),
        ]
    )
    attended = call(
        attention,
        [((256, 256), bf16)],
        lows,
        base,
        up,
        tables,
        cache.reshape(4096, 256),
        fresh.reshape(256, 256),
        tokens=(w_far,),
        limit=SMALL,
        flops=2 * 512 * 512 * 256,
        moved=4 << 20,
    )

    attended_other = to_core(attended)
    far_right, far_left, low = call(
        project_far,
        [((160, 512), bf16), ((160, 512), bf16), ((32, 512), f32)],
        attended,
        attended_other,
        w_far,
        out_down,
        out_down_other,
        limit=SMALL,
        flops=2 * 256 * 512 * 512,
        moved=1 << 20,
    )
    from_left = to_right(far_right)
    from_right = to_left(far_left)
    near_right, near_left = call(
        project_near,
        [((256, 512), f32)] * 2,
        attended,
        attended_other,
        w_near,
        limit=SMALL,
        flops=2 * 256 * 512 * 1024,
        moved=2 << 20,
    )
    later_right, later_left, keep, later_near_right, later_near_left, later_keep = call(
        project_later,
        [((128, 512), bf16)] * 2 + [((256, 512), f32)] * 4,
        attended,
        attended_other,
        w_later,
        limit=SMALL,
        flops=2 * 256 * 512 * 2560,
        moved=5 << 20,
    )
    later_from_left = to_right(later_right)
    later_from_right = to_left(later_left)
    go_right, go_left = call(
        forward,
        [((288, 512), bf16)] * 2,
        near_right,
        near_left,
        from_left,
        from_right,
        limit=SMALL,
    )
    got_left = to_right(go_right)
    got_right = to_left(go_left)
    later_go_right, later_go_left = call(
        forward,
        [((256, 512), bf16)] * 2,
        later_near_right,
        later_near_left,
        later_from_left,
        later_from_right,
        limit=SMALL,
    )
    later_got_left = to_right(later_go_right)
    later_got_right = to_left(later_go_left)
    message = call(
        add_x,
        [((288, 512), bf16)],
        keep,
        low,
        from_left,
        from_right,
        got_left,
        got_right,
        limit=SMALL,
    )
    from_z = to_z(message)
    own = call(
        own_part,
        [((256, 512), f32)],
        later_keep,
        later_got_left,
        later_got_right,
        fetch=(hidden,),
        limit=SMALL,
    )
    decoded = call(
        finish, [((256, 512), bf16)], own, message, from_z, take=(out_up,), limit=SMALL
    )
    return (decoded.reshape(2, 128, 512), *updated)


def solution(mesh):
    return jax.shard_map(
        on_device,
        mesh=mesh,
        in_specs=(
            P(None, "rep", "tp"),
            P(None, "tp"),
            P("tp", None),
            P("rep", "tp", None, None),
            P("rep", "tp", None, None),
            P("rep"),
        )
        + (P("rep", None, "tp"),) * 4
        + (P("rep", "tp"),) * 12,
        out_specs=(P(None, "rep", "tp"),) + (P("rep", "tp"),) * 12,
        check_vma=False,
    )
```

time: 223 us -> 155 us (0.70)
  the two profiles are of different devices: /device:TPU:1 before, /device:TPU:78 now
where the time goes in v2:
time: 155 us; the launch traced here: 152 us
  starting transfers between devices  63.2 us (41%)
  waiting for transfers between devices  39.6 us (26%)
  Pallas kernels  39.1 us (25%)
  local copies, waits for them, and re-layouts  7.56 us (5%)
    pallas_call x19, Pallas kernels, call(): pl.pallas_call(body, in_specs=[SMEM] * scalars + [VMEM] * (first - scalar...  34.9 us
    ppermute x23, starting transfers between devices, shift(): return lax.ppermute(value, 'tp', [(i, move(i)) for i in range(N)])  28.5 us
    ppermute x23, waiting for transfers between devices, shift(): return lax.ppermute(value, 'tp', [(i, move(i)) for i in range(N)])  26.8 us
    ppermute x4, waiting for transfers between devices, to_replica(): return lax.ppermute(value, 'rep', [(i, i ^ bit) for i in range(N)])  8.75 us
    all_to_all x1, starting transfers between devices, on_device(): all_parts = lax.all_to_all(message, 'rep', 0, 0)  8.2 us
    all_to_all x1, starting transfers between devices, on_device(): parts = lax.all_to_all(gradient, 'rep', 0, 0)  8.1 us
    all_to_all x1, starting transfers between devices, on_device(): squares = lax.all_to_all(squares_sent, 'tp', 0, 0)  8 us
    unnamed x44, local copies, waits for them, and re-layouts  6.52 us
  transfers between devices with their start and end apart: 31, of which 15 were waited for; matrix products, arithmetic and copies ran while one was open for 1% of the time, Pallas kernels for 21%

profile of v2, /device:TPU:78, one launch (start us, length us, event | category | flops | bytes accessed | tf_op | source)
XLA Modules:
  0.0 152.0 jit_solution(15545866217895698026)
XLA Ops:
  0.6 1.9 %shard_map.309 = f32[16,48,128]{2,1,0:T(8,128)} custom-call(f32[1,64,512]{2,1,0:T(8,128)} %refs_0_.2, f32[1,64,256]{2,1,0:T(8,128)} %refs_1_.7, f32[1,64,256]{2,1,0:T(8,128)} %refs_2_.4, f32[1,64,512]{2,1,0:T(8,128)} %refs_3_.5), custom_call_target="tpu_custom_call" | custom-call | bytes 1048576 | tf_op jit(solution)/shard_map/pallas_call | solution.py:110
  2.5 8.1 %all-to-all-start = ((f32[16,48,128]{2,1,0:T(8,128)}), f32[16,48,128]{2,1,0:T(8,128)S(1)}, u32[]{:S(2)}, u32[]{:S(2)}) async-start(f32[16,48,128]{2,1,0:T(8,128)} %shard_map.309), calls=%async_computation | async-start | bytes 786432 | tf_op jit(solution)/shard_map/all_to_all | solution.py:456
  10.6 3.0 %shard_map.326 = bf16[256,4096]{1,0:T(8,128)(2,1)} custom-call(s32[1]{0:T(128)} %bitcast.3.refs_0_, bf16[256,8192]{1,0:T(8,128)(2,1)} %refs_15_.1, bf16[256,8192]{1,0:T(8,128)(2,1)} %refs_15_.1, bf16[256,8192]{1,0:T(8,128)(2,1)} %refs_15_.1, bf16[256,8192]{1,0:T(8,128)(2,1)} %refs_15_.1, bf16[256,8192]{1,0:T(8,128)(2,1)} %refs_15_.1, ...), custom_call_target="tpu_custom_call" | custom-call | bytes 4194304 | tf_op jit(solution)/shard_map/pallas_call | solution.py:110
  18.9 2.7 %collective-permute-done.2.refs_1_ = bf16[1,144,128]{2,1,0:T(8,128)(2,1)S(1)} collective-permute-done((bf16[1,144,128]{2,1,0:T(8,128)(2,1)}, bf16[1,144,128]{2,1,0:T(8,128)(2,1)S(1)}, u32[]{:S(2)}, u32[]{:S(2)}) %collective-permute-start.2) | collective-permute-done | bytes 36896 | tf_op jit(solution)/shard_map/ppermute | solution.py:49
  23.4 4.5 %collective-permute-done.3.refs_1_ = bf16[2,144,128]{2,1,0:T(8,128)(2,1)S(1)} collective-permute-done((bf16[2,144,128]{2,1,0:T(8,128)(2,1)S(1)}, bf16[2,144,128]{2,1,0:T(8,128)(2,1)S(1)}, u32[]{:S(2)}, u32[]{:S(2)}) %collective-permute-start.3) | collective-permute-done | bytes 73760 | tf_op jit(solution)/shard_map/ppermute | solution.py:49
  29.1 4.6 %collective-permute-start.9 = (bf16[256,512]{1,0:T(8,128)(2,1)S(1)}, bf16[256,512]{1,0:T(8,128)(2,1)S(1)}, u32[]{:S(2)}, u32[]{:S(2)}) collective-permute-start(bf16[256,512]{1,0:T(8,128)(2,1)S(1)} %shard_map.321), channel_id=1, source_target_pairs={{0,2},{1,3},{2,0},{3,1},{4,6},{5,7},{6,4},{7,5},{8,10},{9,11},{10,... | collective-permute-start | bytes 786440 | tf_op jit(solution)/shard_map/ppermute | solution.py:37
  33.6 8.2 %all-to-all-start.1 = ((bf16[16,64,128]{2,1,0:T(8,128)(2,1)}), bf16[16,64,128]{2,1,0:T(8,128)(2,1)S(1)}, u32[]{:S(2)}, u32[]{:S(2)}) async-start(bf16[16,64,128]{2,1,0:T(8,128)(2,1)} %get-tuple-element.49), calls=%async_computation.1 | async-start | bytes 524288 | tf_op jit(solution)/shard_map/all_to_all | solution.py:473
  41.8 4.4 %collective-permute-done.9.refs_0_ = bf16[256,512]{1,0:T(8,128)(2,1)S(1)} collective-permute-done((bf16[256,512]{1,0:T(8,128)(2,1)S(1)}, bf16[256,512]{1,0:T(8,128)(2,1)S(1)}, u32[]{:S(2)}, u32[]{:S(2)}) %collective-permute-start.9) | collective-permute-done | bytes 262176 | tf_op jit(solution)/shard_map/ppermute | solution.py:37
  46.3 2.2 %collective-permute-start.11 = (bf16[256,512]{1,0:T(8,128)(2,1)S(1)}, bf16[256,512]{1,0:T(8,128)(2,1)S(1)}, u32[]{:S(2)}, u32[]{:S(2)}) collective-permute-start(bf16[256,512]{1,0:T(8,128)(2,1)S(1)} %collective-permute-done.9.refs_0_), channel_id=1, source_target_pairs={{0,4},{1,5},{2,6},{3,7},{4,8},{5,9},{6,10},{7,11},{8,12},{9,13},{1... | collective-permute-start | bytes 786440 | tf_op jit(solution)/shard_map/ppermute | solution.py:37
  48.7 3.2 %collective-permute-start.6 = (bf16[128,512]{1,0:T(8,128)(2,1)S(1)}, bf16[128,512]{1,0:T(8,128)(2,1)S(1)}, u32[]{:S(2)}, u32[]{:S(2)}) collective-permute-start(bf16[128,512]{1,0:T(8,128)(2,1)S(1)} %shard_map.317), channel_id=1, source_target_pairs={{0,4},{1,5},{2,6},{3,7},{4,8},{5,9},{6,10},{7,11},{8,12},{9,13},{1... | collective-permute-start | bytes 393224 | tf_op jit(solution)/shard_map/ppermute | solution.py:37
  55.4 2.1 %collective-permute-start.5 = (bf16[8,144,128]{2,1,0:T(8,128)(2,1)S(1)}, bf16[8,144,128]{2,1,0:T(8,128)(2,1)}, u32[]{:S(2)}, u32[]{:S(2)}) collective-permute-start(bf16[8,144,128]{2,1,0:T(8,128)(2,1)S(1)} %shard_map.315.refs_4_), channel_id=1, source_target_pairs={{0,128},{16,144},{32,160},{48,176},{64,192},{80,208},{96,224},{112... | collective-permute-start | bytes 884744 | tf_op jit(solution)/shard_map/ppermute | solution.py:49
  58.3 2.1 %collective-permute-start.12 = (bf16[128,512]{1,0:T(8,128)(2,1)}, bf16[128,512]{1,0:T(8,128)(2,1)S(1)}, u32[]{:S(2)}, u32[]{:S(2)}) collective-permute-start(bf16[128,512]{1,0:T(8,128)(2,1)} %shard_map.322), channel_id=1, source_target_pairs={{0,4},{1,5},{2,6},{3,7},{4,8},{5,9},{6,10},{7,11},{8,12},{9,13},{1... | collective-permute-start | bytes 393224 | tf_op jit(solution)/shard_map/ppermute | solution.py:37
  62.9 8.0 %all-to-all-start.2 = ((f32[16,8,128]{2,1,0:T(8,128)}), f32[16,8,128]{2,1,0:T(8,128)S(1)}, u32[]{:S(2)}, u32[]{:S(2)}) async-start(f32[16,8,128]{2,1,0:T(8,128)} %shard_map.314), calls=%async_computation.2 | async-start | bytes 131072 | tf_op jit(solution)/shard_map/all_to_all | solution.py:484
  75.0 3.9 %all-to-all-done.2.refs_2_.refs_0_ = f32[16,8,128]{2,1,0:T(8,128)S(1)} async-done(((f32[16,8,128]{2,1,0:T(8,128)}), f32[16,8,128]{2,1,0:T(8,128)S(1)}, u32[]{:S(2)}, u32[]{:S(2)}) %all-to-all-start.2) | async-done | bytes 65568 | tf_op jit(solution)/shard_map/all_to_all | solution.py:484
  79.6 2.8 %shard_map.316 = (bf16[16,128,128]{2,1,0:T(8,128)(2,1)}, bf16[64,256]{1,0:T(8,128)(2,1)}, bf16[64,256]{1,0:T(8,128)(2,1)}, bf16[64,512]{1,0:T(8,128)(2,1)}) custom-call(s32[1]{0:T(128)} %bitcast.refs_0_, bf16[256,512]{1,0:T(8,128)(2,1)} %bitcast.5, f32[16,8,128]{2,1,0:T(8,128)} %copy-done.20, bf16[16,64,128]{2,1,0:T(8,128)(2,1)} %copy-done.5, ...), custom_call_target="tpu_custom_call" | custom-call | bytes 50331648 | tf_op jit(solution)/shard_map/pallas_call | solution.py:110
  82.4 5.8 %all-to-all-start.3 = ((bf16[16,128,128]{2,1,0:T(8,128)(2,1)}), bf16[16,128,128]{2,1,0:T(8,128)(2,1)S(1)}, u32[]{:S(2)}, u32[]{:S(2)}) async-start(bf16[16,128,128]{2,1,0:T(8,128)(2,1)} %get-tuple-element.50), calls=%async_computation.3 | async-start | bytes 1048576 | tf_op jit(solution)/shard_map/all_to_all | solution.py:525
  90.5 4.9 %shard_map.320.refs_2_ = f32[256,256]{1,0:T(8,128)} custom-call(s32[8]{0:T(128)} %fusion.4.refs_0_, bf16[8192,256]{1,0:T(8,128)(2,1)} %refs_1_.10, bf16[4,256,512]{2,1,0:T(8,128)(2,1)} %copy-done, bf16[4,256,512]{2,1,0:T(8,128)(2,1)} %collective-permute-done.8.refs_3_), custom_call_target="tpu_custom_call" | custom-call | flops 536870912 | bytes 4194304 | tf_op jit(solution)/shard_map/pallas_call | solution.py:110
  95.4 4.9 %shard_map.327 = (bf16[1,512,512]{2,1,0:T(8,128)(2,1)}, bf16[2,512,512]{2,1,0:T(8,128)(2,1)}, bf16[5,512,512]{2,1,0:T(8,128)(2,1)}) custom-call(s32[8]{0:T(128)} %fusion.4.refs_0_, bf16[256,8192]{1,0:T(8,128)(2,1)} %refs_15_.1, bf16[256,4096]{1,0:T(8,128)(2,1)} %collective-permute-done.15.refs_2_.refs_4_.refs_6_.refs_8_.refs_10_.refs_12_.refs_14_.refs_16_, ...), custom_call_target="tpu_custom_call" | custom-call | bytes 8388608 | tf_op jit(solution)/shard_map/pallas_call | solution.py:110
  100.5 5.1 %shard_map.325.refs_1_ = f32[256,256]{1,0:T(8,128)} custom-call(s32[8]{0:T(128)} %fusion.4.refs_0_, bf16[8192,256]{1,0:T(8,128)(2,1)} %refs_1_.10, f32[256,256]{1,0:T(8,128)} %shard_map.320.refs_2_, bf16[4,256,512]{2,1,0:T(8,128)(2,1)} %copy-done.1, bf16[4,256,512]{2,1,0:T(8,128)(2,1)} %collective-permute-done.14.refs_4_), custom_call_target="tpu_custom_call" | custom-call | flops 536870912 | bytes 4194304 | tf_op jit(solution)/shard_map/pallas_call | solution.py:110
  105.7 1.6 %copy-done.7 = bf16[128,1,32,256]{3,2,1,0:T(8,128)(2,1)S(1)} copy-done((bf16[128,1,32,256]{3,2,1,0:T(8,128)(2,1)S(1)}, bf16[128,1,32,256]{3,2,1,0:T(8,128)(2,1)}, u32[]{:S(2)}) %copy-start.7) | copy-done | bytes 2097176
  108.2 3.3 %shard_map.328.refs_0_ = bf16[256,256]{1,0:T(8,128)(2,1)S(1)} custom-call(bf16[16,128,128]{2,1,0:T(8,128)(2,1)S(1)} %all-to-all-done.3.refs_0_, f32[256,256]{1,0:T(8,128)S(1)} %copy-done.10, bf16[64,256]{1,0:T(8,128)(2,1)S(1)} %copy-done.18, f32[5,128,128]{2,1,0:T(8,128)S(1)} %pad_maximum_fusion.refs_3_, bf16[4096,256]{1,0:T(8,128)(2,1)S(1)} %bitcast.11, ...), custom_call_target="tpu_custom_call" | custom-call | flops 134217728 | bytes 4194304 | tf_op jit(solution)/shard_map/pallas_call | solution.py:110
  113.4 2.5 %collective-permute-start.22 = (bf16[160,512]{1,0:T(8,128)(2,1)S(1)}, bf16[160,512]{1,0:T(8,128)(2,1)S(1)}, u32[]{:S(2)}, u32[]{:S(2)}) collective-permute-start(bf16[160,512]{1,0:T(8,128)(2,1)S(1)} %get-tuple-element.65), channel_id=1, source_target_pairs={{0,4},{1,5},{2,6},{3,7},{4,8},{5,9},{6,10},{7,11},{8,12},{9,13},{1... | collective-permute-start | bytes 491528 | tf_op jit(solution)/shard_map/ppermute | solution.py:37
  116.3 3.6 %collective-permute-done.22.refs_2_ = bf16[160,512]{1,0:T(8,128)(2,1)S(1)} collective-permute-done((bf16[160,512]{1,0:T(8,128)(2,1)S(1)}, bf16[160,512]{1,0:T(8,128)(2,1)S(1)}, u32[]{:S(2)}, u32[]{:S(2)}) %collective-permute-start.22) | collective-permute-done | bytes 163872 | tf_op jit(solution)/shard_map/ppermute | solution.py:37
  119.9 3.3 %collective-permute-done.23.refs_3_ = bf16[160,512]{1,0:T(8,128)(2,1)S(1)} collective-permute-done((bf16[160,512]{1,0:T(8,128)(2,1)S(1)}, bf16[160,512]{1,0:T(8,128)(2,1)S(1)}, u32[]{:S(2)}, u32[]{:S(2)}) %collective-permute-start.23) | collective-permute-done | bytes 163872 | tf_op jit(solution)/shard_map/ppermute | solution.py:37
  123.6 1.7 %collective-permute-start.25 = (bf16[288,512]{1,0:T(8,128)(2,1)S(1)}, bf16[288,512]{1,0:T(8,128)(2,1)S(1)}, u32[]{:S(2)}, u32[]{:S(2)}) collective-permute-start(bf16[288,512]{1,0:T(8,128)(2,1)S(1)} %get-tuple-element.71), channel_id=1, source_target_pairs={{0,12},{1,13},{2,14},{3,15},{4,0},{5,1},{6,2},{7,3},{8,4},{9,5},{1... | collective-permute-start | bytes 884744 | tf_op jit(solution)/shard_map/ppermute | solution.py:37
  126.3 1.6 %collective-permute-start.17 = (bf16[128,512]{1,0:T(8,128)(2,1)S(1)}, bf16[128,512]{1,0:T(8,128)(2,1)S(1)}, u32[]{:S(2)}, u32[]{:S(2)}) collective-permute-start(bf16[128,512]{1,0:T(8,128)(2,1)S(1)} %get-tuple-element.58), channel_id=1, source_target_pairs={{0,4},{1,5},{2,6},{3,7},{4,8},{5,9},{6,10},{7,11},{8,12},{9,13},{1... | collective-permute-start | bytes 393224 | tf_op jit(solution)/shard_map/ppermute | solution.py:37
  128.4 4.5 %collective-permute-done.24.refs_4_ = bf16[288,512]{1,0:T(8,128)(2,1)S(1)} collective-permute-done((bf16[288,512]{1,0:T(8,128)(2,1)S(1)}, bf16[288,512]{1,0:T(8,128)(2,1)S(1)}, u32[]{:S(2)}, u32[]{:S(2)}) %collective-permute-start.24) | collective-permute-done | bytes 294944 | tf_op jit(solution)/shard_map/ppermute | solution.py:37
  134.5 3.6 %collective-permute-start.26 = (bf16[288,512]{1,0:T(8,128)(2,1)S(1)}, bf16[288,512]{1,0:T(8,128)(2,1)S(1)}, u32[]{:S(2)}, u32[]{:S(2)}) collective-permute-start(bf16[288,512]{1,0:T(8,128)(2,1)S(1)} %shard_map.335.refs_1_), channel_id=1, source_target_pairs={{0,2},{1,3},{2,0},{3,1},{4,6},{5,7},{6,4},{7,5},{8,10},{9,11},{10,... | collective-permute-start | bytes 884744 | tf_op jit(solution)/shard_map/ppermute | solution.py:37
  138.5 1.7 %collective-permute-start.20 = (bf16[256,512]{1,0:T(8,128)(2,1)S(1)}, bf16[256,512]{1,0:T(8,128)(2,1)S(1)}, u32[]{:S(2)}, u32[]{:S(2)}) collective-permute-start(bf16[256,512]{1,0:T(8,128)(2,1)S(1)} %get-tuple-element.61), channel_id=1, source_target_pairs={{0,12},{1,13},{2,14},{3,15},{4,0},{5,1},{6,2},{7,3},{8,4},{9,5},{1... | collective-permute-start | bytes 786440 | tf_op jit(solution)/shard_map/ppermute | solution.py:37
  140.3 2.6 %shard_map.337 = (f32[4,512]{1,0:T(4,128)}, f32[4,256]{1,0:T(4,128)}, f32[4,256]{1,0:T(4,128)}, f32[4,512]{1,0:T(4,128)}, f32[4,512]{1,0:T(4,128)}, /*index=5*/f...) custom-call(f32[16,8,128]{2,1,0:T(8,128)} %copy-done.20, ...), custom_call_target="tpu_custom_call" | custom-call | bytes 1048576 | tf_op jit(solution)/shard_map/pallas_call | solution.py:110
  142.9 1.8 %collective-permute-done.19.refs_1_ = bf16[256,512]{1,0:T(8,128)(2,1)S(1)} collective-permute-done((bf16[256,512]{1,0:T(8,128)(2,1)S(1)}, bf16[256,512]{1,0:T(8,128)(2,1)S(1)}, u32[]{:S(2)}, u32[]{:S(2)}) %collective-permute-start.19) | collective-permute-done | bytes 262176 | tf_op jit(solution)/shard_map/ppermute | solution.py:37
  146.2 4.5 %collective-permute-done.26.refs_2_ = bf16[288,512]{1,0:T(8,128)(2,1)S(1)} collective-permute-done((bf16[288,512]{1,0:T(8,128)(2,1)S(1)}, bf16[288,512]{1,0:T(8,128)(2,1)S(1)}, u32[]{:S(2)}, u32[]{:S(2)}) %collective-permute-start.26) | collective-permute-done | bytes 294944 | tf_op jit(solution)/shard_map/ppermute | solution.py:37
  (111 shorter events, 31.9 us)
Async XLA Ops:
  2.5 25.7 %all-to-all-start = ((f32[16,48,128]{2,1,0:T(8,128)}), f32[16,48,128]{2,1,0:T(8,128)S(1)}, u32[]{:S(2)}, u32[]{:S(2)}) async-start(f32[16,48,128]{2,1,0:T(8,128)} %shard_map.309), calls=%async_computation | async-start | bytes 786432 | tf_op jit(solution)/shard_map/all_to_all | solution.py:456
  13.6 81.8 %collective-permute-start.15 = (bf16[256,4096]{1,0:T(8,128)(2,1)}, bf16[256,4096]{1,0:T(8,128)(2,1)}, u32[]{:S(2)}, u32[]{:S(2)}) collective-permute-start(bf16[256,4096]{1,0:T(8,128)(2,1)} %shard_map.326), channel_id=1, source_target_pairs={{0,1},{1,0},{2,3},{3,2},{4,5},{5,4},{6,7},{7,6},{8,9},{9,8},{10,11... | collective-permute-start | bytes 6291464 | tf_op jit(solution)/shard_map/ppermute | solution.py:37
  13.7 14.4 %collective-permute-start = (bf16[256,512]{1,0:T(8,128)(2,1)S(1)}, bf16[256,512]{1,0:T(8,128)(2,1)S(1)}, u32[]{:S(2)}, u32[]{:S(2)}) collective-permute-start(bf16[256,512]{1,0:T(8,128)(2,1)S(1)} %bitcast.6), channel_id=1, source_target_pairs={{0,4},{1,5},{2,6},{3,7},{4,8},{5,9},{6,10},{7,11},{8,12},{9,13},{1... | collective-permute-start | bytes 786440 | tf_op jit(solution)/shard_map/ppermute | solution.py:37
  14.3 13.9 %collective-permute-start.1 = (bf16[256,512]{1,0:T(8,128)(2,1)S(1)}, bf16[256,512]{1,0:T(8,128)(2,1)S(1)}, u32[]{:S(2)}, u32[]{:S(2)}) collective-permute-start(bf16[256,512]{1,0:T(8,128)(2,1)S(1)} %bitcast.7), channel_id=1, source_target_pairs={{0,12},{1,13},{2,14},{3,15},{4,0},{5,1},{6,2},{7,3},{8,4},{9,5},{1... | collective-permute-start | bytes 786440 | tf_op jit(solution)/shard_map/ppermute | solution.py:37
  17.4 4.3 %collective-permute-start.2 = (bf16[1,144,128]{2,1,0:T(8,128)(2,1)}, bf16[1,144,128]{2,1,0:T(8,128)(2,1)S(1)}, u32[]{:S(2)}, u32[]{:S(2)}) collective-permute-start(bf16[1,144,128]{2,1,0:T(8,128)(2,1)} %shard_map.310.refs_0_), channel_id=1, source_target_pairs={{0,16},{16,0},{32,48},{48,32},{64,80},{80,64},{96,112},{112,96},{1... | collective-permute-start | bytes 110600 | tf_op jit(solution)/shard_map/ppermute | solution.py:49
  22.5 5.4 %collective-permute-start.3 = (bf16[2,144,128]{2,1,0:T(8,128)(2,1)S(1)}, bf16[2,144,128]{2,1,0:T(8,128)(2,1)S(1)}, u32[]{:S(2)}, u32[]{:S(2)}) collective-permute-start(bf16[2,144,128]{2,1,0:T(8,128)(2,1)S(1)} %shard_map.311.refs_0_), channel_id=1, source_target_pairs={{0,32},{16,48},{32,0},{48,16},{64,96},{80,112},{96,64},{112,80},{1... | collective-permute-start | bytes 221192 | tf_op jit(solution)/shard_map/ppermute | solution.py:49
  29.0 32.8 %copy-start.16 = (f32[4,1536]{1,0:T(4,128)}, f32[4,1536]{1,0:T(4,128)S(1)}, u32[]{:S(2)}) copy-start(f32[4,1536]{1,0:T(4,128)S(1)} %get-tuple-element.51.refs_1_.refs_13_) | copy-start | bytes 73732
  29.1 17.2 %collective-permute-start.9 = (bf16[256,512]{1,0:T(8,128)(2,1)S(1)}, bf16[256,512]{1,0:T(8,128)(2,1)S(1)}, u32[]{:S(2)}, u32[]{:S(2)}) collective-permute-start(bf16[256,512]{1,0:T(8,128)(2,1)S(1)} %shard_map.321), channel_id=1, source_target_pairs={{0,2},{1,3},{2,0},{3,1},{4,6},{5,7},{6,4},{7,5},{8,10},{9,11},{10,... | collective-permute-start | bytes 786440 | tf_op jit(solution)/shard_map/ppermute | solution.py:37
  33.6 28.3 %all-to-all-start.1 = ((bf16[16,64,128]{2,1,0:T(8,128)(2,1)}), bf16[16,64,128]{2,1,0:T(8,128)(2,1)S(1)}, u32[]{:S(2)}, u32[]{:S(2)}) async-start(bf16[16,64,128]{2,1,0:T(8,128)(2,1)} %get-tuple-element.49), calls=%async_computation.1 | async-start | bytes 524288 | tf_op jit(solution)/shard_map/all_to_all | solution.py:473
  46.3 9.1 %collective-permute-start.11 = (bf16[256,512]{1,0:T(8,128)(2,1)S(1)}, bf16[256,512]{1,0:T(8,128)(2,1)S(1)}, u32[]{:S(2)}, u32[]{:S(2)}) collective-permute-start(bf16[256,512]{1,0:T(8,128)(2,1)S(1)} %collective-permute-done.9.refs_0_), channel_id=1, source_target_pairs={{0,4},{1,5},{2,6},{3,7},{4,8},{5,9},{6,10},{7,11},{8,12},{9,13},{1... | collective-permute-start | bytes 786440 | tf_op jit(solution)/shard_map/ppermute | solution.py:37
  48.5 9.8 %collective-permute-start.10 = (bf16[256,512]{1,0:T(8,128)(2,1)S(1)}, bf16[256,512]{1,0:T(8,128)(2,1)S(1)}, u32[]{:S(2)}, u32[]{:S(2)}) collective-permute-start(bf16[256,512]{1,0:T(8,128)(2,1)S(1)} %collective-permute-done.9.refs_0_), channel_id=1, source_target_pairs={{0,12},{1,13},{2,14},{3,15},{4,0},{5,1},{6,2},{7,3},{8,4},{9,5},{1... | collective-permute-start | bytes 786440 | tf_op jit(solution)/shard_map/ppermute | solution.py:37
  48.5 5.1 %collective-permute-start.4 = (bf16[4,144,128]{2,1,0:T(8,128)(2,1)S(1)}, bf16[4,144,128]{2,1,0:T(8,128)(2,1)S(1)}, u32[]{:S(2)}, u32[]{:S(2)}) collective-permute-start(bf16[4,144,128]{2,1,0:T(8,128)(2,1)S(1)} %shard_map.312.refs_3_.refs_0_), channel_id=1, source_target_pairs={{0,64},{16,80},{32,96},{48,112},{64,0},{80,16},{96,32},{112,48},{1... | collective-permute-start | bytes 442376 | tf_op jit(solution)/shard_map/ppermute | solution.py:49
  48.7 12.5 %collective-permute-start.6 = (bf16[128,512]{1,0:T(8,128)(2,1)S(1)}, bf16[128,512]{1,0:T(8,128)(2,1)S(1)}, u32[]{:S(2)}, u32[]{:S(2)}) collective-permute-start(bf16[128,512]{1,0:T(8,128)(2,1)S(1)} %shard_map.317), channel_id=1, source_target_pairs={{0,4},{1,5},{2,6},{3,7},{4,8},{5,9},{6,10},{7,11},{8,12},{9,13},{1... | collective-permute-start | bytes 393224 | tf_op jit(solution)/shard_map/ppermute | solution.py:37
  53.6 7.7 %collective-permute-start.7 = (bf16[128,512]{1,0:T(8,128)(2,1)S(1)}, bf16[128,512]{1,0:T(8,128)(2,1)S(1)}, u32[]{:S(2)}, u32[]{:S(2)}) collective-permute-start(bf16[128,512]{1,0:T(8,128)(2,1)S(1)} %shard_map.318), channel_id=1, source_target_pairs={{0,12},{1,13},{2,14},{3,15},{4,0},{5,1},{6,2},{7,3},{8,4},{9,5},{1... | collective-permute-start | bytes 393224 | tf_op jit(solution)/shard_map/ppermute | solution.py:37
  55.4 19.6 %collective-permute-start.5 = (bf16[8,144,128]{2,1,0:T(8,128)(2,1)S(1)}, bf16[8,144,128]{2,1,0:T(8,128)(2,1)}, u32[]{:S(2)}, u32[]{:S(2)}) collective-permute-start(bf16[8,144,128]{2,1,0:T(8,128)(2,1)S(1)} %shard_map.315.refs_4_), channel_id=1, source_target_pairs={{0,128},{16,144},{32,160},{48,176},{64,192},{80,208},{96,224},{112... | collective-permute-start | bytes 884744 | tf_op jit(solution)/shard_map/ppermute | solution.py:49
  58.3 12.6 %collective-permute-start.12 = (bf16[128,512]{1,0:T(8,128)(2,1)}, bf16[128,512]{1,0:T(8,128)(2,1)S(1)}, u32[]{:S(2)}, u32[]{:S(2)}) collective-permute-start(bf16[128,512]{1,0:T(8,128)(2,1)} %shard_map.322), channel_id=1, source_target_pairs={{0,4},{1,5},{2,6},{3,7},{4,8},{5,9},{6,10},{7,11},{8,12},{9,13},{1... | collective-permute-start | bytes 393224 | tf_op jit(solution)/shard_map/ppermute | solution.py:37
  61.3 10.3 %collective-permute-start.13 = (bf16[128,512]{1,0:T(8,128)(2,1)}, bf16[128,512]{1,0:T(8,128)(2,1)}, u32[]{:S(2)}, u32[]{:S(2)}) collective-permute-start(bf16[128,512]{1,0:T(8,128)(2,1)} %shard_map.323), channel_id=1, source_target_pairs={{0,12},{1,13},{2,14},{3,15},{4,0},{5,1},{6,2},{7,3},{8,4},{9,5},{1... | collective-permute-start | bytes 393224 | tf_op jit(solution)/shard_map/ppermute | solution.py:37
  61.9 28.7 %collective-permute-start.8 = (bf16[4,256,512]{2,1,0:T(8,128)(2,1)S(1)}, bf16[4,256,512]{2,1,0:T(8,128)(2,1)}, u32[]{:S(2)}, u32[]{:S(2)}) collective-permute-start(bf16[4,256,512]{2,1,0:T(8,128)(2,1)S(1)} %shard_map.319.refs_2_), channel_id=1, source_target_pairs={{0,1},{1,0},{2,3},{3,2},{4,5},{5,4},{6,7},{7,6},{8,9},{9,8},{10,11... | collective-permute-start | bytes 3145736 | tf_op jit(solution)/shard_map/ppermute | solution.py:37
  62.9 16.1 %all-to-all-start.2 = ((f32[16,8,128]{2,1,0:T(8,128)}), f32[16,8,128]{2,1,0:T(8,128)S(1)}, u32[]{:S(2)}, u32[]{:S(2)}) async-start(f32[16,8,128]{2,1,0:T(8,128)} %shard_map.314), calls=%async_computation.2 | async-start | bytes 131072 | tf_op jit(solution)/shard_map/all_to_all | solution.py:484
  74.6 25.8 %collective-permute-start.14 = (bf16[4,256,512]{2,1,0:T(8,128)(2,1)S(1)}, bf16[4,256,512]{2,1,0:T(8,128)(2,1)}, u32[]{:S(2)}, u32[]{:S(2)}) collective-permute-start(bf16[4,256,512]{2,1,0:T(8,128)(2,1)S(1)} %shard_map.324.refs_3_), channel_id=1, source_target_pairs={{0,1},{1,0},{2,3},{3,2},{4,5},{5,4},{6,7},{7,6},{8,9},{9,8},{10,11... | collective-permute-start | bytes 3145736 | tf_op jit(solution)/shard_map/ppermute | solution.py:37
  82.4 23.3 %all-to-all-start.3 = ((bf16[16,128,128]{2,1,0:T(8,128)(2,1)}), bf16[16,128,128]{2,1,0:T(8,128)(2,1)S(1)}, u32[]{:S(2)}, u32[]{:S(2)}) async-start(bf16[16,128,128]{2,1,0:T(8,128)(2,1)} %get-tuple-element.50), calls=%async_computation.3 | async-start | bytes 1048576 | tf_op jit(solution)/shard_map/all_to_all | solution.py:525
  111.5 1.5 collective-permute-start.16
  111.7 1.3 collective-permute-start.21
  113.4 6.5 %collective-permute-start.22 = (bf16[160,512]{1,0:T(8,128)(2,1)S(1)}, bf16[160,512]{1,0:T(8,128)(2,1)S(1)}, u32[]{:S(2)}, u32[]{:S(2)}) collective-permute-start(bf16[160,512]{1,0:T(8,128)(2,1)S(1)} %get-tuple-element.65), channel_id=1, source_target_pairs={{0,4},{1,5},{2,6},{3,7},{4,8},{5,9},{6,10},{7,11},{8,12},{9,13},{1... | collective-permute-start | bytes 491528 | tf_op jit(solution)/shard_map/ppermute | solution.py:37
  115.9 7.4 %collective-permute-start.23 = (bf16[160,512]{1,0:T(8,128)(2,1)S(1)}, bf16[160,512]{1,0:T(8,128)(2,1)S(1)}, u32[]{:S(2)}, u32[]{:S(2)}) collective-permute-start(bf16[160,512]{1,0:T(8,128)(2,1)S(1)} %get-tuple-element.66), channel_id=1, source_target_pairs={{0,12},{1,13},{2,14},{3,15},{4,0},{5,1},{6,2},{7,3},{8,4},{9,5},{1... | collective-permute-start | bytes 491528 | tf_op jit(solution)/shard_map/ppermute | solution.py:37
  123.3 9.6 %collective-permute-start.24 = (bf16[288,512]{1,0:T(8,128)(2,1)S(1)}, bf16[288,512]{1,0:T(8,128)(2,1)S(1)}, u32[]{:S(2)}, u32[]{:S(2)}) collective-permute-start(bf16[288,512]{1,0:T(8,128)(2,1)S(1)} %get-tuple-element.70), channel_id=1, source_target_pairs={{0,4},{1,5},{2,6},{3,7},{4,8},{5,9},{6,10},{7,11},{8,12},{9,13},{1... | collective-permute-start | bytes 884744 | tf_op jit(solution)/shard_map/ppermute | solution.py:37
  123.6 10.8 %collective-permute-start.25 = (bf16[288,512]{1,0:T(8,128)(2,1)S(1)}, bf16[288,512]{1,0:T(8,128)(2,1)S(1)}, u32[]{:S(2)}, u32[]{:S(2)}) collective-permute-start(bf16[288,512]{1,0:T(8,128)(2,1)S(1)} %get-tuple-element.71), channel_id=1, source_target_pairs={{0,12},{1,13},{2,14},{3,15},{4,0},{5,1},{6,2},{7,3},{8,4},{9,5},{1... | collective-permute-start | bytes 884744 | tf_op jit(solution)/shard_map/ppermute | solution.py:37
  126.3 11.8 %collective-permute-start.17 = (bf16[128,512]{1,0:T(8,128)(2,1)S(1)}, bf16[128,512]{1,0:T(8,128)(2,1)S(1)}, u32[]{:S(2)}, u32[]{:S(2)}) collective-permute-start(bf16[128,512]{1,0:T(8,128)(2,1)S(1)} %get-tuple-element.58), channel_id=1, source_target_pairs={{0,4},{1,5},{2,6},{3,7},{4,8},{5,9},{6,10},{7,11},{8,12},{9,13},{1... | collective-permute-start | bytes 393224 | tf_op jit(solution)/shard_map/ppermute | solution.py:37
  127.8 10.3 %collective-permute-start.18 = (bf16[128,512]{1,0:T(8,128)(2,1)S(1)}, bf16[128,512]{1,0:T(8,128)(2,1)S(1)}, u32[]{:S(2)}, u32[]{:S(2)}) collective-permute-start(bf16[128,512]{1,0:T(8,128)(2,1)S(1)} %get-tuple-element.59), channel_id=1, source_target_pairs={{0,12},{1,13},{2,14},{3,15},{4,0},{5,1},{6,2},{7,3},{8,4},{9,5},{1... | collective-permute-start | bytes 393224 | tf_op jit(solution)/shard_map/ppermute | solution.py:37
  134.5 16.2 %collective-permute-start.26 = (bf16[288,512]{1,0:T(8,128)(2,1)S(1)}, bf16[288,512]{1,0:T(8,128)(2,1)S(1)}, u32[]{:S(2)}, u32[]{:S(2)}) collective-permute-start(bf16[288,512]{1,0:T(8,128)(2,1)S(1)} %shard_map.335.refs_1_), channel_id=1, source_target_pairs={{0,2},{1,3},{2,0},{3,1},{4,6},{5,7},{6,4},{7,5},{8,10},{9,11},{10,... | collective-permute-start | bytes 884744 | tf_op jit(solution)/shard_map/ppermute | solution.py:37
  138.2 6.4 %collective-permute-start.19 = (bf16[256,512]{1,0:T(8,128)(2,1)S(1)}, bf16[256,512]{1,0:T(8,128)(2,1)S(1)}, u32[]{:S(2)}, u32[]{:S(2)}) collective-permute-start(bf16[256,512]{1,0:T(8,128)(2,1)S(1)} %get-tuple-element.60), channel_id=1, source_target_pairs={{0,4},{1,5},{2,6},{3,7},{4,8},{5,9},{6,10},{7,11},{8,12},{9,13},{1... | collective-permute-start | bytes 786440 | tf_op jit(solution)/shard_map/ppermute | solution.py:37
  138.5 7.6 %collective-permute-start.20 = (bf16[256,512]{1,0:T(8,128)(2,1)S(1)}, bf16[256,512]{1,0:T(8,128)(2,1)S(1)}, u32[]{:S(2)}, u32[]{:S(2)}) collective-permute-start(bf16[256,512]{1,0:T(8,128)(2,1)S(1)} %get-tuple-element.61), channel_id=1, source_target_pairs={{0,12},{1,13},{2,14},{3,15},{4,0},{5,1},{6,2},{7,3},{8,4},{9,5},{1... | collective-permute-start | bytes 786440 | tf_op jit(solution)/shard_map/ppermute | solution.py:37
  (21 other events, 243.1 us)

commit v3 on v2

--- a/solution.py
+++ b/solution.py
@@ -51,6 +51,10 @@
 
 def to_right(value):
     return shift(value, lambda i: (i + 4) % N)
+
+
+def to_across(value):
+    return shift(value, lambda i: (i + 8) % N)
 
 
 def to_left(value):
@@ -156,7 +160,7 @@
     )(*arrays)
 
 
-ALL, ONE, TWO = pl.ds(0, 256), pl.ds(0, 128), pl.ds(128, 128)
+ALL = pl.ds(0, 256)
 
 
 def both_of(held, bit):
@@ -166,17 +170,9 @@
     )
 
 
-def beyond(left, right, token=None):
-    return (
-        to_right(join((128, 512), [(0, ONE, ONE)], left, token=token)),
-        to_left(join((128, 512), [(0, TWO, ONE)], right, token=token)),
-    )
-
-
-def along_x(own, right, far_a, far_b, left):
-    places = [(0, ALL, (0, ALL)), (1, ALL, (1, ALL)), (4, ALL, (3, ALL))]
-    places += [(2, ONE, (2, ONE)), (3, ONE, (2, TWO))]
-    return join((4, 256, 512), places, own, right, far_a, far_b, left)
+def along_x(*pieces):
+    places = [(dx, ALL, (dx, ALL)) for dx in range(4)]
+    return join((4, 256, 512), places, *pieces)
 
 
 def stacked(pieces):
@@ -265,16 +261,15 @@
         at += width
 
 
-def base_queries(dz, order, weight, *refs):
-    before = refs[0] if dz == 1 else None
-    mine, other, out = refs[dz:]
+def base_queries(order, weight, *refs):
+    sets, out = refs[:4], refs[4]
     total = jnp.zeros((256, 256), f32)
-    weight = weight.there()
-    for dx in range(4):
-        for flip, pieces in enumerate((mine, other)):
-            place = order[2 * dx + dz] ^ flip
-            total += dot(pieces[dx], weight[pl.ds(pl.multiple_of(place * 512, 512), 512), :])
-    out[...] = total if before is None else total + before[...]
+    for i, pieces in enumerate(sets):
+        for dx in range(4):
+            place = order[2 * dx + i // 2] ^ (i % 2)
+            rows = pl.ds(pl.multiple_of(place * 512, 512), 512)
+            total += dot(pieces[dx], weight[rows, :])
+    out[...] = total
 
 
 ROWS = 16
@@ -458,6 +453,7 @@
     hidden = hidden.reshape(256, 512)
     left = to_right(hidden)
     right = to_left(hidden)
+    across = to_across(hidden)
     held = call(pack_state, [((1, 144, HEAD), bf16)], fetch=state)
     held = both_of(held, 1)
     held = both_of(held, 2)
@@ -466,12 +462,11 @@
         sum_gradients,
         [((4, 1536), f32), ((N, 64, HEAD), bf16)],
         parts,
-        tokens=(left, right, held),
+        tokens=(left, right, across, held),
         moved=CHAIN,
         limit=SMALL,
     )
     all_parts = lax.all_to_all(message, "rep", 0, 0)
-    far_a, far_b = beyond(left, right)
     held = both_of(held, 4)
 
     squares_sent = call(
@@ -484,7 +479,7 @@
     squares = lax.all_to_all(squares_sent, "tp", 0, 0)
     zed = to_z(join((256, 512), [(0, ALL, ALL)], hidden, token=summed))
     held_far = to_replica(held, 8)
-    set_h = along_x(hidden, right, far_a, far_b, left)
+    set_h = along_x(hidden, right, across, left)
     set_h_other = to_core(set_h)
 
     def given(k):
@@ -531,26 +526,17 @@
         fetch=state,
         take=(summed,),
     )
-    left_z = to_right(zed)
-    right_z = to_left(zed)
-    set_z = along_x(zed, right_z, *beyond(left_z, right_z), left_z)
+    set_z = along_x(zed, to_left(zed), to_across(zed), to_right(zed))
     set_z_other = to_core(set_z)
-    cost = dict(scalars=1, flops=256 * 8192 * 256, moved=4 << 20)
     base = call(
-        functools.partial(base_queries, 0),
+        base_queries,
         [((256, 256), f32)],
         order,
+        scalars=1,
         fetch=(query_base_weight,),
-        take=(set_h, set_h_other),
-        **cost,
-    )
-    base = call(
-        functools.partial(base_queries, 1),
-        [((256, 256), f32)],
-        order,
-        fetch=(query_base_weight,),
-        take=(base, set_z, set_z_other),
-        **cost,
+        take=(set_h, set_h_other, set_z, set_z_other),
+        flops=2 * 256 * 8192 * 256,
+        moved=8 << 20,
     )
 
     frequency = jnp.power(rope_base, -2.0 * jnp.arange(64, dtype=f32) / HEAD)

time: 155 us -> 149 us (0.961); the launches traced: 152 us -> 148 us
  Pallas kernels: 39.1 us -> 32.5 us
  waiting for transfers between devices: 39.6 us -> 43.9 us
  local copies, waits for them, and re-layouts: 7.56 us -> 5.77 us
    all_to_all x1, waiting for transfers between devices: 3.89 us -> 8.03 us  [on_device(): squares = lax.all_to_all(squares_sent, 'tp', 0, 0)]
    pallas_call x10 -> x6, Pallas kernels: 4.18 us -> 0.9 us  [join(): pl.pallas_call(kernel, in_specs=[ANY] * len(arrays), out_specs=VMEM, out_...]
    pallas_call x19 -> x18, Pallas kernels: 34.9 us -> 31.6 us  [call(): pl.pallas_call(body, in_specs=[SMEM] * scalars + [VMEM] * (first - scalar...]
    unnamed x44 -> x40, local copies, waits for them, and re-layouts: 6.52 us -> 4.09 us
    ppermute x23 -> x21, waiting for transfers between devices: 26.8 us -> 28.4 us  [shift(): return lax.ppermute(value, 'tp', [(i, move(i)) for i in range(N)])]
    ppermute x23 -> x21, starting transfers between devices: 28.5 us -> 27.6 us  [shift(): return lax.ppermute(value, 'tp', [(i, move(i)) for i in range(N)])]
  transfers between devices with their start and end apart: 31 -> 29, of which waited for: 15 -> 14; matrix products, arithmetic and copies ran while one was open for 1% -> 2% of each run, Pallas kernels for 21% -> 17%
where the time goes in v3:
time: 149 us; the launch traced here: 148 us
  starting transfers between devices  63.2 us (42%)
  waiting for transfers between devices  43.9 us (29%)
  Pallas kernels  32.5 us (22%)
  local copies, waits for them, and re-layouts  5.77 us (4%)
    pallas_call x18, Pallas kernels, call(): pl.pallas_call(body, in_specs=[SMEM] * scalars + [VMEM] * (first - scalar...  31.6 us
    ppermute x21, waiting for transfers between devices, shift(): return lax.ppermute(value, 'tp', [(i, move(i)) for i in range(N)])  28.4 us
    ppermute x21, starting transfers between devices, shift(): return lax.ppermute(value, 'tp', [(i, move(i)) for i in range(N)])  27.6 us
    all_to_all x1, starting transfers between devices, on_device(): squares = lax.all_to_all(squares_sent, 'tp', 0, 0)  8.8 us
    all_to_all x1, starting transfers between devices, on_device(): all_parts = lax.all_to_all(message, 'rep', 0, 0)  8.2 us
    all_to_all x1, starting transfers between devices, on_device(): parts = lax.all_to_all(gradient, 'rep', 0, 0)  8.1 us
    all_to_all x1, waiting for transfers between devices, on_device(): squares = lax.all_to_all(squares_sent, 'tp', 0, 0)  8.03 us
    ppermute x4, waiting for transfers between devices, to_replica(): return lax.ppermute(value, 'rep', [(i, i ^ bit) for i in range(N)])  7.5 us
  transfers between devices with their start and end apart: 29, of which 14 were waited for; matrix products, arithmetic and copies ran while one was open for 2% of the time, Pallas kernels for 17%

profile of v3, /device:TPU:78, one launch (start us, length us, event | category | flops | bytes accessed | tf_op | source)
XLA Modules:
  0.0 147.9 jit_solution(5933444820990938607)
XLA Ops:
  0.6 1.9 %shard_map.309 = f32[16,48,128]{2,1,0:T(8,128)} custom-call(f32[1,64,512]{2,1,0:T(8,128)} %refs_0_.2, f32[1,64,256]{2,1,0:T(8,128)} %refs_1_.6, f32[1,64,256]{2,1,0:T(8,128)} %refs_2_.4, f32[1,64,512]{2,1,0:T(8,128)} %refs_3_.5), custom_call_target="tpu_custom_call" | custom-call | bytes 1048576 | tf_op jit(solution)/shard_map/pallas_call | solution.py:114
  2.5 8.1 %all-to-all-start = ((f32[16,48,128]{2,1,0:T(8,128)}), f32[16,48,128]{2,1,0:T(8,128)S(1)}, u32[]{:S(2)}, u32[]{:S(2)}) async-start(f32[16,48,128]{2,1,0:T(8,128)} %shard_map.309), calls=%async_computation | async-start | bytes 786432 | tf_op jit(solution)/shard_map/all_to_all | solution.py:451
  10.6 3.0 %shard_map.321 = bf16[256,4096]{1,0:T(8,128)(2,1)} custom-call(s32[1]{0:T(128)} %bitcast.3.refs_0_, bf16[256,8192]{1,0:T(8,128)(2,1)} %refs_15_.1, bf16[256,8192]{1,0:T(8,128)(2,1)} %refs_15_.1, bf16[256,8192]{1,0:T(8,128)(2,1)} %refs_15_.1, bf16[256,8192]{1,0:T(8,128)(2,1)} %refs_15_.1, bf16[256,8192]{1,0:T(8,128)(2,1)} %refs_15_.1, ...), custom_call_target="tpu_custom_call" | custom-call | bytes 4194304 | tf_op jit(solution)/shard_map/pallas_call | solution.py:114
  14.3 1.5 %collective-permute-start.1 = (bf16[256,512]{1,0:T(8,128)(2,1)S(1)}, bf16[256,512]{1,0:T(8,128)(2,1)S(1)}, u32[]{:S(2)}, u32[]{:S(2)}) collective-permute-start(bf16[256,512]{1,0:T(8,128)(2,1)S(1)} %bitcast.7), channel_id=1, source_target_pairs={{0,12},{1,13},{2,14},{3,15},{4,0},{5,1},{6,2},{7,3},{8,4},{9,5},{1... | collective-permute-start | bytes 786440 | tf_op jit(solution)/shard_map/ppermute | solution.py:37
  17.3 1.6 %shard_map.310.refs_0_ = bf16[1,144,128]{2,1,0:T(8,128)(2,1)} custom-call(f32[4,512]{1,0:T(4,128)} %refs_1_.11, f32[4,256]{1,0:T(4,128)} %refs_2_.7, f32[4,256]{1,0:T(4,128)} %refs_3_.9, f32[4,512]{1,0:T(4,128)} %refs_4_.5, f32[4,512]{1,0:T(4,128)} %refs_5_.7, f32[4,256]{1,0:T(4,128)} %refs_6_.5, f32[4,256]{1,0:T(4,128)} %refs_7_.7, f32[4,512]{1,0:T(4,128)} %refs_8_.5, ...), custom_call_target="tpu_custom_call" | custom-call | bytes 1048576 | tf_op jit(solution)/shard_map/pallas_call | solution.py:114
  18.8 1.5 %collective-permute-start.3 = (bf16[1,144,128]{2,1,0:T(8,128)(2,1)}, bf16[1,144,128]{2,1,0:T(8,128)(2,1)S(1)}, u32[]{:S(2)}, u32[]{:S(2)}) collective-permute-start(bf16[1,144,128]{2,1,0:T(8,128)(2,1)} %shard_map.310.refs_0_), channel_id=1, source_target_pairs={{0,16},{16,0},{32,48},{48,32},{64,80},{80,64},{96,112},{112,96},{1... | collective-permute-start | bytes 110600 | tf_op jit(solution)/shard_map/ppermute | solution.py:49
  20.4 2.7 %collective-permute-done.3.refs_1_ = bf16[1,144,128]{2,1,0:T(8,128)(2,1)S(1)} collective-permute-done((bf16[1,144,128]{2,1,0:T(8,128)(2,1)}, bf16[1,144,128]{2,1,0:T(8,128)(2,1)S(1)}, u32[]{:S(2)}, u32[]{:S(2)}) %collective-permute-start.3) | collective-permute-done | bytes 36896 | tf_op jit(solution)/shard_map/ppermute | solution.py:49
  24.6 4.8 %collective-permute-done.4.refs_1_ = bf16[2,144,128]{2,1,0:T(8,128)(2,1)S(1)} collective-permute-done((bf16[2,144,128]{2,1,0:T(8,128)(2,1)S(1)}, bf16[2,144,128]{2,1,0:T(8,128)(2,1)S(1)}, u32[]{:S(2)}, u32[]{:S(2)}) %collective-permute-start.4) | collective-permute-done | bytes 73760 | tf_op jit(solution)/shard_map/ppermute | solution.py:49
  30.5 4.6 %collective-permute-start.8 = (bf16[256,512]{1,0:T(8,128)(2,1)S(1)}, bf16[256,512]{1,0:T(8,128)(2,1)S(1)}, u32[]{:S(2)}, u32[]{:S(2)}) collective-permute-start(bf16[256,512]{1,0:T(8,128)(2,1)S(1)} %shard_map.318), channel_id=1, source_target_pairs={{0,2},{1,3},{2,0},{3,1},{4,6},{5,7},{6,4},{7,5},{8,10},{9,11},{10,... | collective-permute-start | bytes 786440 | tf_op jit(solution)/shard_map/ppermute | solution.py:37
  35.1 8.2 %all-to-all-start.1 = ((bf16[16,64,128]{2,1,0:T(8,128)(2,1)}), bf16[16,64,128]{2,1,0:T(8,128)(2,1)S(1)}, u32[]{:S(2)}, u32[]{:S(2)}) async-start(bf16[16,64,128]{2,1,0:T(8,128)(2,1)} %get-tuple-element.49), calls=%async_computation.1 | async-start | bytes 524288 | tf_op jit(solution)/shard_map/all_to_all | solution.py:469
  43.9 4.8 %collective-permute-done.8.refs_0_ = bf16[256,512]{1,0:T(8,128)(2,1)S(1)} collective-permute-done((bf16[256,512]{1,0:T(8,128)(2,1)S(1)}, bf16[256,512]{1,0:T(8,128)(2,1)S(1)}, u32[]{:S(2)}, u32[]{:S(2)}) %collective-permute-start.8) | collective-permute-done | bytes 262176 | tf_op jit(solution)/shard_map/ppermute | solution.py:37
  48.8 3.1 %collective-permute-start.10 = (bf16[256,512]{1,0:T(8,128)(2,1)S(1)}, bf16[256,512]{1,0:T(8,128)(2,1)S(1)}, u32[]{:S(2)}, u32[]{:S(2)}) collective-permute-start(bf16[256,512]{1,0:T(8,128)(2,1)S(1)} %collective-permute-done.8.refs_0_), channel_id=1, source_target_pairs={{0,8},{1,9},{2,10},{3,11},{4,12},{5,13},{6,14},{7,15},{8,0},{9,1},... | collective-permute-start | bytes 786440 | tf_op jit(solution)/shard_map/ppermute | solution.py:37
  53.7 2.2 %collective-permute-start.6 = (bf16[8,144,128]{2,1,0:T(8,128)(2,1)S(1)}, bf16[8,144,128]{2,1,0:T(8,128)(2,1)S(1)}, u32[]{:S(2)}, u32[]{:S(2)}) collective-permute-start(bf16[8,144,128]{2,1,0:T(8,128)(2,1)S(1)} %shard_map.315.refs_4_), channel_id=1, source_target_pairs={{0,128},{16,144},{32,160},{48,176},{64,192},{80,208},{96,224},{112... | collective-permute-start | bytes 884744 | tf_op jit(solution)/shard_map/ppermute | solution.py:49
  56.0 2.9 %collective-permute-done.9.refs_1_ = bf16[256,512]{1,0:T(8,128)(2,1)S(1)} collective-permute-done((bf16[256,512]{1,0:T(8,128)(2,1)S(1)}, bf16[256,512]{1,0:T(8,128)(2,1)S(1)}, u32[]{:S(2)}, u32[]{:S(2)}) %collective-permute-start.9) | collective-permute-done | bytes 262176 | tf_op jit(solution)/shard_map/ppermute | solution.py:37
  59.0 4.7 %collective-permute-done.10.refs_2_ = bf16[256,512]{1,0:T(8,128)(2,1)S(1)} collective-permute-done((bf16[256,512]{1,0:T(8,128)(2,1)S(1)}, bf16[256,512]{1,0:T(8,128)(2,1)S(1)}, u32[]{:S(2)}, u32[]{:S(2)}) %collective-permute-start.10) | collective-permute-done | bytes 262176 | tf_op jit(solution)/shard_map/ppermute | solution.py:37
  66.1 8.8 %all-to-all-start.2 = ((f32[16,8,128]{2,1,0:T(8,128)}), f32[16,8,128]{2,1,0:T(8,128)S(1)}, u32[]{:S(2)}, u32[]{:S(2)}) async-start(f32[16,8,128]{2,1,0:T(8,128)} %shard_map.314), calls=%async_computation.2 | async-start | bytes 131072 | tf_op jit(solution)/shard_map/all_to_all | solution.py:479
  75.0 8.0 %all-to-all-done.2.refs_2_.refs_0_ = f32[16,8,128]{2,1,0:T(8,128)S(1)} async-done(((f32[16,8,128]{2,1,0:T(8,128)}), f32[16,8,128]{2,1,0:T(8,128)S(1)}, u32[]{:S(2)}, u32[]{:S(2)}) %all-to-all-start.2) | async-done | bytes 65568 | tf_op jit(solution)/shard_map/all_to_all | solution.py:479
  83.6 2.9 %shard_map.316 = (bf16[16,128,128]{2,1,0:T(8,128)(2,1)}, bf16[64,256]{1,0:T(8,128)(2,1)}, bf16[64,256]{1,0:T(8,128)(2,1)}, bf16[64,512]{1,0:T(8,128)(2,1)}) custom-call(s32[1]{0:T(128)} %bitcast.refs_0_, bf16[256,512]{1,0:T(8,128)(2,1)} %bitcast.5, f32[16,8,128]{2,1,0:T(8,128)} %copy-done.17, bf16[16,64,128]{2,1,0:T(8,128)(2,1)} %copy-done.5, ...), custom_call_target="tpu_custom_call" | custom-call | bytes 50331648 | tf_op jit(solution)/shard_map/pallas_call | solution.py:114
  86.5 5.6 %all-to-all-start.3 = ((bf16[16,128,128]{2,1,0:T(8,128)(2,1)}), bf16[16,128,128]{2,1,0:T(8,128)(2,1)S(1)}, u32[]{:S(2)}, u32[]{:S(2)}) async-start(bf16[16,128,128]{2,1,0:T(8,128)(2,1)} %get-tuple-element.50), calls=%async_computation.3 | async-start | bytes 1048576 | tf_op jit(solution)/shard_map/all_to_all | solution.py:520
  92.1 1.6 %reshape.74.refs_5_ = bf16[256,256]{1,0:T(8,128)(2,1)} reshape(bf16[128,1,2,256]{3,2,1,0:T(2,128)(2,1)} %param.26) | data formatting | bytes 262144 | tf_op jit(solution)/shard_map/reshape | solution.py:562
  95.0 5.0 %shard_map.322 = (bf16[1,512,512]{2,1,0:T(8,128)(2,1)}, bf16[2,512,512]{2,1,0:T(8,128)(2,1)}, bf16[5,512,512]{2,1,0:T(8,128)(2,1)}) custom-call(s32[8]{0:T(128)} %fusion.4.refs_0_, bf16[256,8192]{1,0:T(8,128)(2,1)} %refs_15_.1, bf16[256,4096]{1,0:T(8,128)(2,1)} %collective-permute-done.13.refs_2_.refs_4_.refs_6_.refs_8_.refs_10_.refs_12_.refs_14_.refs_16_, ...), custom_call_target="tpu_custom_call" | custom-call | bytes 8388608 | tf_op jit(solution)/shard_map/pallas_call | solution.py:114
  100.1 6.6 %shard_map.320.refs_1_ = f32[256,256]{1,0:T(8,128)} custom-call(s32[8]{0:T(128)} %fusion.4.refs_0_, bf16[8192,256]{1,0:T(8,128)(2,1)} %refs_1_.8, bf16[4,256,512]{2,1,0:T(8,128)(2,1)} %copy-done, bf16[4,256,512]{2,1,0:T(8,128)(2,1)} %collective-permute-done.7.refs_3_, bf16[4,256,512]{2,1,0:T(8,128)(2,1)} %copy-done.1, ...), custom_call_target="tpu_custom_call" | custom-call | flops 1073741824 | bytes 8388608 | tf_op jit(solution)/shard_map/pallas_call | solution.py:114
  108.6 3.3 %shard_map.323.refs_0_ = bf16[256,256]{1,0:T(8,128)(2,1)S(1)} custom-call(bf16[16,128,128]{2,1,0:T(8,128)(2,1)S(1)} %all-to-all-done.3.refs_0_, f32[256,256]{1,0:T(8,128)S(1)} %copy-done.10, bf16[64,256]{1,0:T(8,128)(2,1)S(1)} %copy-done.15, f32[5,128,128]{2,1,0:T(8,128)S(1)} %pad_maximum_fusion.refs_3_, bf16[4096,256]{1,0:T(8,128)(2,1)S(1)} %bitcast.12, ...), custom_call_target="tpu_custom_call" | custom-call | flops 134217728 | bytes 4194304 | tf_op jit(solution)/shard_map/pallas_call | solution.py:114
  114.2 1.7 %collective-permute-start.21 = (bf16[160,512]{1,0:T(8,128)(2,1)S(1)}, bf16[160,512]{1,0:T(8,128)(2,1)S(1)}, u32[]{:S(2)}, u32[]{:S(2)}) collective-permute-start(bf16[160,512]{1,0:T(8,128)(2,1)S(1)} %get-tuple-element.66), channel_id=1, source_target_pairs={{0,12},{1,13},{2,14},{3,15},{4,0},{5,1},{6,2},{7,3},{8,4},{9,5},{1... | collective-permute-start | bytes 491528 | tf_op jit(solution)/shard_map/ppermute | solution.py:37
  116.3 4.0 %collective-permute-done.20.refs_2_ = bf16[160,512]{1,0:T(8,128)(2,1)S(1)} collective-permute-done((bf16[160,512]{1,0:T(8,128)(2,1)S(1)}, bf16[160,512]{1,0:T(8,128)(2,1)S(1)}, u32[]{:S(2)}, u32[]{:S(2)}) %collective-permute-start.20) | collective-permute-done | bytes 163872 | tf_op jit(solution)/shard_map/ppermute | solution.py:37
  122.1 1.6 %collective-permute-start.23 = (bf16[288,512]{1,0:T(8,128)(2,1)S(1)}, bf16[288,512]{1,0:T(8,128)(2,1)S(1)}, u32[]{:S(2)}, u32[]{:S(2)}) collective-permute-start(bf16[288,512]{1,0:T(8,128)(2,1)S(1)} %get-tuple-element.71), channel_id=1, source_target_pairs={{0,12},{1,13},{2,14},{3,15},{4,0},{5,1},{6,2},{7,3},{8,4},{9,5},{1... | collective-permute-start | bytes 884744 | tf_op jit(solution)/shard_map/ppermute | solution.py:37
  124.6 1.7 %collective-permute-start.15 = (bf16[128,512]{1,0:T(8,128)(2,1)S(1)}, bf16[128,512]{1,0:T(8,128)(2,1)S(1)}, u32[]{:S(2)}, u32[]{:S(2)}) collective-permute-start(bf16[128,512]{1,0:T(8,128)(2,1)S(1)} %get-tuple-element.58), channel_id=1, source_target_pairs={{0,4},{1,5},{2,6},{3,7},{4,8},{5,9},{6,10},{7,11},{8,12},{9,13},{1... | collective-permute-start | bytes 393224 | tf_op jit(solution)/shard_map/ppermute | solution.py:37
  126.7 4.5 %collective-permute-done.22.refs_4_ = bf16[288,512]{1,0:T(8,128)(2,1)S(1)} collective-permute-done((bf16[288,512]{1,0:T(8,128)(2,1)S(1)}, bf16[288,512]{1,0:T(8,128)(2,1)S(1)}, u32[]{:S(2)}, u32[]{:S(2)}) %collective-permute-start.22) | collective-permute-done | bytes 294944 | tf_op jit(solution)/shard_map/ppermute | solution.py:37
  132.9 5.6 %collective-permute-start.24 = (bf16[288,512]{1,0:T(8,128)(2,1)S(1)}, bf16[288,512]{1,0:T(8,128)(2,1)S(1)}, u32[]{:S(2)}, u32[]{:S(2)}) collective-permute-start(bf16[288,512]{1,0:T(8,128)(2,1)S(1)} %shard_map.330.refs_1_), channel_id=1, source_target_pairs={{0,2},{1,3},{2,0},{3,1},{4,6},{5,7},{6,4},{7,5},{8,10},{9,11},{10,... | collective-permute-start | bytes 884744 | tf_op jit(solution)/shard_map/ppermute | solution.py:37
  138.9 1.7 %collective-permute-start.18 = (bf16[256,512]{1,0:T(8,128)(2,1)S(1)}, bf16[256,512]{1,0:T(8,128)(2,1)S(1)}, u32[]{:S(2)}, u32[]{:S(2)}) collective-permute-start(bf16[256,512]{1,0:T(8,128)(2,1)S(1)} %get-tuple-element.61), channel_id=1, source_target_pairs={{0,12},{1,13},{2,14},{3,15},{4,0},{5,1},{6,2},{7,3},{8,4},{9,5},{1... | collective-permute-start | bytes 786440 | tf_op jit(solution)/shard_map/ppermute | solution.py:37
  140.7 2.6 %shard_map.332 = (f32[4,512]{1,0:T(4,128)}, f32[4,256]{1,0:T(4,128)}, f32[4,256]{1,0:T(4,128)}, f32[4,512]{1,0:T(4,128)}, f32[4,512]{1,0:T(4,128)}, /*index=5*/f...) custom-call(f32[16,8,128]{2,1,0:T(8,128)} %copy-done.17, ...), custom_call_target="tpu_custom_call" | custom-call | bytes 1048576 | tf_op jit(solution)/shard_map/pallas_call | solution.py:114
  143.3 1.8 %collective-permute-done.17.refs_1_ = bf16[256,512]{1,0:T(8,128)(2,1)S(1)} collective-permute-done((bf16[256,512]{1,0:T(8,128)(2,1)S(1)}, bf16[256,512]{1,0:T(8,128)(2,1)S(1)}, u32[]{:S(2)}, u32[]{:S(2)}) %collective-permute-start.17) | collective-permute-done | bytes 262176 | tf_op jit(solution)/shard_map/ppermute | solution.py:37
  (98 shorter events, 24.2 us)
Async XLA Ops:
  2.5 27.1 %all-to-all-start = ((f32[16,48,128]{2,1,0:T(8,128)}), f32[16,48,128]{2,1,0:T(8,128)S(1)}, u32[]{:S(2)}, u32[]{:S(2)}) async-start(f32[16,48,128]{2,1,0:T(8,128)} %shard_map.309), calls=%async_computation | async-start | bytes 786432 | tf_op jit(solution)/shard_map/all_to_all | solution.py:451
  13.6 81.4 %collective-permute-start.13 = (bf16[256,4096]{1,0:T(8,128)(2,1)}, bf16[256,4096]{1,0:T(8,128)(2,1)}, u32[]{:S(2)}, u32[]{:S(2)}) collective-permute-start(bf16[256,4096]{1,0:T(8,128)(2,1)} %shard_map.321), channel_id=1, source_target_pairs={{0,1},{1,0},{2,3},{3,2},{4,5},{5,4},{6,7},{7,6},{8,9},{9,8},{10,11... | collective-permute-start | bytes 6291464 | tf_op jit(solution)/shard_map/ppermute | solution.py:37
  13.7 15.8 %collective-permute-start = (bf16[256,512]{1,0:T(8,128)(2,1)S(1)}, bf16[256,512]{1,0:T(8,128)(2,1)S(1)}, u32[]{:S(2)}, u32[]{:S(2)}) collective-permute-start(bf16[256,512]{1,0:T(8,128)(2,1)S(1)} %bitcast.6), channel_id=1, source_target_pairs={{0,4},{1,5},{2,6},{3,7},{4,8},{5,9},{6,10},{7,11},{8,12},{9,13},{1... | collective-permute-start | bytes 786440 | tf_op jit(solution)/shard_map/ppermute | solution.py:37
  14.3 15.3 %collective-permute-start.1 = (bf16[256,512]{1,0:T(8,128)(2,1)S(1)}, bf16[256,512]{1,0:T(8,128)(2,1)S(1)}, u32[]{:S(2)}, u32[]{:S(2)}) collective-permute-start(bf16[256,512]{1,0:T(8,128)(2,1)S(1)} %bitcast.7), channel_id=1, source_target_pairs={{0,12},{1,13},{2,14},{3,15},{4,0},{5,1},{6,2},{7,3},{8,4},{9,5},{1... | collective-permute-start | bytes 786440 | tf_op jit(solution)/shard_map/ppermute | solution.py:37
  15.9 13.7 %collective-permute-start.2 = (bf16[256,512]{1,0:T(8,128)(2,1)S(1)}, bf16[256,512]{1,0:T(8,128)(2,1)S(1)}, u32[]{:S(2)}, u32[]{:S(2)}) collective-permute-start(bf16[256,512]{1,0:T(8,128)(2,1)S(1)} %bitcast.8), channel_id=1, source_target_pairs={{0,8},{1,9},{2,10},{3,11},{4,12},{5,13},{6,14},{7,15},{8,0},{9,1},... | collective-permute-start | bytes 786440 | tf_op jit(solution)/shard_map/ppermute | solution.py:37
  18.8 4.3 %collective-permute-start.3 = (bf16[1,144,128]{2,1,0:T(8,128)(2,1)}, bf16[1,144,128]{2,1,0:T(8,128)(2,1)S(1)}, u32[]{:S(2)}, u32[]{:S(2)}) collective-permute-start(bf16[1,144,128]{2,1,0:T(8,128)(2,1)} %shard_map.310.refs_0_), channel_id=1, source_target_pairs={{0,16},{16,0},{32,48},{48,32},{64,80},{80,64},{96,112},{112,96},{1... | collective-permute-start | bytes 110600 | tf_op jit(solution)/shard_map/ppermute | solution.py:49
  23.9 5.4 %collective-permute-start.4 = (bf16[2,144,128]{2,1,0:T(8,128)(2,1)S(1)}, bf16[2,144,128]{2,1,0:T(8,128)(2,1)S(1)}, u32[]{:S(2)}, u32[]{:S(2)}) collective-permute-start(bf16[2,144,128]{2,1,0:T(8,128)(2,1)S(1)} %shard_map.311.refs_0_), channel_id=1, source_target_pairs={{0,32},{16,48},{32,0},{48,16},{64,96},{80,112},{96,64},{112,80},{1... | collective-permute-start | bytes 221192 | tf_op jit(solution)/shard_map/ppermute | solution.py:49
  30.5 18.1 %collective-permute-start.8 = (bf16[256,512]{1,0:T(8,128)(2,1)S(1)}, bf16[256,512]{1,0:T(8,128)(2,1)S(1)}, u32[]{:S(2)}, u32[]{:S(2)}) collective-permute-start(bf16[256,512]{1,0:T(8,128)(2,1)S(1)} %shard_map.318), channel_id=1, source_target_pairs={{0,2},{1,3},{2,0},{3,1},{4,6},{5,7},{6,4},{7,5},{8,10},{9,11},{10,... | collective-permute-start | bytes 786440 | tf_op jit(solution)/shard_map/ppermute | solution.py:37
  35.1 29.4 %all-to-all-start.1 = ((bf16[16,64,128]{2,1,0:T(8,128)(2,1)}), bf16[16,64,128]{2,1,0:T(8,128)(2,1)S(1)}, u32[]{:S(2)}, u32[]{:S(2)}) async-start(bf16[16,64,128]{2,1,0:T(8,128)(2,1)} %get-tuple-element.49), calls=%async_computation.1 | async-start | bytes 524288 | tf_op jit(solution)/shard_map/all_to_all | solution.py:469
  43.3 10.0 %collective-permute-start.5 = (bf16[4,144,128]{2,1,0:T(8,128)(2,1)S(1)}, bf16[4,144,128]{2,1,0:T(8,128)(2,1)S(1)}, u32[]{:S(2)}, u32[]{:S(2)}) collective-permute-start(bf16[4,144,128]{2,1,0:T(8,128)(2,1)S(1)} %shard_map.312.refs_4_.refs_0_), channel_id=1, source_target_pairs={{0,64},{16,80},{32,96},{48,112},{64,0},{80,16},{96,32},{112,48},{1... | collective-permute-start | bytes 442376 | tf_op jit(solution)/shard_map/ppermute | solution.py:49
  48.6 10.3 %collective-permute-start.9 = (bf16[256,512]{1,0:T(8,128)(2,1)S(1)}, bf16[256,512]{1,0:T(8,128)(2,1)S(1)}, u32[]{:S(2)}, u32[]{:S(2)}) collective-permute-start(bf16[256,512]{1,0:T(8,128)(2,1)S(1)} %collective-permute-done.8.refs_0_), channel_id=1, source_target_pairs={{0,12},{1,13},{2,14},{3,15},{4,0},{5,1},{6,2},{7,3},{8,4},{9,5},{1... | collective-permute-start | bytes 786440 | tf_op jit(solution)/shard_map/ppermute | solution.py:37
  48.8 14.9 %collective-permute-start.10 = (bf16[256,512]{1,0:T(8,128)(2,1)S(1)}, bf16[256,512]{1,0:T(8,128)(2,1)S(1)}, u32[]{:S(2)}, u32[]{:S(2)}) collective-permute-start(bf16[256,512]{1,0:T(8,128)(2,1)S(1)} %collective-permute-done.8.refs_0_), channel_id=1, source_target_pairs={{0,8},{1,9},{2,10},{3,11},{4,12},{5,13},{6,14},{7,15},{8,0},{9,1},... | collective-permute-start | bytes 786440 | tf_op jit(solution)/shard_map/ppermute | solution.py:37
  51.9 12.3 %collective-permute-start.11 = (bf16[256,512]{1,0:T(8,128)(2,1)S(1)}, bf16[256,512]{1,0:T(8,128)(2,1)S(1)}, u32[]{:S(2)}, u32[]{:S(2)}) collective-permute-start(bf16[256,512]{1,0:T(8,128)(2,1)S(1)} %collective-permute-done.8.refs_0_), channel_id=1, source_target_pairs={{0,4},{1,5},{2,6},{3,7},{4,8},{5,9},{6,10},{7,11},{8,12},{9,13},{1... | collective-permute-start | bytes 786440 | tf_op jit(solution)/shard_map/ppermute | solution.py:37
  53.7 21.2 %collective-permute-start.6 = (bf16[8,144,128]{2,1,0:T(8,128)(2,1)S(1)}, bf16[8,144,128]{2,1,0:T(8,128)(2,1)S(1)}, u32[]{:S(2)}, u32[]{:S(2)}) collective-permute-start(bf16[8,144,128]{2,1,0:T(8,128)(2,1)S(1)} %shard_map.315.refs_4_), channel_id=1, source_target_pairs={{0,128},{16,144},{32,160},{48,176},{64,192},{80,208},{96,224},{112... | collective-permute-start | bytes 884744 | tf_op jit(solution)/shard_map/ppermute | solution.py:49
  56.0 38.8 %copy-start = (bf16[4,256,512]{2,1,0:T(8,128)(2,1)}, bf16[4,256,512]{2,1,0:T(8,128)(2,1)S(1)}, u32[]{:S(2)}) copy-start(bf16[4,256,512]{2,1,0:T(8,128)(2,1)S(1)} %shard_map.317.refs_2_) | copy-start | bytes 3145732
  56.0 36.1 %copy-start.19 = (s32[128]{0:T(128)S(1)}, s32[128]{0:T(128)}, u32[]{:S(2)}) copy-start(s32[128]{0:T(128)} %param.27) | copy-start | bytes 1540
  59.0 41.1 %collective-permute-start.7 = (bf16[4,256,512]{2,1,0:T(8,128)(2,1)S(1)}, bf16[4,256,512]{2,1,0:T(8,128)(2,1)}, u32[]{:S(2)}, u32[]{:S(2)}) collective-permute-start(bf16[4,256,512]{2,1,0:T(8,128)(2,1)S(1)} %shard_map.317.refs_2_), channel_id=1, source_target_pairs={{0,1},{1,0},{2,3},{3,2},{4,5},{5,4},{6,7},{7,6},{8,9},{9,8},{10,11... | collective-permute-start | bytes 3145736 | tf_op jit(solution)/shard_map/ppermute | solution.py:37
  64.3 35.7 %copy-start.1 = (bf16[4,256,512]{2,1,0:T(8,128)(2,1)}, bf16[4,256,512]{2,1,0:T(8,128)(2,1)S(1)}, u32[]{:S(2)}) copy-start(bf16[4,256,512]{2,1,0:T(8,128)(2,1)S(1)} %shard_map.319.refs_4_) | copy-start | bytes 3145732
  64.3 35.7 %collective-permute-start.12 = (bf16[4,256,512]{2,1,0:T(8,128)(2,1)S(1)}, bf16[4,256,512]{2,1,0:T(8,128)(2,1)}, u32[]{:S(2)}, u32[]{:S(2)}) collective-permute-start(bf16[4,256,512]{2,1,0:T(8,128)(2,1)S(1)} %shard_map.319.refs_4_), channel_id=1, source_target_pairs={{0,1},{1,0},{2,3},{3,2},{4,5},{5,4},{6,7},{7,6},{8,9},{9,8},{10,11... | collective-permute-start | bytes 3145736 | tf_op jit(solution)/shard_map/ppermute | solution.py:37
  66.1 16.9 %all-to-all-start.2 = ((f32[16,8,128]{2,1,0:T(8,128)}), f32[16,8,128]{2,1,0:T(8,128)S(1)}, u32[]{:S(2)}, u32[]{:S(2)}) async-start(f32[16,8,128]{2,1,0:T(8,128)} %shard_map.314), calls=%async_computation.2 | async-start | bytes 131072 | tf_op jit(solution)/shard_map/all_to_all | solution.py:479
  86.5 20.1 %all-to-all-start.3 = ((bf16[16,128,128]{2,1,0:T(8,128)(2,1)}), bf16[16,128,128]{2,1,0:T(8,128)(2,1)S(1)}, u32[]{:S(2)}, u32[]{:S(2)}) async-start(bf16[16,128,128]{2,1,0:T(8,128)(2,1)} %get-tuple-element.50), calls=%async_computation.3 | async-start | bytes 1048576 | tf_op jit(solution)/shard_map/all_to_all | solution.py:520
  111.9 1.5 %collective-permute-start.14 = (bf16[256,256]{1,0:T(8,128)(2,1)S(1)}, bf16[256,256]{1,0:T(8,128)(2,1)S(1)}, u32[]{:S(2)}, u32[]{:S(2)}) collective-permute-start(bf16[256,256]{1,0:T(8,128)(2,1)S(1)} %shard_map.323.refs_0_), channel_id=1, source_target_pairs={{0,1},{1,0},{2,3},{3,2},{4,5},{5,4},{6,7},{7,6},{8,9},{9,8},{10,11... | collective-permute-start | bytes 393224 | tf_op jit(solution)/shard_map/ppermute | solution.py:37
  112.2 1.2 collective-permute-start.19
  113.8 6.5 %collective-permute-start.20 = (bf16[160,512]{1,0:T(8,128)(2,1)S(1)}, bf16[160,512]{1,0:T(8,128)(2,1)S(1)}, u32[]{:S(2)}, u32[]{:S(2)}) collective-permute-start(bf16[160,512]{1,0:T(8,128)(2,1)S(1)} %get-tuple-element.65), channel_id=1, source_target_pairs={{0,4},{1,5},{2,6},{3,7},{4,8},{5,9},{6,10},{7,11},{8,12},{9,13},{1... | collective-permute-start | bytes 491528 | tf_op jit(solution)/shard_map/ppermute | solution.py:37
  114.2 7.4 %collective-permute-start.21 = (bf16[160,512]{1,0:T(8,128)(2,1)S(1)}, bf16[160,512]{1,0:T(8,128)(2,1)S(1)}, u32[]{:S(2)}, u32[]{:S(2)}) collective-permute-start(bf16[160,512]{1,0:T(8,128)(2,1)S(1)} %get-tuple-element.66), channel_id=1, source_target_pairs={{0,12},{1,13},{2,14},{3,15},{4,0},{5,1},{6,2},{7,3},{8,4},{9,5},{1... | collective-permute-start | bytes 491528 | tf_op jit(solution)/shard_map/ppermute | solution.py:37
  121.7 9.6 %collective-permute-start.22 = (bf16[288,512]{1,0:T(8,128)(2,1)S(1)}, bf16[288,512]{1,0:T(8,128)(2,1)S(1)}, u32[]{:S(2)}, u32[]{:S(2)}) collective-permute-start(bf16[288,512]{1,0:T(8,128)(2,1)S(1)} %get-tuple-element.70), channel_id=1, source_target_pairs={{0,4},{1,5},{2,6},{3,7},{4,8},{5,9},{6,10},{7,11},{8,12},{9,13},{1... | collective-permute-start | bytes 884744 | tf_op jit(solution)/shard_map/ppermute | solution.py:37
  122.1 10.7 %collective-permute-start.23 = (bf16[288,512]{1,0:T(8,128)(2,1)S(1)}, bf16[288,512]{1,0:T(8,128)(2,1)S(1)}, u32[]{:S(2)}, u32[]{:S(2)}) collective-permute-start(bf16[288,512]{1,0:T(8,128)(2,1)S(1)} %get-tuple-element.71), channel_id=1, source_target_pairs={{0,12},{1,13},{2,14},{3,15},{4,0},{5,1},{6,2},{7,3},{8,4},{9,5},{1... | collective-permute-start | bytes 884744 | tf_op jit(solution)/shard_map/ppermute | solution.py:37
  124.6 13.8 %collective-permute-start.15 = (bf16[128,512]{1,0:T(8,128)(2,1)S(1)}, bf16[128,512]{1,0:T(8,128)(2,1)S(1)}, u32[]{:S(2)}, u32[]{:S(2)}) collective-permute-start(bf16[128,512]{1,0:T(8,128)(2,1)S(1)} %get-tuple-element.58), channel_id=1, source_target_pairs={{0,4},{1,5},{2,6},{3,7},{4,8},{5,9},{6,10},{7,11},{8,12},{9,13},{1... | collective-permute-start | bytes 393224 | tf_op jit(solution)/shard_map/ppermute | solution.py:37
  126.3 12.2 %collective-permute-start.16 = (bf16[128,512]{1,0:T(8,128)(2,1)S(1)}, bf16[128,512]{1,0:T(8,128)(2,1)S(1)}, u32[]{:S(2)}, u32[]{:S(2)}) collective-permute-start(bf16[128,512]{1,0:T(8,128)(2,1)S(1)} %get-tuple-element.59), channel_id=1, source_target_pairs={{0,12},{1,13},{2,14},{3,15},{4,0},{5,1},{6,2},{7,3},{8,4},{9,5},{1... | collective-permute-start | bytes 393224 | tf_op jit(solution)/shard_map/ppermute | solution.py:37
  132.9 13.8 %collective-permute-start.24 = (bf16[288,512]{1,0:T(8,128)(2,1)S(1)}, bf16[288,512]{1,0:T(8,128)(2,1)S(1)}, u32[]{:S(2)}, u32[]{:S(2)}) collective-permute-start(bf16[288,512]{1,0:T(8,128)(2,1)S(1)} %shard_map.330.refs_1_), channel_id=1, source_target_pairs={{0,2},{1,3},{2,0},{3,1},{4,6},{5,7},{6,4},{7,5},{8,10},{9,11},{10,... | collective-permute-start | bytes 884744 | tf_op jit(solution)/shard_map/ppermute | solution.py:37
  138.6 6.4 %collective-permute-start.17 = (bf16[256,512]{1,0:T(8,128)(2,1)S(1)}, bf16[256,512]{1,0:T(8,128)(2,1)S(1)}, u32[]{:S(2)}, u32[]{:S(2)}) collective-permute-start(bf16[256,512]{1,0:T(8,128)(2,1)S(1)} %get-tuple-element.60), channel_id=1, source_target_pairs={{0,4},{1,5},{2,6},{3,7},{4,8},{5,9},{6,10},{7,11},{8,12},{9,13},{1... | collective-permute-start | bytes 786440 | tf_op jit(solution)/shard_map/ppermute | solution.py:37
  138.9 7.6 %collective-permute-start.18 = (bf16[256,512]{1,0:T(8,128)(2,1)S(1)}, bf16[256,512]{1,0:T(8,128)(2,1)S(1)}, u32[]{:S(2)}, u32[]{:S(2)}) collective-permute-start(bf16[256,512]{1,0:T(8,128)(2,1)S(1)} %get-tuple-element.61), channel_id=1, source_target_pairs={{0,12},{1,13},{2,14},{3,15},{4,0},{5,1},{6,2},{7,3},{8,4},{9,5},{1... | collective-permute-start | bytes 786440 | tf_op jit(solution)/shard_map/ppermute | solution.py:37
  (17 other events, 176.3 us)

commit v4 on v3

--- a/solution.py
+++ b/solution.py
@@ -327,12 +327,6 @@
                 ] = result[first : first + ROWS].astype(bf16)
 
 
-def give_columns(core, *refs):
-    weight, out = refs[:8], refs[8]
-    for k in range(8):
-        out[:, k * 512 : (k + 1) * 512] = weight[k][...]
-
-
 def columns(k, other):
     def view(ref, order):
         place = order[k] >> 1 if other else order[k]
@@ -345,13 +339,29 @@
     return [(w, (256, 512), columns(k, i == 1)) for i, w in enumerate(weights)]
 
 
-def lay_out(counts, order, *refs):
-    total = sum(counts)
-    blocks, outs = list(refs[: 2 * total]), refs[2 * total :]
-    for out, count in zip(outs, counts):
-        for i in range(count):
-            out[i, :256] = blocks.pop(0)[...]
-            out[i, 256:] = blocks.pop(0)[...]
+def gather_blocks(shapes, places, scalar, *arrays, moved):
+    count = len(arrays)
+
+    def body(*refs):
+        outs, sems = refs[1 + count : -1], refs[-1]
+        copies = [
+            pltpu.make_async_copy(view(refs[1 + i], refs[0]), outs[o].at[index], sems.at[n])
+            for n, (i, view, o, index) in enumerate(places)
+        ]
+        for copy in copies:
+            copy.start()
+        for copy in copies:
+            copy.wait()
+
+    return pl.pallas_call(
+        body,
+        in_specs=[SMEM] + [HBM] * count,
+        out_specs=[VMEM] * len(shapes),
+        out_shape=[jax.ShapeDtypeStruct(shape, bf16) for shape in shapes],
+        scratch_shapes=[pltpu.SemaphoreType.DMA((len(places),))],
+        cost_estimate=pl.CostEstimate(flops=0, bytes_accessed=moved, transcendentals=0),
+        compiler_params=pltpu.CompilerParams(vmem_limit_bytes=LARGE),
+    )(scalar, *arrays)
 
 
 def project_far(mine, other, weight, down, down_other, right, left, low):
@@ -487,23 +497,26 @@
             :, pl.ds(pl.multiple_of((2 * k + 1 - core[0]) * 512, 512), 512)
         ]
 
-    give = call(
-        give_columns,
-        [((256, 4096), bf16)],
+    (give,) = gather_blocks(
+        [(256, 4096)],
+        [(0, given(k), 0, (slice(None), pl.ds(512 * k, 512))) for k in range(8)],
         core.reshape(1),
-        scalars=1,
-        fetch=[(output_base_weight, (256, 512), given(k)) for k in range(8)],
+        output_base_weight,
         moved=4 << 20,
     )
     weights = (output_base_weight, to_core(give))
     used = ((5,), (3, 7), (4, 1, 2, 6, 0))
     counts = tuple(map(len, used))
-    w_far, w_near, w_later = call(
-        functools.partial(lay_out, counts),
-        [((count, 512, 512), bf16) for count in counts],
+    w_far, w_near, w_later = gather_blocks(
+        [(count, 512, 512) for count in counts],
+        [
+            (i, columns(k, i == 1), o, (n, pl.ds(256 * i, 256)))
+            for o, ks in enumerate(used)
+            for n, k in enumerate(ks)
+            for i in range(2)
+        ],
         order,
-        scalars=1,
-        fetch=[one for ks in used for k in ks for one in columns_of(weights, k)],
+        *weights,
         moved=8 << 20,
     )
 

time: 149 us -> 149 us (level)
    pallas_call x18 -> x16, Pallas kernels: 31.6 us -> 23.6 us  [call(): pl.pallas_call(body, in_specs=[SMEM] * scalars + [VMEM] * (first - scalar...]
    pallas_call x0 -> x2, Pallas kernels: none -> 7.92 us  [gather_blocks(): pl.pallas_call(body, in_specs=[SMEM] + [HBM] * count, out_specs=[VMEM] *...]
where the time goes in v4:
time: 149 us; the launch traced here: 148 us
  starting transfers between devices  63.2 us (42%)
  waiting for transfers between devices  43.9 us (29%)
  Pallas kernels  32.5 us (22%)
  local copies, waits for them, and re-layouts  5.77 us (4%)
    ppermute x21, waiting for transfers between devices, shift(): return lax.ppermute(value, 'tp', [(i, move(i)) for i in range(N)])  28.4 us
    ppermute x21, starting transfers between devices, shift(): return lax.ppermute(value, 'tp', [(i, move(i)) for i in range(N)])  27.6 us
    pallas_call x16, Pallas kernels, call(): pl.pallas_call(body, in_specs=[SMEM] * scalars + [VMEM] * (first - scalar...  23.6 us
    all_to_all x1, starting transfers between devices, on_device(): squares = lax.all_to_all(squares_sent, 'tp', 0, 0)  8.8 us
    all_to_all x1, starting transfers between devices, on_device(): all_parts = lax.all_to_all(message, 'rep', 0, 0)  8.2 us
    all_to_all x1, starting transfers between devices, on_device(): parts = lax.all_to_all(gradient, 'rep', 0, 0)  8.1 us
    all_to_all x1, waiting for transfers between devices, on_device(): squares = lax.all_to_all(squares_sent, 'tp', 0, 0)  8.03 us
    pallas_call x2, Pallas kernels, gather_blocks(): pl.pallas_call(body, in_specs=[SMEM] + [HBM] * count, out_specs=[VMEM] *...  7.92 us
  transfers between devices with their start and end apart: 29, of which 14 were waited for; matrix products, arithmetic and copies ran while one was open for 2% of the time, Pallas kernels for 17%

profile of v4, /device:TPU:78, one launch (start us, length us, event | category | flops | bytes accessed | tf_op | source)
XLA Modules:
  0.0 147.9 jit_solution(15053912129930704171)
XLA Ops:
  0.6 1.9 %shard_map.309 = f32[16,48,128]{2,1,0:T(8,128)} custom-call(f32[1,64,512]{2,1,0:T(8,128)} %refs_0_.2, f32[1,64,256]{2,1,0:T(8,128)} %refs_1_.6, f32[1,64,256]{2,1,0:T(8,128)} %refs_2_.3, f32[1,64,512]{2,1,0:T(8,128)} %refs_3_.3), custom_call_target="tpu_custom_call" | custom-call | bytes 1048576 | tf_op jit(solution)/shard_map/pallas_call | solution.py:114
  2.5 8.1 %all-to-all-start = ((f32[16,48,128]{2,1,0:T(8,128)}), f32[16,48,128]{2,1,0:T(8,128)S(1)}, u32[]{:S(2)}, u32[]{:S(2)}) async-start(f32[16,48,128]{2,1,0:T(8,128)} %shard_map.309), calls=%async_computation | async-start | bytes 786432 | tf_op jit(solution)/shard_map/all_to_all | solution.py:461
  10.6 3.0 %shard_map.321 = bf16[256,4096]{1,0:T(8,128)(2,1)} custom-call(s32[1]{0:T(128)} %bitcast.3.refs_0_, bf16[256,8192]{1,0:T(8,128)(2,1)} %refs_1_.10), custom_call_target="tpu_custom_call" | custom-call | bytes 4194304 | tf_op jit(solution)/shard_map/pallas_call | solution.py:356
  14.3 1.5 %collective-permute-start.1 = (bf16[256,512]{1,0:T(8,128)(2,1)S(1)}, bf16[256,512]{1,0:T(8,128)(2,1)S(1)}, u32[]{:S(2)}, u32[]{:S(2)}) collective-permute-start(bf16[256,512]{1,0:T(8,128)(2,1)S(1)} %bitcast.7), channel_id=1, source_target_pairs={{0,12},{1,13},{2,14},{3,15},{4,0},{5,1},{6,2},{7,3},{8,4},{9,5},{1... | collective-permute-start | bytes 786440 | tf_op jit(solution)/shard_map/ppermute | solution.py:37
  17.2 1.6 %shard_map.310.refs_0_ = bf16[1,144,128]{2,1,0:T(8,128)(2,1)} custom-call(f32[4,512]{1,0:T(4,128)} %refs_1_.11, f32[4,256]{1,0:T(4,128)} %refs_2_.5, f32[4,256]{1,0:T(4,128)} %refs_3_.5, f32[4,512]{1,0:T(4,128)} %refs_4_.3, f32[4,512]{1,0:T(4,128)} %refs_5_.3, f32[4,256]{1,0:T(4,128)} %refs_6_.3, f32[4,256]{1,0:T(4,128)} %refs_7_.3, f32[4,512]{1,0:T(4,128)} %refs_8_.3, ...), custom_call_target="tpu_custom_call" | custom-call | bytes 1048576 | tf_op jit(solution)/shard_map/pallas_call | solution.py:114
  18.8 1.5 %collective-permute-start.3 = (bf16[1,144,128]{2,1,0:T(8,128)(2,1)}, bf16[1,144,128]{2,1,0:T(8,128)(2,1)S(1)}, u32[]{:S(2)}, u32[]{:S(2)}) collective-permute-start(bf16[1,144,128]{2,1,0:T(8,128)(2,1)} %shard_map.310.refs_0_), channel_id=1, source_target_pairs={{0,16},{16,0},{32,48},{48,32},{64,80},{80,64},{96,112},{112,96},{1... | collective-permute-start | bytes 110600 | tf_op jit(solution)/shard_map/ppermute | solution.py:49
  20.4 2.7 %collective-permute-done.3.refs_1_ = bf16[1,144,128]{2,1,0:T(8,128)(2,1)S(1)} collective-permute-done((bf16[1,144,128]{2,1,0:T(8,128)(2,1)}, bf16[1,144,128]{2,1,0:T(8,128)(2,1)S(1)}, u32[]{:S(2)}, u32[]{:S(2)}) %collective-permute-start.3) | collective-permute-done | bytes 36896 | tf_op jit(solution)/shard_map/ppermute | solution.py:49
  24.6 4.8 %collective-permute-done.4.refs_1_ = bf16[2,144,128]{2,1,0:T(8,128)(2,1)S(1)} collective-permute-done((bf16[2,144,128]{2,1,0:T(8,128)(2,1)S(1)}, bf16[2,144,128]{2,1,0:T(8,128)(2,1)S(1)}, u32[]{:S(2)}, u32[]{:S(2)}) %collective-permute-start.4) | collective-permute-done | bytes 73760 | tf_op jit(solution)/shard_map/ppermute | solution.py:49
  30.5 4.6 %collective-permute-start.8 = (bf16[256,512]{1,0:T(8,128)(2,1)S(1)}, bf16[256,512]{1,0:T(8,128)(2,1)S(1)}, u32[]{:S(2)}, u32[]{:S(2)}) collective-permute-start(bf16[256,512]{1,0:T(8,128)(2,1)S(1)} %shard_map.318), channel_id=1, source_target_pairs={{0,2},{1,3},{2,0},{3,1},{4,6},{5,7},{6,4},{7,5},{8,10},{9,11},{10,... | collective-permute-start | bytes 786440 | tf_op jit(solution)/shard_map/ppermute | solution.py:37
  35.1 8.2 %all-to-all-start.1 = ((bf16[16,64,128]{2,1,0:T(8,128)(2,1)}), bf16[16,64,128]{2,1,0:T(8,128)(2,1)S(1)}, u32[]{:S(2)}, u32[]{:S(2)}) async-start(bf16[16,64,128]{2,1,0:T(8,128)(2,1)} %get-tuple-element.49), calls=%async_computation.1 | async-start | bytes 524288 | tf_op jit(solution)/shard_map/all_to_all | solution.py:479
  43.8 4.8 %collective-permute-done.8.refs_0_ = bf16[256,512]{1,0:T(8,128)(2,1)S(1)} collective-permute-done((bf16[256,512]{1,0:T(8,128)(2,1)S(1)}, bf16[256,512]{1,0:T(8,128)(2,1)S(1)}, u32[]{:S(2)}, u32[]{:S(2)}) %collective-permute-start.8) | collective-permute-done | bytes 262176 | tf_op jit(solution)/shard_map/ppermute | solution.py:37
  48.7 3.1 %collective-permute-start.10 = (bf16[256,512]{1,0:T(8,128)(2,1)S(1)}, bf16[256,512]{1,0:T(8,128)(2,1)S(1)}, u32[]{:S(2)}, u32[]{:S(2)}) collective-permute-start(bf16[256,512]{1,0:T(8,128)(2,1)S(1)} %collective-permute-done.8.refs_0_), channel_id=1, source_target_pairs={{0,8},{1,9},{2,10},{3,11},{4,12},{5,13},{6,14},{7,15},{8,0},{9,1},... | collective-permute-start | bytes 786440 | tf_op jit(solution)/shard_map/ppermute | solution.py:37
  53.7 2.2 %collective-permute-start.6 = (bf16[8,144,128]{2,1,0:T(8,128)(2,1)S(1)}, bf16[8,144,128]{2,1,0:T(8,128)(2,1)S(1)}, u32[]{:S(2)}, u32[]{:S(2)}) collective-permute-start(bf16[8,144,128]{2,1,0:T(8,128)(2,1)S(1)} %shard_map.315.refs_4_), channel_id=1, source_target_pairs={{0,128},{16,144},{32,160},{48,176},{64,192},{80,208},{96,224},{112... | collective-permute-start | bytes 884744 | tf_op jit(solution)/shard_map/ppermute | solution.py:49
  56.0 2.9 %collective-permute-done.9.refs_1_ = bf16[256,512]{1,0:T(8,128)(2,1)S(1)} collective-permute-done((bf16[256,512]{1,0:T(8,128)(2,1)S(1)}, bf16[256,512]{1,0:T(8,128)(2,1)S(1)}, u32[]{:S(2)}, u32[]{:S(2)}) %collective-permute-start.9) | collective-permute-done | bytes 262176 | tf_op jit(solution)/shard_map/ppermute | solution.py:37
  58.9 4.7 %collective-permute-done.10.refs_2_ = bf16[256,512]{1,0:T(8,128)(2,1)S(1)} collective-permute-done((bf16[256,512]{1,0:T(8,128)(2,1)S(1)}, bf16[256,512]{1,0:T(8,128)(2,1)S(1)}, u32[]{:S(2)}, u32[]{:S(2)}) %collective-permute-start.10) | collective-permute-done | bytes 262176 | tf_op jit(solution)/shard_map/ppermute | solution.py:37
  66.1 8.8 %all-to-all-start.2 = ((f32[16,8,128]{2,1,0:T(8,128)}), f32[16,8,128]{2,1,0:T(8,128)S(1)}, u32[]{:S(2)}, u32[]{:S(2)}) async-start(f32[16,8,128]{2,1,0:T(8,128)} %shard_map.314), calls=%async_computation.2 | async-start | bytes 131072 | tf_op jit(solution)/shard_map/all_to_all | solution.py:489
  74.9 8.0 %all-to-all-done.2.refs_2_.refs_0_ = f32[16,8,128]{2,1,0:T(8,128)S(1)} async-done(((f32[16,8,128]{2,1,0:T(8,128)}), f32[16,8,128]{2,1,0:T(8,128)S(1)}, u32[]{:S(2)}, u32[]{:S(2)}) %all-to-all-start.2) | async-done | bytes 65568 | tf_op jit(solution)/shard_map/all_to_all | solution.py:489
  83.6 2.9 %shard_map.316 = (bf16[16,128,128]{2,1,0:T(8,128)(2,1)}, bf16[64,256]{1,0:T(8,128)(2,1)}, bf16[64,256]{1,0:T(8,128)(2,1)}, bf16[64,512]{1,0:T(8,128)(2,1)}) custom-call(s32[1]{0:T(128)} %bitcast.refs_0_, bf16[256,512]{1,0:T(8,128)(2,1)} %bitcast.5, f32[16,8,128]{2,1,0:T(8,128)} %copy-done.17, bf16[16,64,128]{2,1,0:T(8,128)(2,1)} %copy-done.5, ...), custom_call_target="tpu_custom_call" | custom-call | bytes 50331648 | tf_op jit(solution)/shard_map/pallas_call | solution.py:114
  86.5 5.6 %all-to-all-start.3 = ((bf16[16,128,128]{2,1,0:T(8,128)(2,1)}), bf16[16,128,128]{2,1,0:T(8,128)(2,1)S(1)}, u32[]{:S(2)}, u32[]{:S(2)}) async-start(bf16[16,128,128]{2,1,0:T(8,128)(2,1)} %get-tuple-element.50), calls=%async_computation.3 | async-start | bytes 1048576 | tf_op jit(solution)/shard_map/all_to_all | solution.py:533
  92.1 1.6 %reshape.74.refs_5_ = bf16[256,256]{1,0:T(8,128)(2,1)} reshape(bf16[128,1,2,256]{3,2,1,0:T(2,128)(2,1)} %param.26) | data formatting | bytes 262144 | tf_op jit(solution)/shard_map/reshape | solution.py:575
  95.0 4.9 %shard_map.322 = (bf16[1,512,512]{2,1,0:T(8,128)(2,1)}, bf16[2,512,512]{2,1,0:T(8,128)(2,1)}, bf16[5,512,512]{2,1,0:T(8,128)(2,1)}) custom-call(s32[8]{0:T(128)} %fusion.4.refs_0_, bf16[256,8192]{1,0:T(8,128)(2,1)} %refs_1_.10, bf16[256,4096]{1,0:T(8,128)(2,1)} %collective-permute-done.13.refs_2_), custom_call_target="tpu_custom_call" | custom-call | bytes 8388608 | tf_op jit(solution)/shard_map/pallas_call | solution.py:356
  100.0 6.6 %shard_map.320.refs_1_ = f32[256,256]{1,0:T(8,128)} custom-call(s32[8]{0:T(128)} %fusion.4.refs_0_, bf16[8192,256]{1,0:T(8,128)(2,1)} %refs_1_.8, bf16[4,256,512]{2,1,0:T(8,128)(2,1)} %copy-done, bf16[4,256,512]{2,1,0:T(8,128)(2,1)} %collective-permute-done.7.refs_3_, bf16[4,256,512]{2,1,0:T(8,128)(2,1)} %copy-done.1, ...), custom_call_target="tpu_custom_call" | custom-call | flops 1073741824 | bytes 8388608 | tf_op jit(solution)/shard_map/pallas_call | solution.py:114
  108.6 3.3 %shard_map.323.refs_0_ = bf16[256,256]{1,0:T(8,128)(2,1)S(1)} custom-call(bf16[16,128,128]{2,1,0:T(8,128)(2,1)S(1)} %all-to-all-done.3.refs_0_, f32[256,256]{1,0:T(8,128)S(1)} %copy-done.10, bf16[64,256]{1,0:T(8,128)(2,1)S(1)} %copy-done.15, f32[5,128,128]{2,1,0:T(8,128)S(1)} %pad_maximum_fusion.refs_3_, bf16[4096,256]{1,0:T(8,128)(2,1)S(1)} %bitcast.12, ...), custom_call_target="tpu_custom_call" | custom-call | flops 134217728 | bytes 4194304 | tf_op jit(solution)/shard_map/pallas_call | solution.py:114
  114.2 1.7 %collective-permute-start.21 = (bf16[160,512]{1,0:T(8,128)(2,1)S(1)}, bf16[160,512]{1,0:T(8,128)(2,1)S(1)}, u32[]{:S(2)}, u32[]{:S(2)}) collective-permute-start(bf16[160,512]{1,0:T(8,128)(2,1)S(1)} %get-tuple-element.66), channel_id=1, source_target_pairs={{0,12},{1,13},{2,14},{3,15},{4,0},{5,1},{6,2},{7,3},{8,4},{9,5},{1... | collective-permute-start | bytes 491528 | tf_op jit(solution)/shard_map/ppermute | solution.py:37
  116.3 4.0 %collective-permute-done.20.refs_2_ = bf16[160,512]{1,0:T(8,128)(2,1)S(1)} collective-permute-done((bf16[160,512]{1,0:T(8,128)(2,1)S(1)}, bf16[160,512]{1,0:T(8,128)(2,1)S(1)}, u32[]{:S(2)}, u32[]{:S(2)}) %collective-permute-start.20) | collective-permute-done | bytes 163872 | tf_op jit(solution)/shard_map/ppermute | solution.py:37
  122.1 1.6 %collective-permute-start.23 = (bf16[288,512]{1,0:T(8,128)(2,1)S(1)}, bf16[288,512]{1,0:T(8,128)(2,1)S(1)}, u32[]{:S(2)}, u32[]{:S(2)}) collective-permute-start(bf16[288,512]{1,0:T(8,128)(2,1)S(1)} %get-tuple-element.71), channel_id=1, source_target_pairs={{0,12},{1,13},{2,14},{3,15},{4,0},{5,1},{6,2},{7,3},{8,4},{9,5},{1... | collective-permute-start | bytes 884744 | tf_op jit(solution)/shard_map/ppermute | solution.py:37
  124.6 1.7 %collective-permute-start.15 = (bf16[128,512]{1,0:T(8,128)(2,1)S(1)}, bf16[128,512]{1,0:T(8,128)(2,1)S(1)}, u32[]{:S(2)}, u32[]{:S(2)}) collective-permute-start(bf16[128,512]{1,0:T(8,128)(2,1)S(1)} %get-tuple-element.58), channel_id=1, source_target_pairs={{0,4},{1,5},{2,6},{3,7},{4,8},{5,9},{6,10},{7,11},{8,12},{9,13},{1... | collective-permute-start | bytes 393224 | tf_op jit(solution)/shard_map/ppermute | solution.py:37
  126.7 4.5 %collective-permute-done.22.refs_4_ = bf16[288,512]{1,0:T(8,128)(2,1)S(1)} collective-permute-done((bf16[288,512]{1,0:T(8,128)(2,1)S(1)}, bf16[288,512]{1,0:T(8,128)(2,1)S(1)}, u32[]{:S(2)}, u32[]{:S(2)}) %collective-permute-start.22) | collective-permute-done | bytes 294944 | tf_op jit(solution)/shard_map/ppermute | solution.py:37
  132.8 5.6 %collective-permute-start.24 = (bf16[288,512]{1,0:T(8,128)(2,1)S(1)}, bf16[288,512]{1,0:T(8,128)(2,1)S(1)}, u32[]{:S(2)}, u32[]{:S(2)}) collective-permute-start(bf16[288,512]{1,0:T(8,128)(2,1)S(1)} %shard_map.330.refs_1_), channel_id=1, source_target_pairs={{0,2},{1,3},{2,0},{3,1},{4,6},{5,7},{6,4},{7,5},{8,10},{9,11},{10,... | collective-permute-start | bytes 884744 | tf_op jit(solution)/shard_map/ppermute | solution.py:37
  138.9 1.7 %collective-permute-start.18 = (bf16[256,512]{1,0:T(8,128)(2,1)S(1)}, bf16[256,512]{1,0:T(8,128)(2,1)S(1)}, u32[]{:S(2)}, u32[]{:S(2)}) collective-permute-start(bf16[256,512]{1,0:T(8,128)(2,1)S(1)} %get-tuple-element.61), channel_id=1, source_target_pairs={{0,12},{1,13},{2,14},{3,15},{4,0},{5,1},{6,2},{7,3},{8,4},{9,5},{1... | collective-permute-start | bytes 786440 | tf_op jit(solution)/shard_map/ppermute | solution.py:37
  140.6 2.6 %shard_map.332 = (f32[4,512]{1,0:T(4,128)}, f32[4,256]{1,0:T(4,128)}, f32[4,256]{1,0:T(4,128)}, f32[4,512]{1,0:T(4,128)}, f32[4,512]{1,0:T(4,128)}, /*index=5*/f...) custom-call(f32[16,8,128]{2,1,0:T(8,128)} %copy-done.17, ...), custom_call_target="tpu_custom_call" | custom-call | bytes 1048576 | tf_op jit(solution)/shard_map/pallas_call | solution.py:114
  143.2 1.8 %collective-permute-done.17.refs_1_ = bf16[256,512]{1,0:T(8,128)(2,1)S(1)} collective-permute-done((bf16[256,512]{1,0:T(8,128)(2,1)S(1)}, bf16[256,512]{1,0:T(8,128)(2,1)S(1)}, u32[]{:S(2)}, u32[]{:S(2)}) %collective-permute-start.17) | collective-permute-done | bytes 262176 | tf_op jit(solution)/shard_map/ppermute | solution.py:37
  (98 shorter events, 24.2 us)
Async XLA Ops:
  2.5 27.1 %all-to-all-start = ((f32[16,48,128]{2,1,0:T(8,128)}), f32[16,48,128]{2,1,0:T(8,128)S(1)}, u32[]{:S(2)}, u32[]{:S(2)}) async-start(f32[16,48,128]{2,1,0:T(8,128)} %shard_map.309), calls=%async_computation | async-start | bytes 786432 | tf_op jit(solution)/shard_map/all_to_all | solution.py:461
  13.6 81.4 %collective-permute-start.13 = (bf16[256,4096]{1,0:T(8,128)(2,1)}, bf16[256,4096]{1,0:T(8,128)(2,1)}, u32[]{:S(2)}, u32[]{:S(2)}) collective-permute-start(bf16[256,4096]{1,0:T(8,128)(2,1)} %shard_map.321), channel_id=1, source_target_pairs={{0,1},{1,0},{2,3},{3,2},{4,5},{5,4},{6,7},{7,6},{8,9},{9,8},{10,11... | collective-permute-start | bytes 6291464 | tf_op jit(solution)/shard_map/ppermute | solution.py:37
  13.7 15.8 %collective-permute-start = (bf16[256,512]{1,0:T(8,128)(2,1)S(1)}, bf16[256,512]{1,0:T(8,128)(2,1)S(1)}, u32[]{:S(2)}, u32[]{:S(2)}) collective-permute-start(bf16[256,512]{1,0:T(8,128)(2,1)S(1)} %bitcast.6), channel_id=1, source_target_pairs={{0,4},{1,5},{2,6},{3,7},{4,8},{5,9},{6,10},{7,11},{8,12},{9,13},{1... | collective-permute-start | bytes 786440 | tf_op jit(solution)/shard_map/ppermute | solution.py:37
  14.3 15.3 %collective-permute-start.1 = (bf16[256,512]{1,0:T(8,128)(2,1)S(1)}, bf16[256,512]{1,0:T(8,128)(2,1)S(1)}, u32[]{:S(2)}, u32[]{:S(2)}) collective-permute-start(bf16[256,512]{1,0:T(8,128)(2,1)S(1)} %bitcast.7), channel_id=1, source_target_pairs={{0,12},{1,13},{2,14},{3,15},{4,0},{5,1},{6,2},{7,3},{8,4},{9,5},{1... | collective-permute-start | bytes 786440 | tf_op jit(solution)/shard_map/ppermute | solution.py:37
  15.8 13.7 %collective-permute-start.2 = (bf16[256,512]{1,0:T(8,128)(2,1)S(1)}, bf16[256,512]{1,0:T(8,128)(2,1)S(1)}, u32[]{:S(2)}, u32[]{:S(2)}) collective-permute-start(bf16[256,512]{1,0:T(8,128)(2,1)S(1)} %bitcast.8), channel_id=1, source_target_pairs={{0,8},{1,9},{2,10},{3,11},{4,12},{5,13},{6,14},{7,15},{8,0},{9,1},... | collective-permute-start | bytes 786440 | tf_op jit(solution)/shard_map/ppermute | solution.py:37
  18.8 4.3 %collective-permute-start.3 = (bf16[1,144,128]{2,1,0:T(8,128)(2,1)}, bf16[1,144,128]{2,1,0:T(8,128)(2,1)S(1)}, u32[]{:S(2)}, u32[]{:S(2)}) collective-permute-start(bf16[1,144,128]{2,1,0:T(8,128)(2,1)} %shard_map.310.refs_0_), channel_id=1, source_target_pairs={{0,16},{16,0},{32,48},{48,32},{64,80},{80,64},{96,112},{112,96},{1... | collective-permute-start | bytes 110600 | tf_op jit(solution)/shard_map/ppermute | solution.py:49
  23.9 5.4 %collective-permute-start.4 = (bf16[2,144,128]{2,1,0:T(8,128)(2,1)S(1)}, bf16[2,144,128]{2,1,0:T(8,128)(2,1)S(1)}, u32[]{:S(2)}, u32[]{:S(2)}) collective-permute-start(bf16[2,144,128]{2,1,0:T(8,128)(2,1)S(1)} %shard_map.311.refs_0_), channel_id=1, source_target_pairs={{0,32},{16,48},{32,0},{48,16},{64,96},{80,112},{96,64},{112,80},{1... | collective-permute-start | bytes 221192 | tf_op jit(solution)/shard_map/ppermute | solution.py:49
  30.5 18.1 %collective-permute-start.8 = (bf16[256,512]{1,0:T(8,128)(2,1)S(1)}, bf16[256,512]{1,0:T(8,128)(2,1)S(1)}, u32[]{:S(2)}, u32[]{:S(2)}) collective-permute-start(bf16[256,512]{1,0:T(8,128)(2,1)S(1)} %shard_map.318), channel_id=1, source_target_pairs={{0,2},{1,3},{2,0},{3,1},{4,6},{5,7},{6,4},{7,5},{8,10},{9,11},{10,... | collective-permute-start | bytes 786440 | tf_op jit(solution)/shard_map/ppermute | solution.py:37
  35.1 29.4 %all-to-all-start.1 = ((bf16[16,64,128]{2,1,0:T(8,128)(2,1)}), bf16[16,64,128]{2,1,0:T(8,128)(2,1)S(1)}, u32[]{:S(2)}, u32[]{:S(2)}) async-start(bf16[16,64,128]{2,1,0:T(8,128)(2,1)} %get-tuple-element.49), calls=%async_computation.1 | async-start | bytes 524288 | tf_op jit(solution)/shard_map/all_to_all | solution.py:479
  43.3 10.0 %collective-permute-start.5 = (bf16[4,144,128]{2,1,0:T(8,128)(2,1)S(1)}, bf16[4,144,128]{2,1,0:T(8,128)(2,1)S(1)}, u32[]{:S(2)}, u32[]{:S(2)}) collective-permute-start(bf16[4,144,128]{2,1,0:T(8,128)(2,1)S(1)} %shard_map.312.refs_4_.refs_0_), channel_id=1, source_target_pairs={{0,64},{16,80},{32,96},{48,112},{64,0},{80,16},{96,32},{112,48},{1... | collective-permute-start | bytes 442376 | tf_op jit(solution)/shard_map/ppermute | solution.py:49
  48.6 10.3 %collective-permute-start.9 = (bf16[256,512]{1,0:T(8,128)(2,1)S(1)}, bf16[256,512]{1,0:T(8,128)(2,1)S(1)}, u32[]{:S(2)}, u32[]{:S(2)}) collective-permute-start(bf16[256,512]{1,0:T(8,128)(2,1)S(1)} %collective-permute-done.8.refs_0_), channel_id=1, source_target_pairs={{0,12},{1,13},{2,14},{3,15},{4,0},{5,1},{6,2},{7,3},{8,4},{9,5},{1... | collective-permute-start | bytes 786440 | tf_op jit(solution)/shard_map/ppermute | solution.py:37
  48.7 14.9 %collective-permute-start.10 = (bf16[256,512]{1,0:T(8,128)(2,1)S(1)}, bf16[256,512]{1,0:T(8,128)(2,1)S(1)}, u32[]{:S(2)}, u32[]{:S(2)}) collective-permute-start(bf16[256,512]{1,0:T(8,128)(2,1)S(1)} %collective-permute-done.8.refs_0_), channel_id=1, source_target_pairs={{0,8},{1,9},{2,10},{3,11},{4,12},{5,13},{6,14},{7,15},{8,0},{9,1},... | collective-permute-start | bytes 786440 | tf_op jit(solution)/shard_map/ppermute | solution.py:37
  51.9 12.3 %collective-permute-start.11 = (bf16[256,512]{1,0:T(8,128)(2,1)S(1)}, bf16[256,512]{1,0:T(8,128)(2,1)S(1)}, u32[]{:S(2)}, u32[]{:S(2)}) collective-permute-start(bf16[256,512]{1,0:T(8,128)(2,1)S(1)} %collective-permute-done.8.refs_0_), channel_id=1, source_target_pairs={{0,4},{1,5},{2,6},{3,7},{4,8},{5,9},{6,10},{7,11},{8,12},{9,13},{1... | collective-permute-start | bytes 786440 | tf_op jit(solution)/shard_map/ppermute | solution.py:37
  53.7 21.2 %collective-permute-start.6 = (bf16[8,144,128]{2,1,0:T(8,128)(2,1)S(1)}, bf16[8,144,128]{2,1,0:T(8,128)(2,1)S(1)}, u32[]{:S(2)}, u32[]{:S(2)}) collective-permute-start(bf16[8,144,128]{2,1,0:T(8,128)(2,1)S(1)} %shard_map.315.refs_4_), channel_id=1, source_target_pairs={{0,128},{16,144},{32,160},{48,176},{64,192},{80,208},{96,224},{112... | collective-permute-start | bytes 884744 | tf_op jit(solution)/shard_map/ppermute | solution.py:49
  56.0 38.8 %copy-start = (bf16[4,256,512]{2,1,0:T(8,128)(2,1)}, bf16[4,256,512]{2,1,0:T(8,128)(2,1)S(1)}, u32[]{:S(2)}) copy-start(bf16[4,256,512]{2,1,0:T(8,128)(2,1)S(1)} %shard_map.317.refs_2_) | copy-start | bytes 3145732
  56.0 36.1 %copy-start.19 = (s32[128]{0:T(128)S(1)}, s32[128]{0:T(128)}, u32[]{:S(2)}) copy-start(s32[128]{0:T(128)} %param.27) | copy-start | bytes 1540
  58.9 41.0 %collective-permute-start.7 = (bf16[4,256,512]{2,1,0:T(8,128)(2,1)S(1)}, bf16[4,256,512]{2,1,0:T(8,128)(2,1)}, u32[]{:S(2)}, u32[]{:S(2)}) collective-permute-start(bf16[4,256,512]{2,1,0:T(8,128)(2,1)S(1)} %shard_map.317.refs_2_), channel_id=1, source_target_pairs={{0,1},{1,0},{2,3},{3,2},{4,5},{5,4},{6,7},{7,6},{8,9},{9,8},{10,11... | collective-permute-start | bytes 3145736 | tf_op jit(solution)/shard_map/ppermute | solution.py:37
  64.3 35.6 %copy-start.1 = (bf16[4,256,512]{2,1,0:T(8,128)(2,1)}, bf16[4,256,512]{2,1,0:T(8,128)(2,1)S(1)}, u32[]{:S(2)}) copy-start(bf16[4,256,512]{2,1,0:T(8,128)(2,1)S(1)} %shard_map.319.refs_4_) | copy-start | bytes 3145732
  64.3 35.7 %collective-permute-start.12 = (bf16[4,256,512]{2,1,0:T(8,128)(2,1)S(1)}, bf16[4,256,512]{2,1,0:T(8,128)(2,1)}, u32[]{:S(2)}, u32[]{:S(2)}) collective-permute-start(bf16[4,256,512]{2,1,0:T(8,128)(2,1)S(1)} %shard_map.319.refs_4_), channel_id=1, source_target_pairs={{0,1},{1,0},{2,3},{3,2},{4,5},{5,4},{6,7},{7,6},{8,9},{9,8},{10,11... | collective-permute-start | bytes 3145736 | tf_op jit(solution)/shard_map/ppermute | solution.py:37
  66.1 16.9 %all-to-all-start.2 = ((f32[16,8,128]{2,1,0:T(8,128)}), f32[16,8,128]{2,1,0:T(8,128)S(1)}, u32[]{:S(2)}, u32[]{:S(2)}) async-start(f32[16,8,128]{2,1,0:T(8,128)} %shard_map.314), calls=%async_computation.2 | async-start | bytes 131072 | tf_op jit(solution)/shard_map/all_to_all | solution.py:489
  86.5 20.1 %all-to-all-start.3 = ((bf16[16,128,128]{2,1,0:T(8,128)(2,1)}), bf16[16,128,128]{2,1,0:T(8,128)(2,1)S(1)}, u32[]{:S(2)}, u32[]{:S(2)}) async-start(bf16[16,128,128]{2,1,0:T(8,128)(2,1)} %get-tuple-element.50), calls=%async_computation.3 | async-start | bytes 1048576 | tf_op jit(solution)/shard_map/all_to_all | solution.py:533
  111.9 1.5 %collective-permute-start.14 = (bf16[256,256]{1,0:T(8,128)(2,1)S(1)}, bf16[256,256]{1,0:T(8,128)(2,1)S(1)}, u32[]{:S(2)}, u32[]{:S(2)}) collective-permute-start(bf16[256,256]{1,0:T(8,128)(2,1)S(1)} %shard_map.323.refs_0_), channel_id=1, source_target_pairs={{0,1},{1,0},{2,3},{3,2},{4,5},{5,4},{6,7},{7,6},{8,9},{9,8},{10,11... | collective-permute-start | bytes 393224 | tf_op jit(solution)/shard_map/ppermute | solution.py:37
  112.1 1.2 collective-permute-start.19
  113.7 6.5 %collective-permute-start.20 = (bf16[160,512]{1,0:T(8,128)(2,1)S(1)}, bf16[160,512]{1,0:T(8,128)(2,1)S(1)}, u32[]{:S(2)}, u32[]{:S(2)}) collective-permute-start(bf16[160,512]{1,0:T(8,128)(2,1)S(1)} %get-tuple-element.65), channel_id=1, source_target_pairs={{0,4},{1,5},{2,6},{3,7},{4,8},{5,9},{6,10},{7,11},{8,12},{9,13},{1... | collective-permute-start | bytes 491528 | tf_op jit(solution)/shard_map/ppermute | solution.py:37
  114.2 7.4 %collective-permute-start.21 = (bf16[160,512]{1,0:T(8,128)(2,1)S(1)}, bf16[160,512]{1,0:T(8,128)(2,1)S(1)}, u32[]{:S(2)}, u32[]{:S(2)}) collective-permute-start(bf16[160,512]{1,0:T(8,128)(2,1)S(1)} %get-tuple-element.66), channel_id=1, source_target_pairs={{0,12},{1,13},{2,14},{3,15},{4,0},{5,1},{6,2},{7,3},{8,4},{9,5},{1... | collective-permute-start | bytes 491528 | tf_op jit(solution)/shard_map/ppermute | solution.py:37
  121.6 9.6 %collective-permute-start.22 = (bf16[288,512]{1,0:T(8,128)(2,1)S(1)}, bf16[288,512]{1,0:T(8,128)(2,1)S(1)}, u32[]{:S(2)}, u32[]{:S(2)}) collective-permute-start(bf16[288,512]{1,0:T(8,128)(2,1)S(1)} %get-tuple-element.70), channel_id=1, source_target_pairs={{0,4},{1,5},{2,6},{3,7},{4,8},{5,9},{6,10},{7,11},{8,12},{9,13},{1... | collective-permute-start | bytes 884744 | tf_op jit(solution)/shard_map/ppermute | solution.py:37
  122.1 10.7 %collective-permute-start.23 = (bf16[288,512]{1,0:T(8,128)(2,1)S(1)}, bf16[288,512]{1,0:T(8,128)(2,1)S(1)}, u32[]{:S(2)}, u32[]{:S(2)}) collective-permute-start(bf16[288,512]{1,0:T(8,128)(2,1)S(1)} %get-tuple-element.71), channel_id=1, source_target_pairs={{0,12},{1,13},{2,14},{3,15},{4,0},{5,1},{6,2},{7,3},{8,4},{9,5},{1... | collective-permute-start | bytes 884744 | tf_op jit(solution)/shard_map/ppermute | solution.py:37
  124.6 13.8 %collective-permute-start.15 = (bf16[128,512]{1,0:T(8,128)(2,1)S(1)}, bf16[128,512]{1,0:T(8,128)(2,1)S(1)}, u32[]{:S(2)}, u32[]{:S(2)}) collective-permute-start(bf16[128,512]{1,0:T(8,128)(2,1)S(1)} %get-tuple-element.58), channel_id=1, source_target_pairs={{0,4},{1,5},{2,6},{3,7},{4,8},{5,9},{6,10},{7,11},{8,12},{9,13},{1... | collective-permute-start | bytes 393224 | tf_op jit(solution)/shard_map/ppermute | solution.py:37
  126.3 12.2 %collective-permute-start.16 = (bf16[128,512]{1,0:T(8,128)(2,1)S(1)}, bf16[128,512]{1,0:T(8,128)(2,1)S(1)}, u32[]{:S(2)}, u32[]{:S(2)}) collective-permute-start(bf16[128,512]{1,0:T(8,128)(2,1)S(1)} %get-tuple-element.59), channel_id=1, source_target_pairs={{0,12},{1,13},{2,14},{3,15},{4,0},{5,1},{6,2},{7,3},{8,4},{9,5},{1... | collective-permute-start | bytes 393224 | tf_op jit(solution)/shard_map/ppermute | solution.py:37
  132.8 13.8 %collective-permute-start.24 = (bf16[288,512]{1,0:T(8,128)(2,1)S(1)}, bf16[288,512]{1,0:T(8,128)(2,1)S(1)}, u32[]{:S(2)}, u32[]{:S(2)}) collective-permute-start(bf16[288,512]{1,0:T(8,128)(2,1)S(1)} %shard_map.330.refs_1_), channel_id=1, source_target_pairs={{0,2},{1,3},{2,0},{3,1},{4,6},{5,7},{6,4},{7,5},{8,10},{9,11},{10,... | collective-permute-start | bytes 884744 | tf_op jit(solution)/shard_map/ppermute | solution.py:37
  138.5 6.4 %collective-permute-start.17 = (bf16[256,512]{1,0:T(8,128)(2,1)S(1)}, bf16[256,512]{1,0:T(8,128)(2,1)S(1)}, u32[]{:S(2)}, u32[]{:S(2)}) collective-permute-start(bf16[256,512]{1,0:T(8,128)(2,1)S(1)} %get-tuple-element.60), channel_id=1, source_target_pairs={{0,4},{1,5},{2,6},{3,7},{4,8},{5,9},{6,10},{7,11},{8,12},{9,13},{1... | collective-permute-start | bytes 786440 | tf_op jit(solution)/shard_map/ppermute | solution.py:37
  138.9 7.6 %collective-permute-start.18 = (bf16[256,512]{1,0:T(8,128)(2,1)S(1)}, bf16[256,512]{1,0:T(8,128)(2,1)S(1)}, u32[]{:S(2)}, u32[]{:S(2)}) collective-permute-start(bf16[256,512]{1,0:T(8,128)(2,1)S(1)} %get-tuple-element.61), channel_id=1, source_target_pairs={{0,12},{1,13},{2,14},{3,15},{4,0},{5,1},{6,2},{7,3},{8,4},{9,5},{1... | collective-permute-start | bytes 786440 | tf_op jit(solution)/shard_map/ppermute | solution.py:37
  (17 other events, 176.3 us)
